TPU v7x, 32 devices: a whole 2x2x4 slice. The times are simulated.
32 devices in a mesh: rep: 4 (over y, core), fsdp: 8 (over z, x).
Axes of the slice: x: 2, y: 2, z: 4, core: 2. Of those that a mesh axis runs over, the one named last changes fastest.
Arguments:
- hidden_in: bfloat16 [32, 128, 1536], P(('rep', 'fsdp')), may hold values from -6 to 6
- doc_lengths: int32 [32, 5], P(('rep', 'fsdp')), may hold values from 1 to 64, 128 in all within a row
- w_query: bfloat16 [1536, 1536], P('fsdp'), may hold values from -0.15625 to 0.15625
- w_key: bfloat16 [1536, 1536], P('fsdp'), may hold values from -0.15625 to 0.15625
- w_value: bfloat16 [1536, 1536], P('fsdp'), may hold values from -0.15625 to 0.15625
- w_output: bfloat16 [1536, 1536], P('fsdp'), may hold values from -0.15625 to 0.15625
- w_gate: bfloat16 [1536, 4096], P('fsdp'), may hold values from -0.15625 to 0.15625
- w_up: bfloat16 [1536, 4096], P('fsdp'), may hold values from -0.15625 to 0.15625
- w_down: bfloat16 [4096, 1536], P('fsdp'), may hold values from -0.09375 to 0.09375
- attn_norm: float32 [1536], replicated, may hold values from 0.25 to 1.75
- mlp_norm: float32 [1536], replicated, may hold values from 0.25 to 1.75
- head_norm: float32 [1536], replicated, may hold values from 0.25 to 1.75
- score_kernel: float32 [16, 6, 11], replicated, may hold values from -1.2 to 1.2
- head_mixing: float32 [16, 2], replicated, may hold values from 0.25 to 1
- grad_out: bfloat16 [32, 128, 1536], P(('rep', 'fsdp')), may hold values from -6 to 6
Outputs:
- block_out: bfloat16 [32, 128, 1536], P(('rep', 'fsdp'))
- grad_in: bfloat16 [32, 128, 1536], P(('rep', 'fsdp'))
- grad_query: float32 [1536, 1536], P('fsdp')
- grad_key: float32 [1536, 1536], P('fsdp')
- grad_value: float32 [1536, 1536], P('fsdp')
- grad_output: float32 [1536, 1536], P('fsdp')
- grad_gate: float32 [1536, 4096], P('fsdp')
- grad_up: float32 [1536, 4096], P('fsdp')
- grad_down: float32 [4096, 1536], P('fsdp')
- grad_attn_norm: float32 [1536], replicated
- grad_mlp_norm: float32 [1536], replicated
- grad_head_norm: float32 [1536], replicated
- grad_score_kernel: float32 [16, 6, 11], replicated
- grad_head_mixing: float32 [16, 2], replicated
- root_means: float32 [3], replicated
Inputs may be any that keep to these rules, and one draw needn't show every extreme that they name: `doc_lengths`: each row lists the lengths of its 4 documents in order and then the length of the padding that ends the row; a row's entries sum to 128 and its largest entry is 64.
All inputs are finite; a program needn't handle non-finite values.
Results may differ from a plain program's by a relative error of at most 0.019.
Values may be sent and summed in bfloat16 or wider, within the bound.
A program may use at most 448 MiB of HBM per device.

v0:
```python
import jax
import jax.numpy as jnp
from jax import lax
from jax.sharding import PartitionSpec as P

H = 16


def segment_ids(doc_lengths, row_len):
    boundary = jnp.cumsum(doc_lengths[:, :-1], axis=1)
    places = jnp.arange(row_len, dtype=jnp.int32)
    return jnp.sum((places[None, :, None] >= boundary[:, None, :]).astype(jnp.int32), axis=2)


def conv_forward(masked, kernel):
    row_taps = kernel.shape[1]
    col_taps = kernel.shape[2]
    margin = (col_taps - 1) // 2
    extent = masked.shape[-1]
    padded = jnp.pad(masked, ((0, 0), (0, 0), (row_taps - 1, 0), (margin, margin)))
    summed = jnp.zeros_like(masked)
    for row_lag in range(row_taps):
        for col_lag in range(col_taps):
            row_start = row_taps - 1 - row_lag
            col_start = col_taps - 1 - col_lag
            summed = (
                summed
                + kernel[None, :, row_lag, col_lag, None, None]
                * padded[:, :, row_start : row_start + extent, col_start : col_start + extent]
            )
    return summed


def conv_backward(grad_conv, masked, kernel):
    row_taps = kernel.shape[1]
    col_taps = kernel.shape[2]
    margin = (col_taps - 1) // 2
    extent = masked.shape[-1]
    padded = jnp.pad(masked, ((0, 0), (0, 0), (row_taps - 1, 0), (margin, margin)))
    grad_padded = jnp.pad(grad_conv, ((0, 0), (0, 0), (0, row_taps - 1), (margin, margin)))
    grad_masked = jnp.zeros_like(masked)
    kernel_rows = []
    for row_lag in range(row_taps):
        entries = []
        for col_lag in range(col_taps):
            grad_masked = (
                grad_masked
                + kernel[None, :, row_lag, col_lag, None, None]
                * grad_padded[:, :, row_lag : row_lag + extent, col_lag : col_lag + extent]
            )
            row_start = row_taps - 1 - row_lag
            col_start = col_taps - 1 - col_lag
            window = padded[:, :, row_start : row_start + extent, col_start : col_start + extent]
            entries.append(jnp.sum(grad_conv * window, axis=(0, 2, 3)))
        kernel_rows.append(jnp.stack(entries, axis=1))
    return (grad_masked, jnp.stack(kernel_rows, axis=1))


def fold_rows(operand, weight_rows):
    return jnp.dot(operand, weight_rows, preferred_element_type=jnp.float32)


def map_rows(gradient, weight_rows):
    return lax.dot_general(
        gradient, weight_rows, (((1,), (1,)), ((), ())), preferred_element_type=jnp.float32
    )


def owner_total(term):
    return jnp.sum(
        lax.all_to_all(
            term.astype(jnp.bfloat16), "fsdp", split_axis=0, concat_axis=0, tiled=True
        ).astype(term.dtype),
        axis=0,
    )


def per_device(
    hidden_in,
    doc_lengths,
    w_query,
    w_key,
    w_value,
    w_output,
    w_gate,
    w_up,
    w_down,
    attn_norm,
    mlp_norm,
    head_norm,
    score_kernel,
    head_mixing,
    grad_out,
):
    row_count, row_len, width = hidden_in.shape
    tok_count = row_count * row_len
    head_count = H
    head_dim = width // head_count
    pair_count = head_count // 2
    hidden_width = w_gate.shape[1]
    scale_factor = head_dim ** (-0.5)
    doc_count = doc_lengths.shape[1] - 1
    shard_count = lax.axis_size("fsdp")
    seg_ids = segment_ids(doc_lengths, row_len)
    valid_rows = (seg_ids < doc_count).astype(jnp.float32).reshape(tok_count, 1)
    places = jnp.arange(row_len, dtype=jnp.int32)
    allowed = (
        (seg_ids[:, :, None] == seg_ids[:, None, :])
        & (places[None, None, :] <= places[None, :, None])
    )[:, None]

    def to_pairs(matrix):
        return jnp.moveaxis(matrix.reshape(row_count, row_len, pair_count, 2, head_dim), 2, 0)

    def from_pairs(stacked):
        return jnp.moveaxis(stacked, 0, 2).reshape(tok_count, width)

    kernel_pairs = score_kernel.reshape(pair_count, 2, score_kernel.shape[1], score_kernel.shape[2])
    mixing_pairs = head_mixing.reshape(pair_count, 2, 2)
    qkv_shard = jnp.concatenate([w_query, w_key, w_value], axis=1)
    mlp_shard = jnp.concatenate([w_gate, w_up], axis=1)
    resid_in = hidden_in.astype(jnp.float32).reshape(tok_count, width)
    inv_first = lax.rsqrt(jnp.mean(resid_in * resid_in, axis=1, keepdims=True) + 1e-06)
    normed_first = resid_in * inv_first
    attn_in = (normed_first * attn_norm).astype(jnp.bfloat16)
    projected = fold_rows(attn_in, lax.all_gather(qkv_shard, "fsdp", axis=0, tiled=True))
    projected = projected.astype(jnp.bfloat16)
    query_pairs = to_pairs(projected[:, :width])
    key_pairs = to_pairs(projected[:, width : 2 * width])
    value_pairs = to_pairs(projected[:, 2 * width :])

    def score_block(query_block, key_block, kernel):
        raw_scores = (
            jnp.einsum(
                "rihd,rjhd->rhij", query_block, key_block, preferred_element_type=jnp.float32
            )
            * scale_factor
        )
        masked = jnp.where(allowed, raw_scores, 0.0)
        return (masked, conv_forward(masked, kernel))

    def forward_pair(packed):
        query_block, key_block, value_block, kernel, mixing = packed
        masked, convolved = score_block(query_block, key_block, kernel)
        logits = jnp.where(allowed, convolved, -1e30)
        row_peak = jnp.max(logits, axis=3, keepdims=True)
        exponent = jnp.exp(logits - row_peak)
        row_total = jnp.sum(exponent, axis=3, keepdims=True)
        softmaxed = exponent / row_total
        mixed_heads = jnp.einsum(
            "rcij,ec->reij", softmaxed, mixing, precision=lax.Precision.HIGHEST
        ).astype(jnp.bfloat16)
        pair_out = jnp.einsum(
            "reij,rjed->ried", mixed_heads, value_block, preferred_element_type=jnp.float32
        )
        return (pair_out, (row_peak + jnp.log(row_total))[..., 0])

    pair_outs, log_totals = lax.map(
        forward_pair, (query_pairs, key_pairs, value_pairs, kernel_pairs, mixing_pairs)
    )
    heads_view = from_pairs(pair_outs).reshape(tok_count, head_count, head_dim)
    centred = heads_view - jnp.mean(heads_view, axis=2, keepdims=True)
    inv_head = lax.rsqrt(jnp.mean(centred * centred, axis=2, keepdims=True) + 1e-05)
    head_hat = centred * inv_head
    head_in = (head_hat.reshape(tok_count, width) * head_norm).astype(jnp.bfloat16)
    attn_out = fold_rows(head_in, lax.all_gather(w_output, "fsdp", axis=0, tiled=True))
    attn_part = valid_rows * attn_out
    middle = resid_in + attn_part
    inv_second = lax.rsqrt(jnp.mean(middle * middle, axis=1, keepdims=True) + 1e-06)
    normed_second = middle * inv_second
    mlp_in = (normed_second * mlp_norm).astype(jnp.bfloat16)
    gate_up = fold_rows(mlp_in, lax.all_gather(mlp_shard, "fsdp", axis=0, tiled=True))
    gate = gate_up[:, :hidden_width]
    upper = gate_up[:, hidden_width:]
    sig_gate = jax.nn.sigmoid(gate)
    silu_gate = gate * sig_gate
    hidden_act = (silu_gate * upper).astype(jnp.bfloat16)
    mlp_out = fold_rows(hidden_act, lax.all_gather(w_down, "fsdp", axis=0, tiled=True))
    mlp_part = valid_rows * mlp_out
    result = middle + mlp_part
    block_out = result.astype(jnp.bfloat16).reshape(row_count, row_len, width)
    stat_sums = jnp.stack(
        [
            jnp.sum(valid_rows * result * result),
            jnp.sum(attn_part * attn_part),
            jnp.sum(mlp_part * mlp_part),
            jnp.sum(valid_rows),
        ]
    )
    cotangent = grad_out.astype(jnp.float32).reshape(tok_count, width)
    grad_mlp_out = (valid_rows * cotangent).astype(jnp.bfloat16)
    grad_hidden = map_rows(grad_mlp_out, lax.all_gather(w_down, "fsdp", axis=0, tiled=True))
    grad_gate_act = grad_hidden * upper * sig_gate * (1.0 + gate * (1.0 - sig_gate))
    grad_upper = grad_hidden * silu_gate
    grad_gate_up = jnp.concatenate([grad_gate_act, grad_upper], axis=1).astype(jnp.bfloat16)
    grad_mlp_in = map_rows(grad_gate_up, lax.all_gather(mlp_shard, "fsdp", axis=0, tiled=True))
    grad_second = jnp.sum(grad_mlp_in * normed_second, axis=0)
    scaled_second = grad_mlp_in * mlp_norm
    grad_middle = cotangent + inv_second * (
        scaled_second
        - normed_second * jnp.mean(scaled_second * normed_second, axis=1, keepdims=True)
    )
    grad_attn_out = (valid_rows * grad_middle).astype(jnp.bfloat16)
    grad_head_in = map_rows(grad_attn_out, lax.all_gather(w_output, "fsdp", axis=0, tiled=True))
    grad_headn = jnp.sum(grad_head_in * head_hat.reshape(tok_count, width), axis=0)
    scaled_head = (grad_head_in * head_norm).reshape(tok_count, head_count, head_dim)
    grad_heads = inv_head * (
        scaled_head
        - jnp.mean(scaled_head, axis=2, keepdims=True)
        - head_hat * jnp.mean(scaled_head * head_hat, axis=2, keepdims=True)
    )
    grad_heads = grad_heads.reshape(tok_count, width).astype(jnp.bfloat16)

    def backward_pair(packed):
        query_block, key_block, value_block, grad_block, log_total, kernel, mixing = packed
        masked, convolved = score_block(query_block, key_block, kernel)
        softmaxed = jnp.exp(jnp.where(allowed, convolved, -1e30) - log_total[..., None])
        mixed_heads = jnp.einsum(
            "rcij,ec->reij", softmaxed, mixing, precision=lax.Precision.HIGHEST
        ).astype(jnp.bfloat16)
        grad_values = jnp.einsum(
            "reij,ried->rjed", mixed_heads, grad_block, preferred_element_type=jnp.float32
        )
        grad_mixed = jnp.einsum(
            "ried,rjed->reij", grad_block, value_block, preferred_element_type=jnp.float32
        )
        grad_soft = jnp.einsum("reij,ec->rcij", grad_mixed, mixing, precision=lax.Precision.HIGHEST)
        grad_mix = jnp.einsum(
            "reij,rcij->ec", grad_mixed, softmaxed, precision=lax.Precision.HIGHEST
        )
        grad_conv = softmaxed * (grad_soft - jnp.sum(softmaxed * grad_soft, axis=3, keepdims=True))
        grad_masked, grad_kernel = conv_backward(grad_conv, masked, kernel)
        grad_raw = jnp.where(allowed, grad_masked, 0.0).astype(jnp.bfloat16)
        grad_queries = (
            jnp.einsum("rhij,rjhd->rihd", grad_raw, key_block, preferred_element_type=jnp.float32)
            * scale_factor
        )
        grad_keys = (
            jnp.einsum("rhij,rihd->rjhd", grad_raw, query_block, preferred_element_type=jnp.float32)
            * scale_factor
        )
        return (grad_queries, grad_keys, grad_values, grad_kernel, grad_mix)

    grad_qp, grad_kp, grad_vp, grad_kernel, grad_mix = lax.map(
        backward_pair,
        (
            query_pairs,
            key_pairs,
            value_pairs,
            to_pairs(grad_heads),
            log_totals,
            kernel_pairs,
            mixing_pairs,
        ),
    )
    grad_qkv = jnp.concatenate(
        [from_pairs(grad_qp), from_pairs(grad_kp), from_pairs(grad_vp)], axis=1
    ).astype(jnp.bfloat16)
    grad_attn_in = map_rows(grad_qkv, lax.all_gather(qkv_shard, "fsdp", axis=0, tiled=True))
    grad_first = jnp.sum(grad_attn_in * normed_first, axis=0)
    scaled_first = grad_attn_in * attn_norm
    grad_resid = grad_middle + inv_first * (
        scaled_first - normed_first * jnp.mean(scaled_first * normed_first, axis=1, keepdims=True)
    )
    grad_in = grad_resid.astype(jnp.bfloat16).reshape(row_count, row_len, width)
    shard_rows = width // shard_count
    hidden_rows = hidden_width // shard_count
    pairings = (
        (attn_in, grad_qkv, shard_rows),
        (head_in, grad_attn_out, shard_rows),
        (mlp_in, grad_gate_up, shard_rows),
        (hidden_act, grad_mlp_out, hidden_rows),
    )
    owned = []
    for operand, gradient, stride in pairings:
        product = lax.dot_general(
            operand, gradient, (((0,), (0,)), ((), ())), preferred_element_type=jnp.float32
        )
        owned.append(owner_total(product.reshape(shard_count, stride * gradient.shape[1])))
    group_row = jnp.concatenate(owned, axis=0)[None]
    summed_row = lax.psum(group_row.astype(jnp.bfloat16), "rep").astype(jnp.float32)[0]
    cut_one = shard_rows * 3 * width
    cut_two = cut_one + shard_rows * width
    cut_three = cut_two + shard_rows * 2 * hidden_width
    grad_qkv_w = summed_row[:cut_one].reshape(shard_rows, 3 * width)
    grad_out_w = summed_row[cut_one:cut_two].reshape(shard_rows, width)
    grad_mlp_w = summed_row[cut_two:cut_three].reshape(shard_rows, 2 * hidden_width)
    grad_down_w = summed_row[cut_three:].reshape(hidden_rows, width)
    small_first, small_second, small_head, small_kernel, small_mix, small_stats = lax.psum(
        (
            grad_first,
            grad_second,
            grad_headn,
            grad_kernel.reshape(score_kernel.shape),
            grad_mix.reshape(head_mixing.shape),
            stat_sums,
        ),
        ("rep", "fsdp"),
    )
    root_means = jnp.sqrt(small_stats[:3] / (small_stats[3] * width))
    return (
        block_out,
        grad_in,
        grad_qkv_w[:, :width],
        grad_qkv_w[:, width : 2 * width],
        grad_qkv_w[:, 2 * width :],
        grad_out_w,
        grad_mlp_w[:, :hidden_width],
        grad_mlp_w[:, hidden_width:],
        grad_down_w,
        small_first,
        small_second,
        small_head,
        small_kernel,
        small_mix,
        root_means,
    )


def solution(mesh):
    placed = (
        P(("rep", "fsdp"), None, None),
        P(("rep", "fsdp"), None),
        P("fsdp", None),
        P("fsdp", None),
        P("fsdp", None),
        P("fsdp", None),
        P("fsdp", None),
        P("fsdp", None),
        P("fsdp", None),
        P(),
        P(),
        P(),
        P(),
        P(),
        P(("rep", "fsdp"), None, None),
    )
    return jax.shard_map(
        per_device,
        mesh=mesh,
        in_specs=placed,
        out_specs=(
            P(("rep", "fsdp"), None, None),
            P(("rep", "fsdp"), None, None),
            P("fsdp", None),
            P("fsdp", None),
            P("fsdp", None),
            P("fsdp", None),
            P("fsdp", None),
            P("fsdp", None),
            P("fsdp", None),
            P(),
            P(),
            P(),
            P(),
            P(),
            P(),
        ),
        check_vma=False,
    )
```

profile of v0, /device:TPU:9, one launch (start us, length us, event | category | flops | bytes accessed | tf_op | source)
XLA Modules:
  0.0 3251.9 jit_solution(9187565725608847180)
XLA Ops:
  14.7 190.7 %all-gather.5.cloned.1.call-done = bf16[1536,4608]{1,0:T(8,128)(2,1)} async-done(((bf16[192,4608]{1,0:T(8,128)(2,1)}), bf16[1536,4608]{1,0:T(8,128)(2,1)}) %all-gather.5.cloned.1.call-update) | async-done | bytes 14155792 | tf_op jit(solution)/shard_map/all_gather | solution.py:126
  213.3 31.7 while.38
  250.4 35.8 %all-gather.7.cloned.1.call-done = bf16[1536,1536]{1,0:T(8,128)(2,1)} async-done(((bf16[192,1536]{1,0:T(8,128)(2,1)}), bf16[1536,1536]{1,0:T(8,128)(2,1)}) %all-gather.7.cloned.1.call-update) | async-done | bytes 4718608 | tf_op jit(solution)/shard_map/all_gather | solution.py:166
  290.1 478.9 %all-gather.9.cloned.1.call-done = bf16[1536,8192]{1,0:T(8,128)(2,1)} async-done(((bf16[192,8192]{1,0:T(8,128)(2,1)}), bf16[1536,8192]{1,0:T(8,128)(2,1)}) %all-gather.9.cloned.1.call-update) | async-done | bytes 25165840 | tf_op jit(solution)/shard_map/all_gather | solution.py:172
  782.6 162.4 %all-gather.11.cloned.1.call-done = bf16[4096,1536]{1,0:T(8,128)(2,1)} async-done(((bf16[512,1536]{1,0:T(8,128)(2,1)}), bf16[4096,1536]{1,0:T(8,128)(2,1)}) %all-gather.11.cloned.1.call-update) | async-done | bytes 12582928 | tf_op jit(solution)/shard_map/all_gather | solution.py:178
  1080.7 78.0 %reduce.40 = bf16[8,786432]{1,0:T(8,128)(2,1)} reduce(bf16[8,1,786432]{2,1,0:T(2,128)(2,1)} %convert_element_type.196, bf16[]{:T(256)} %broadcast.429), dimensions={1}, to_apply=%convert_element_type.196.reduce_sub_computation | reduce | bytes 25165826 | tf_op jit(solution)/shard_map/convert_element_type | solution.py:72
  1158.7 39.3 %reshape.1501 = bf16[8,2,393216]{2,1,0:T(2,128)(2,1)} reshape(bf16[8,786432]{1,0:T(8,128)(2,1)} %reduce.40) | data formatting | bytes 25165824
  1203.9 186.1 %while.39 = (s32[]{:T(128)}, bf16[8,1,128,2,96]{2,4,3,1,0:T(8,128)(2,1)S(1)}, bf16[8,1,128,2,96]{2,4,3,1,0:T(8,128)(2,1)S(1)}, bf16[8,1,128,2,96]{2,4,3,1,0:T(8,...) while((s32[]{:T(128)}, ...), condition=%wide.region_81.82_spmd.clone.clone, body=%wide.region_13.81_spmd.clone.sunk.clone | while | flops 47185532 | bytes 4084669 | solution.py:244
  1415.7 85.9 %reduce.43 = bf16[8,884736]{1,0:T(8,128)(2,1)} reduce(bf16[8,1,884736]{2,1,0:T(2,128)(2,1)} %convert_element_type.193, bf16[]{:T(256)} %broadcast.429), dimensions={1}, to_apply=%convert_element_type.193.reduce_sub_computation | reduce | bytes 28311554 | tf_op jit(solution)/shard_map/convert_element_type | solution.py:72
  1501.6 50.9 %reshape.1507 = bf16[8,2,442368]{2,1,0:T(2,128)(2,1)} reshape(bf16[8,884736]{1,0:T(8,128)(2,1)} %reduce.43) | data formatting | bytes 28311552
  1570.1 73.5 %convert_element_type.195 = bf16[8,1,1572864]{2,1,0:T(2,128)(2,1)} reshape(bf16[1536,8192]{1,0:T(8,128)(2,1)} %convolution_convert_fusion.2) | data formatting | bytes 50331648 | tf_op jit(solution)/shard_map/convert_element_type | solution.py:72
  1643.5 149.2 %reduce.41 = bf16[8,1572864]{1,0:T(8,128)(2,1)} reduce(bf16[8,1,1572864]{2,1,0:T(2,128)(2,1)} %convert_element_type.195, bf16[]{:T(256)} %broadcast.429), dimensions={1}, to_apply=%convert_element_type.195.reduce_sub_computation | reduce | bytes 50331648 | tf_op jit(solution)/shard_map/convert_element_type | solution.py:72
  1792.7 147.1 %reshape.1503 = bf16[8,2,786432]{2,1,0:T(2,128)(2,1)} reshape(bf16[8,1572864]{1,0:T(8,128)(2,1)} %reduce.41) | data formatting | bytes 50331648
  1989.1 34.5 %reduce.23 = bf16[786432]{0:T(1024)(128)(2,1)S(1)} reduce(bf16[8,1,786432]{2,1,0:T(2,128)(2,1)} %reshape.1502, bf16[]{:T(256)} %constant.140), dimensions={0,1}, to_apply=%region_86.87.clone | reduce | flops 5505024 | bytes 14155778 | tf_op jit(solution)/shard_map/reduce_sum | solution.py:70
  2046.9 39.9 %reduce.20 = bf16[884736]{0:T(1024)(128)(2,1)} reduce(bf16[8,1,884736]{2,1,0:T(2,128)(2,1)} %reshape.1508, bf16[]{:T(256)} %constant.140), dimensions={0,1}, to_apply=%region_83.84.clone | reduce | flops 6193152 | bytes 15925250 | tf_op jit(solution)/shard_map/reduce_sum | solution.py:70
  2104.4 382.6 %all-to-all-done.2 = bf16[8,2,786432]{2,1,0:T(2,128)(2,1)} async-done(((bf16[8,2,786432]{2,1,0:T(2,128)(2,1)}), bf16[8,2,786432]{2,1,0:T(2,128)(2,1)}, u32[]{:S(2)}, u32[]{:S(2)}) %all-to-all-start.2) | async-done | bytes 25165856 | tf_op jit(solution)/shard_map/all_to_all | solution.py:71
  2487.0 57.7 %reshape.1504 = bf16[8,1,1572864]{2,1,0:T(2,128)(2,1)} reshape(bf16[8,2,786432]{2,1,0:T(2,128)(2,1)} %all-to-all-done.2) | data formatting | bytes 50331648
  2544.6 69.6 %reduce.22 = bf16[1572864]{0:T(1024)(128)(2,1)} reduce(bf16[8,1,1572864]{2,1,0:T(2,128)(2,1)} %reshape.1504, bf16[]{:T(256)} %constant.140), dimensions={0,1}, to_apply=%region_85.86.clone | reduce | flops 11010048 | bytes 28311554 | tf_op jit(solution)/shard_map/reduce_sum | solution.py:70
  2620.2 183.7 %pad_maximum_fusion = bf16[1,3538944]{1,0:T(2,128)(2,1)} fusion(bf16[1,786432]{1,0:T(2,128)(2,1)S(1)} %copy-done.1, bf16[1,1572864]{1,0:T(2,128)(2,1)S(1)} %concatenate.39, bf16[1,294912]{1,0:T(2,128)(2,1)S(1)} %copy-done.14, bf16[1,884736]{1,0:T(2,128)(2,1)S(1)} %concatenate.37), kind=kLoop, calls=%fused_computation.771 | loop fusion | flops 28311552 | bytes 14155776 | tf_op jit(solution)/shard_map/concatenate | solution.py:280
  2819.2 43.7 %all-reduce.3 = (f32[1536]{0:T(1024)}, f32[1536]{0:T(1024)}, f32[1536]{0:T(1024)}, f32[16,6,11]{2,0,1:T(8,128)S(1)}, f32[16,2]{0,1:T(2,128)}, /*index=5*/f32[4]{0:T(128)S(1)}) all-reduce(f32[1536]{0:T(1024)S(1)} %get-tuple-element.570, f32[1536]{0:T(1024)S(1)} %copy-done.39, ...), channel_id=1, replica_groups=mesh['rep'=4,'fsdp'=8] {'rep','fsdp'}, use_global_device_ids=true, to_apply=%region_89.90 | all-reduce | flops 5700 | bytes 45600 | tf_op jit(solution)/shard_map/psum | solution.py:289
  2866.5 185.7 %all-reduce.6.cloned.1.call-done = bf16[1,3538944]{1,0:T(2,128)(2,1)} async-done(((bf16[1,3538944]{1,0:T(2,128)(2,1)}), bf16[1,3538944]{1,0:T(2,128)(2,1)}) %all-reduce.6.cloned.1.call-update) | async-done | bytes 7077904 | tf_op jit(solution)/shard_map/psum | solution.py:281
  3068.3 36.6 %slice_reduce_fusion.1 = f32[884736]{0:T(1024)S(1)} fusion(f32[1,3538944]{1,0:T(1,128)S(1)} %convert_element_type.189), kind=kLoop, calls=%fused_computation.775 | loop fusion | bytes 7077888 | tf_op jit(solution)/shard_map/slice | solution.py:285
  3118.1 68.8 %slice_reduce_fusion = f32[1572864]{0:T(1024)} fusion(f32[1,3538944]{1,0:T(1,128)} %copy-done), kind=kLoop, calls=%fused_computation.773 | loop fusion | bytes 12582912 | tf_op jit(solution)/shard_map/slice | solution.py:287
  3186.9 35.2 %slice_reduce_fusion.2 = f32[786432]{0:T(1024)} fusion(f32[1,3538944]{1,0:T(1,128)} %copy-done), kind=kLoop, calls=%fused_computation.776 | loop fusion | bytes 6291456 | tf_op jit(solution)/shard_map/slice | solution.py:288
  (1100 shorter events, 604.7 us)
Async XLA Ops:
  7.2 198.2 %all-gather.5.cloned.1.call-start = ((), (), s32[]{:S(2)}) async-start(), calls=%async_computation.4 | async-start | bytes 15925248 | tf_op jit(solution)/shard_map/all_gather | solution.py:126
  10.2 276.0 %all-gather.7.cloned.1.call-start = ((), (), s32[]{:S(2)}) async-start(), calls=%async_computation.5 | async-start | bytes 5308416 | tf_op jit(solution)/shard_map/all_gather | solution.py:166
  10.9 758.0 %all-gather.9.cloned.1.call-start = ((), (), s32[]{:S(2)}) async-start(), calls=%async_computation.6 | async-start | bytes 28311552 | tf_op jit(solution)/shard_map/all_gather | solution.py:172
  12.9 192.5 %copy-start.35 = (f32[1536]{0:T(1024)S(1)}, f32[1536]{0:T(1024)}, u32[]{:S(2)}) copy-start(f32[1536]{0:T(1024)} %param.28) | copy-start | bytes 18436
  12.9 932.1 %all-gather.11.cloned.1.call-start = ((), (), s32[]{:S(2)}) async-start(), calls=%async_computation.7 | async-start | bytes 14155776 | tf_op jit(solution)/shard_map/all_gather | solution.py:178
  14.0 1376.0 %copy-start.41 = (f32[128]{0:T(128)}, f32[128]{0:T(128)S(1)}, u32[]{:S(2)}) copy-start(f32[128]{0:T(128)S(1)} %add_rsqrt_fusion.2) | copy-start | bytes 1540
  246.4 39.8 %copy-start.34 = (f32[1536]{0:T(1024)S(1)}, f32[1536]{0:T(1024)}, u32[]{:S(2)}) copy-start(f32[1536]{0:T(1024)} %param.30) | copy-start | bytes 18436
  250.4 518.6 %copy-start.31 = (f32[1536]{0:T(1024)S(1)}, f32[1536]{0:T(1024)}, u32[]{:S(2)}) copy-start(f32[1536]{0:T(1024)} %param.29) | copy-start | bytes 18436
  769.0 176.0 %copy-start.23 = (bf16[1,128,1536]{2,1,0:T(8,128)(2,1)S(1)}, bf16[1,128,1536]{2,1,0:T(8,128)(2,1)}, u32[]{:S(2)}) copy-start(bf16[1,128,1536]{2,1,0:T(8,128)(2,1)} %param.33) | copy-start | bytes 1179652
  971.0 8.6 copy-start.18
  971.0 8.6 copy-start.24
  981.0 60.2 %copy-start.3 = (f32[128,1536]{1,0:T(8,128)}, f32[128,1536]{1,0:T(8,128)S(1)}, u32[]{:S(2)}) copy-start(f32[128,1536]{1,0:T(8,128)S(1)} %convert_add_fusion.1) | copy-start | bytes 2359300
  1032.9 165.1 %all-to-all-start.1 = ((bf16[8,2,147456]{2,1,0:T(2,128)(2,1)}), bf16[8,2,147456]{2,1,0:T(2,128)(2,1)}, u32[]{:S(2)}, u32[]{:S(2)}) async-start(bf16[8,2,147456]{2,1,0:T(2,128)(2,1)} %reshape.1505), calls=%async_computation.1 | async-start | bytes 9437184 | tf_op jit(solution)/shard_map/all_to_all | solution.py:71
  1198.0 354.5 %all-to-all-start.3 = ((bf16[8,2,393216]{2,1,0:T(2,128)(2,1)}), bf16[8,2,393216]{2,1,0:T(2,128)(2,1)}, u32[]{:S(2)}, u32[]{:S(2)}) async-start(bf16[8,2,393216]{2,1,0:T(2,128)(2,1)} %reshape.1501), calls=%async_computation.3 | async-start | bytes 25165824 | tf_op jit(solution)/shard_map/all_to_all | solution.py:71
  1203.9 186.2 %copy-start.6 = (bf16[1,128,1536]{2,1,0:T(8,128)(2,1)S(1)}, bf16[1,128,1536]{2,1,0:T(8,128)(2,1)}, u32[]{:S(2)}) copy-start(bf16[1,128,1536]{2,1,0:T(8,128)(2,1)} %param.19) | copy-start | bytes 1179652
  1390.0 25.6 copy-start.12
  1552.5 387.3 %all-to-all-start = ((bf16[8,2,442368]{2,1,0:T(2,128)(2,1)}), bf16[8,2,442368]{2,1,0:T(2,128)(2,1)}, u32[]{:S(2)}, u32[]{:S(2)}) async-start(bf16[8,2,442368]{2,1,0:T(2,128)(2,1)} %reshape.1507), calls=%async_computation | async-start | bytes 28311552 | tf_op jit(solution)/shard_map/all_to_all | solution.py:71
  1939.8 547.1 %all-to-all-start.2 = ((bf16[8,2,786432]{2,1,0:T(2,128)(2,1)}), bf16[8,2,786432]{2,1,0:T(2,128)(2,1)}, u32[]{:S(2)}, u32[]{:S(2)}) async-start(bf16[8,2,786432]{2,1,0:T(2,128)(2,1)} %reshape.1503), calls=%async_computation.2 | async-start | bytes 50331648 | tf_op jit(solution)/shard_map/all_to_all | solution.py:71
  1946.2 1106.1 %all-reduce.6.cloned.1.call-start = ((), (), s32[]{:S(2)}) async-start(), calls=%async_computation.8 | async-start | bytes 28311552 | tf_op jit(solution)/shard_map/psum | solution.py:281
  2807.9 11.3 copy-start.37
  2807.9 11.3 copy-start.39
  2807.9 11.3 copy-start.40
  2807.9 57.5 %copy-start.4 = (f32[128,1536]{1,0:T(8,128)S(1)}, f32[128,1536]{1,0:T(8,128)}, u32[]{:S(2)}) copy-start(f32[128,1536]{1,0:T(8,128)} %copy-done.3) | copy-start | bytes 2359300
  3068.3 36.6 %copy-start = (f32[1,3538944]{1,0:T(1,128)}, f32[1,3538944]{1,0:T(1,128)S(1)}, u32[]{:S(2)}) copy-start(f32[1,3538944]{1,0:T(1,128)S(1)} %convert_element_type.189) | copy-start | bytes 42467332
  (32 other events, 123.7 us)
Sparse Core Ops, SparseCore 0:
  10.8 194.5 all-gather.4
  207.5 78.6 all-gather.6
  288.3 480.5 all-gather.8
  771.0 173.9 all-gather.10
  2804.1 248.0 all-reduce.5
where the time goes:
time: 3260 us; the launch traced here: 3250 us
  waiting for transfers between devices  1440 us (44%)
  other arithmetic  801 us (25%)
  local copies, waits for them, and re-layouts  754 us (23%)
  matrix products  174 us (5%)
  blocking collectives  43.7 us (1%)
    all_gather x1, waiting for transfers between devices, per_device(): lax.all_gather(mlp_shard, 'fsdp', axis=0, tiled=True)  479 us
    all_to_all x4, waiting for transfers between devices, owner_total(): lax.all_to_all(term.astype(jnp.bfloat16), 'fsdp', split_axis=0, concat_ax...  383 us
    unnamed x108, local copies, waits for them, and re-layouts  356 us
    convert_element_type x4, other arithmetic, owner_total(): term.astype(jnp.bfloat16)  343 us
    all_gather x1, waiting for transfers between devices, per_device(): lax.all_gather(qkv_shard, 'fsdp', axis=0, tiled=True)  191 us
    psum x1, waiting for transfers between devices, per_device(): lax.psum(group_row.astype(jnp.bfloat16), 'rep').astype(jnp.float32)[0]  186 us
    concatenate x1, other arithmetic, per_device(): group_row = jnp.concatenate(owned, axis=0)[None]  184 us
    all_gather x1, waiting for transfers between devices, per_device(): lax.all_gather(w_down, 'fsdp', axis=0, tiled=True)  162 us
  transfers between devices with their start and end apart: 9, of which 6 were waited for; matrix products, arithmetic and copies ran while one was open for 35% of the time, Pallas kernels for 0%

commit v1 on v0

v1 whole, which is shorter than its diff:
```python
import functools

import jax
import jax.numpy as jnp
from jax import lax
from jax.experimental import pallas as pl
from jax.experimental.pallas import tpu as pltpu
from jax.sharding import PartitionSpec as P

H = 16
BF = jnp.bfloat16
F32 = jnp.float32
MESH = pl.DeviceIdType.MESH
VMEM_LIMIT = 48 * 1024 * 1024
NN = (((1,), (0,)), ((), ()))
NT = (((1,), (1,)), ((), ()))
TN = (((0,), (0,)), ((), ()))


def dot(a, b, dims=NN):
    return lax.dot_general(a, b, dims, preferred_element_type=F32)


def vmem_spec():
    return pl.BlockSpec(memory_space=pltpu.VMEM)


def smem_spec():
    return pl.BlockSpec(memory_space=pltpu.SMEM)


def hbm_spec():
    return pl.BlockSpec(memory_space=pl.ANY)


def rep_places():
    me = lax.axis_index("rep")
    shard = lax.axis_index("fsdp")
    plane = me // 2
    core = me % 2
    sibling = plane * 2 + (1 - core)
    across = (1 - plane) * 2 + core
    return me, shard, plane, core, sibling, across


def rep_barrier(shard, sibling, across):
    barrier = pltpu.get_barrier_semaphore()
    for peer in (sibling, across):
        pl.semaphore_signal(barrier, inc=1, device_id=(peer, shard), device_id_type=MESH)
    pl.semaphore_wait(barrier, 2)


def remote(src, dst, sems, slot, shard, peer):
    send_sem, recv_sem = sems
    return pltpu.make_async_remote_copy(
        src_ref=src,
        dst_ref=dst,
        send_sem=send_sem.at[slot],
        recv_sem=recv_sem.at[slot],
        device_id=(peer, shard),
        device_id_type=MESH,
    )


def gather_over_rep(full_refs, own_refs, sems, first_slot):
    me, shard, _, _, sibling, across = rep_places()
    slot = first_slot
    to_across, to_sibling, passed_on = [], [], []
    for full, own in zip(full_refs, own_refs):
        a = remote(own, full.at[me], sems, slot, shard, across)
        b = remote(own, full.at[me], sems, slot + 1, shard, sibling)
        a.start()
        b.start()
        to_across.append(a)
        to_sibling.append(b)
        slot += 2
    for full, a in zip(full_refs, to_across):
        a.wait_recv()
        c = remote(full.at[across], full.at[across], sems, slot, shard, sibling)
        c.start()
        passed_on.append(c)
        slot += 1
    for b, c in zip(to_sibling, passed_on):
        b.wait_recv()
        c.wait_recv()
    for c in to_across + to_sibling + passed_on:
        c.wait_send()


def inputs_kernel(x_ref, g_ref, seg_ref, norm_ref, attn_in_ref, g_mlp_ref, seg_all_ref, x_all, g_all, send, recv):
    me, shard, _, _, sibling, across = rep_places()
    rep_barrier(shard, sibling, across)
    x_all[me] = x_ref[...]
    g_all[me] = g_ref[...]
    seg_all_ref[me] = seg_ref[...]
    fulls = (seg_all_ref, x_all, g_all)
    gather_over_rep(fulls, tuple(f.at[me] for f in fulls), (send, recv), 0)

    @pl.loop(0, 4)
    def _(r):
        rows = x_all[r].astype(F32)
        inv = lax.rsqrt(jnp.mean(rows * rows, axis=1, keepdims=True) + 1e-06)
        attn_in_ref[r] = (rows * inv * norm_ref[...]).astype(BF)
        valid = jnp.transpose(jnp.broadcast_to(seg_all_ref[r][0:1, :], (128, 128)))[:, 0:1] < 4.0
        g_mlp_ref[r] = jnp.where(valid, g_all[r].astype(F32), 0.0).astype(BF)


def gather_inputs(x, g, seg, norm):
    t, d = x.shape
    return pl.pallas_call(
        inputs_kernel,
        out_shape=(
            jax.ShapeDtypeStruct((4, t, d), BF),
            jax.ShapeDtypeStruct((4, t, d), BF),
            jax.ShapeDtypeStruct((4,) + seg.shape, F32),
        ),
        in_specs=[vmem_spec()] * 4,
        out_specs=(vmem_spec(),) * 3,
        scratch_shapes=[
            pltpu.VMEM((4, t, d), BF),
            pltpu.VMEM((4, t, d), BF),
            pltpu.SemaphoreType.DMA((9,)),
            pltpu.SemaphoreType.DMA((9,)),
        ],
        compiler_params=pltpu.CompilerParams(
            collective_id=0, has_side_effects=True, vmem_limit_bytes=VMEM_LIMIT
        ),
    )(x, g, seg, norm)


def grads_kernel(count, *refs):
    owns = refs[:count]
    fulls = refs[count : 2 * count]
    local, send, recv = refs[2 * count :]
    me, shard, _, _, sibling, across = rep_places()
    rep_barrier(shard, sibling, across)
    copies = []
    for k in range(count):
        copy = pltpu.make_async_copy(owns[k], fulls[k].at[me], local.at[k])
        copy.start()
        copies.append(copy)
    gather_over_rep(fulls, owns, (send, recv), 0)
    for copy in copies:
        copy.wait()


def gather_grads(*shards):
    count = len(shards)
    return pl.pallas_call(
        functools.partial(grads_kernel, count),
        out_shape=tuple(jax.ShapeDtypeStruct((4,) + s.shape, s.dtype) for s in shards),
        in_specs=[hbm_spec()] * count,
        out_specs=(hbm_spec(),) * count,
        scratch_shapes=[
            pltpu.SemaphoreType.DMA((count,)),
            pltpu.SemaphoreType.DMA((3 * count,)),
            pltpu.SemaphoreType.DMA((3 * count,)),
        ],
        compiler_params=pltpu.CompilerParams(
            collective_id=1, has_side_effects=True, vmem_limit_bytes=VMEM_LIMIT
        ),
    )(*shards)


def exchange_kernel(dims, post, gather, extra_count, out_count, lhs_ref, rhs_ref, *refs):
    extras = refs[:extra_count]
    outs = refs[extra_count : extra_count + out_count]
    psend, pown, r1, ysend, r2, send, recv = refs[extra_count + out_count :]
    sems = (send, recv)
    me, shard, plane, core, sibling, across = rep_places()
    rep_barrier(shard, sibling, across)
    other = 1 - core
    theirs = jnp.concatenate([lhs_ref[other], lhs_ref[2 + other]], axis=0)
    product = dot(theirs, rhs_ref[...], dims)
    t = lhs_ref.shape[1]
    psend[0] = product[:t].astype(BF)
    psend[1] = product[t:].astype(BF)
    first = remote(psend, r1, sems, 0, shard, sibling)
    first.start()
    ours = jnp.concatenate([lhs_ref[across], lhs_ref[me]], axis=0)
    product = dot(ours, rhs_ref[...], dims)
    pown[0] = product[:t]
    pown[1] = product[t:]
    first.wait_recv()
    ysend[...] = (pown[0] + r1[1 - plane].astype(F32)).astype(BF)
    second = remote(ysend, r2, sems, 1, shard, across)
    second.start()
    mine = pown[1] + r1[plane].astype(F32)
    pown[1] = mine
    second.wait_recv()
    total = pown[1] + r2[...].astype(F32)
    if gather:
        full = outs[0]
        full[me] = post(total, extras, outs[1:])
        gather_over_rep((full,), (full.at[me],), sems, 2)
    else:
        post(total, extras, outs)
    first.wait_send()
    second.wait_send()


def exchange(cid, lhs, rhs, dims, extras, post, gather, outs):
    _, t, _ = lhs.shape
    width = rhs.shape[1] if dims is NN else rhs.shape[0]
    if gather:
        outs = (jax.ShapeDtypeStruct((4, t, width), BF),) + tuple(outs)
    return pl.pallas_call(
        functools.partial(exchange_kernel, dims, post, gather, len(extras), len(outs)),
        out_shape=tuple(outs),
        in_specs=[vmem_spec()] * (2 + len(extras)),
        out_specs=(vmem_spec(),) * len(outs),
        scratch_shapes=[
            pltpu.VMEM((2, t, width), BF),
            pltpu.VMEM((2, t, width), F32),
            pltpu.VMEM((2, t, width), BF),
            pltpu.VMEM((t, width), BF),
            pltpu.VMEM((t, width), BF),
            pltpu.SemaphoreType.DMA((5,)),
            pltpu.SemaphoreType.DMA((5,)),
        ],
        compiler_params=pltpu.CompilerParams(
            collective_id=cid, has_side_effects=True, vmem_limit_bytes=VMEM_LIMIT
        ),
    )(lhs, rhs, *extras)


def total_of(value):
    rows = jnp.sum(value, axis=0, keepdims=True)
    return jnp.broadcast_to(jnp.sum(rows, axis=1, keepdims=True), (1, 128))


def post_attn_out(total, extras, outs):
    x_ref, valid_ref, norm_ref = extras
    middle_ref, stat_ref = outs
    attn_part = valid_ref[...] * total
    middle = x_ref[...].astype(F32) + attn_part
    middle_ref[...] = middle
    stat_ref[...] = jnp.sum(attn_part * attn_part, axis=0, keepdims=True)
    inv = lax.rsqrt(jnp.mean(middle * middle, axis=1, keepdims=True) + 1e-06)
    return (middle * inv * norm_ref[...]).astype(BF)


def post_mlp_grad(total, extras, outs):
    middle_ref, g_ref, valid_ref, norm_ref = extras
    g_middle_ref, g_norm_ref = outs
    middle = middle_ref[...]
    inv = lax.rsqrt(jnp.mean(middle * middle, axis=1, keepdims=True) + 1e-06)
    normed = middle * inv
    prod = total * normed
    g_norm_ref[...] = jnp.sum(prod, axis=0, keepdims=True)
    scaled = total * norm_ref[...]
    mean = jnp.mean(prod * norm_ref[...], axis=1, keepdims=True)
    g_middle = g_ref[...].astype(F32) + inv * (scaled - normed * mean)
    g_middle_ref[...] = g_middle
    return (valid_ref[...] * g_middle).astype(BF)


def post_input_grad(total, extras, outs):
    x_ref, g_middle_ref, norm_ref = extras
    grad_in_ref, g_norm_ref = outs
    x = x_ref[...].astype(F32)
    inv = lax.rsqrt(jnp.mean(x * x, axis=1, keepdims=True) + 1e-06)
    normed = x * inv
    prod = total * normed
    g_norm_ref[...] = jnp.sum(prod, axis=0, keepdims=True)
    scaled = total * norm_ref[...]
    mean = jnp.mean(prod * norm_ref[...], axis=1, keepdims=True)
    grad_in_ref[...] = (g_middle_ref[...] + inv * (scaled - normed * mean)).astype(BF)


def post_block_out(total, extras, outs):
    middle_ref, valid_ref = extras
    out_ref, stat_ref = outs
    mlp_part = valid_ref[...] * total
    result = middle_ref[...] + mlp_part
    out_ref[...] = result.astype(BF)
    stat_ref[0:1, :] = jnp.sum(valid_ref[...] * result * result, axis=0, keepdims=True)
    stat_ref[1:2, :] = jnp.sum(mlp_part * mlp_part, axis=0, keepdims=True)


def grids(t):
    rows = lax.broadcasted_iota(jnp.int32, (t, t), 0)
    cols = lax.broadcasted_iota(jnp.int32, (t, t), 1)
    return rows, cols


def allowed_of(seg_row, rows, cols):
    t = rows.shape[0]
    along = jnp.broadcast_to(seg_row, (t, t))
    return (along == jnp.transpose(along)) & (cols <= rows)


def build_bands(score_ref, bands, heads, taps, span, rows, cols):
    t = rows.shape[0]
    diff = cols - rows + (span - 1) // 2

    @pl.loop(0, heads)
    def _(h):
        for a in range(taps):
            band = jnp.zeros((t, t), F32)
            for b in range(span):
                band = jnp.where(diff == b, score_ref[h, a * span + b], band)
            bands[h, a * t : (a + 1) * t, :] = band.astype(BF)


def lagged(masked, taps, rows):
    parts = [masked.astype(BF)]
    for a in range(1, taps):
        parts.append(jnp.where(rows >= a, pltpu.roll(masked, a, 0), 0.0).astype(BF))
    return jnp.concatenate(parts, axis=1)


def attend_kernel(heads, hd, taps, span, score_ref, mix_ref, qkv_ref, seg_ref, gain_ref, head_in_ref, hat_ref, inv_ref, probs_ref, masked_ref, bands):
    t = qkv_ref.shape[1]
    width = heads * hd
    rows, cols = grids(t)

    @pl.when(pl.program_id(0) == 0)
    def _():
        build_bands(score_ref, bands, heads, taps, span, rows, cols)

    allowed = allowed_of(seg_ref[0, 0:1, :], rows, cols)
    for pair in range(heads // 2):
        probs = []
        for c in range(2):
            h = 2 * pair + c
            q = qkv_ref[0, :, h * hd : (h + 1) * hd]
            k = qkv_ref[0, :, width + h * hd : width + (h + 1) * hd]
            masked = jnp.where(allowed, dot(q, k, NT) * hd**-0.5, 0.0)
            masked_ref[0, h] = masked.astype(BF)
            conv = dot(lagged(masked, taps, rows), bands[h])
            logits = jnp.where(allowed, conv, -1e30)
            e = jnp.exp(logits - jnp.max(logits, axis=1, keepdims=True))
            p = e / jnp.sum(e, axis=1, keepdims=True)
            probs_ref[0, h] = p
            probs.append(p)
        for e in range(2):
            h = 2 * pair + e
            mixed = (mix_ref[h, 0] * probs[0] + mix_ref[h, 1] * probs[1]).astype(BF)
            v = qkv_ref[0, :, 2 * width + h * hd : 2 * width + (h + 1) * hd]
            out = dot(mixed, v)
            centred = out - jnp.mean(out, axis=1, keepdims=True)
            inv = lax.rsqrt(jnp.mean(centred * centred, axis=1, keepdims=True) + 1e-05)
            hat_ref[0, :, h * hd : (h + 1) * hd] = centred * inv
            inv_ref[0, :, h * hd : (h + 1) * hd] = jnp.broadcast_to(inv, (t, hd))
    head_in_ref[0] = (hat_ref[0] * gain_ref[...]).astype(BF)


def attend(score, mix, qkv, seg, gain, heads, hd, taps, span):
    n, t, _ = qkv.shape
    width = heads * hd

    def row(*shape):
        return pl.BlockSpec((1,) + shape, lambda i: (i,) + (0,) * len(shape))

    def out(dtype, *shape):
        return jax.ShapeDtypeStruct((n,) + shape, dtype)

    return pl.pallas_call(
        functools.partial(attend_kernel, heads, hd, taps, span),
        grid=(n,),
        out_shape=(out(BF, t, width), out(F32, t, width), out(F32, t, width), out(F32, heads, t, t), out(BF, heads, t, t)),
        in_specs=[smem_spec(), smem_spec(), row(t, 3 * width), row(8, t), pl.BlockSpec((1, width), lambda i: (0, 0))],
        out_specs=(row(t, width), row(t, width), row(t, width), row(heads, t, t), row(heads, t, t)),
        scratch_shapes=[pltpu.VMEM((heads, taps * t, t), BF)],
        compiler_params=pltpu.CompilerParams(vmem_limit_bytes=VMEM_LIMIT),
    )(score, mix, qkv, seg, gain)


def attend_back_kernel(heads, hd, taps, span, score_ref, mix_ref, qkv_ref, seg_ref, gain_ref, g_in_ref, hat_ref, inv_ref, probs_ref, masked_ref, g_qkv_ref, g_gain_ref, g_score_ref, g_mix_ref, bands, corr, g_wide):
    t = qkv_ref.shape[1]
    width = heads * hd
    rows, cols = grids(t)
    step = pl.program_id(0)

    @pl.when(step == 0)
    def _():
        build_bands(score_ref, bands, heads, taps, span, rows, cols)
        corr[...] = jnp.zeros_like(corr)
        g_gain_ref[...] = jnp.zeros_like(g_gain_ref)
        g_mix_ref[...] = jnp.zeros_like(g_mix_ref)

    allowed = allowed_of(seg_ref[0, 0:1, :], rows, cols)
    g_in = g_in_ref[0]
    g_gain_ref[...] += jnp.sum(g_in * hat_ref[0], axis=0, keepdims=True)
    g_wide[:, :width] = g_in * gain_ref[...]
    for pair in range(heads // 2):
        g_heads = []
        g_mixed = []
        probs = [probs_ref[0, 2 * pair + c] for c in range(2)]
        for e in range(2):
            h = 2 * pair + e
            scaled = g_wide[:, h * hd : (h + 1) * hd]
            hat = hat_ref[0, :, h * hd : (h + 1) * hd]
            inv = inv_ref[0, :, h * hd : (h + 1) * hd]
            g = inv * (scaled - jnp.mean(scaled, axis=1, keepdims=True) - hat * jnp.mean(scaled * hat, axis=1, keepdims=True))
            g = g.astype(BF)
            g_heads.append(g)
            v = qkv_ref[0, :, 2 * width + h * hd : 2 * width + (h + 1) * hd]
            g_mixed.append(dot(g, v, NT))
        for e in range(2):
            h = 2 * pair + e
            mixed = (mix_ref[h, 0] * probs[0] + mix_ref[h, 1] * probs[1]).astype(BF)
            g_wide[:, 2 * width + h * hd : 2 * width + (h + 1) * hd] = dot(mixed, g_heads[e], TN)
            for c in range(2):
                place = (2 * pair + e) * 2 + c
                g_mix_ref[place : place + 1, :] += jnp.sum(g_mixed[e] * probs[c], axis=0, keepdims=True)
        for c in range(2):
            h = 2 * pair + c
            g_probs = mix_ref[2 * pair, c] * g_mixed[0] + mix_ref[2 * pair + 1, c] * g_mixed[1]
            weighted = probs[c] * g_probs
            g_conv = weighted - probs[c] * jnp.sum(weighted, axis=1, keepdims=True)
            corr[h] += dot(lagged(masked_ref[0, h].astype(F32), taps, rows), g_conv.astype(BF), TN)
            parts = [g_conv.astype(BF)]
            for a in range(1, taps):
                parts.append(jnp.where(rows < t - a, pltpu.roll(g_conv, t - a, 0), 0.0).astype(BF))
            g_masked = jnp.zeros((t, t), F32)
            for a in range(taps):
                g_masked += dot(parts[a], bands[h, a * t : (a + 1) * t, :], NT)
            g_raw = jnp.where(allowed, g_masked, 0.0).astype(BF)
            q = qkv_ref[0, :, h * hd : (h + 1) * hd]
            k = qkv_ref[0, :, width + h * hd : width + (h + 1) * hd]
            g_k = dot(g_raw, q, TN) * hd**-0.5
            g_wide[:, width + h * hd : width + (h + 1) * hd] = g_k
            g_q = dot(g_raw, k) * hd**-0.5
            g_qkv_ref[0, :, h * hd : (h + 1) * hd] = g_q.astype(BF)
    g_qkv_ref[0, :, width:] = g_wide[:, width:].astype(BF)

    @pl.when(step == pl.num_programs(0) - 1)
    def _():
        diff = cols - rows + (span - 1) // 2

        @pl.loop(0, heads)
        def _(h):
            for a in range(taps):
                tile = corr[h, a * t : (a + 1) * t, :]
                for b in range(span):
                    g_score_ref[h, a * span + b : a * span + b + 1, :] = jnp.sum(
                        jnp.where(diff == b, tile, 0.0), axis=0, keepdims=True
                    )


def attend_back(score, mix, qkv, seg, gain, g_in, hat, inv, probs, masked, heads, hd, taps, span):
    n, t, _ = qkv.shape
    width = heads * hd
    lines = -(-taps * span // 8) * 8

    def row(*shape):
        return pl.BlockSpec((1,) + shape, lambda i: (i,) + (0,) * len(shape))

    def whole(*shape):
        return pl.BlockSpec(shape, lambda i: (0,) * len(shape))

    return pl.pallas_call(
        functools.partial(attend_back_kernel, heads, hd, taps, span),
        grid=(n,),
        out_shape=(
            jax.ShapeDtypeStruct((n, t, 3 * width), BF),
            jax.ShapeDtypeStruct((1, width), F32),
            jax.ShapeDtypeStruct((heads, lines, t), F32),
            jax.ShapeDtypeStruct((2 * heads, t), F32),
        ),
        in_specs=[
            smem_spec(),
            smem_spec(),
            row(t, 3 * width),
            row(8, t),
            whole(1, width),
            row(t, width),
            row(t, width),
            row(t, width),
            row(heads, t, t),
            row(heads, t, t),
        ],
        out_specs=(row(t, 3 * width), whole(1, width), whole(heads, lines, t), whole(2 * heads, t)),
        scratch_shapes=[
            pltpu.VMEM((heads, taps * t, t), BF),
            pltpu.VMEM((heads, taps * t, t), F32),
            pltpu.VMEM((t, 3 * width), F32),
        ],
        compiler_params=pltpu.CompilerParams(vmem_limit_bytes=VMEM_LIMIT),
    )(score, mix, qkv, seg, gain, g_in, hat, inv, probs, masked)


def per_device(
    hidden_in,
    doc_lengths,
    w_query,
    w_key,
    w_value,
    w_output,
    w_gate,
    w_up,
    w_down,
    attn_norm,
    mlp_norm,
    head_norm,
    score_kernel,
    head_mixing,
    grad_out,
):
    _, t, d = hidden_in.shape
    reps = lax.axis_size("rep")
    shards = lax.axis_size("fsdp")
    me = lax.axis_index("rep")
    hidden = w_gate.shape[1]
    heads = H // reps
    hd = d // H
    quarter = d // reps
    units = hidden // reps
    strip = units // shards
    taps, span = score_kernel.shape[1:]
    docs = doc_lengths.shape[1] - 1
    shape_of = jax.ShapeDtypeStruct

    def mine(array, size, axis):
        return lax.dynamic_slice_in_dim(array, me * size, size, axis)

    first_shard = jnp.concatenate([mine(w, quarter, 1) for w in (w_query, w_key, w_value, w_output)], axis=1)
    rows_here = w_gate.shape[0]

    def strips(w):
        return mine(w.reshape(rows_here, shards, reps, strip), 1, 2).reshape(rows_here, units)

    mlp_shard = jnp.concatenate([strips(w_gate), strips(w_up)], axis=1)
    down_shard = mine(w_down, strip, 0)
    w_first = lax.all_gather(first_shard, "fsdp", axis=0, tiled=True)
    w_mlp = lax.all_gather(mlp_shard, "fsdp", axis=0, tiled=True)
    w_dn = lax.all_gather(down_shard, "fsdp", axis=0, tiled=True)

    boundary = jnp.cumsum(doc_lengths[:, :-1], axis=1)
    places = jnp.arange(t, dtype=jnp.int32)
    seg_ids = jnp.sum((places[None, :, None] >= boundary[:, None, :]).astype(jnp.int32), axis=2)
    seg_own = jnp.broadcast_to(seg_ids.astype(F32), (8, t))
    valid = (seg_ids < docs).astype(F32).reshape(t, 1)
    x = hidden_in.reshape(t, d)
    g_out = grad_out.reshape(t, d)
    gain_first, gain_second = attn_norm.reshape(1, d), mlp_norm.reshape(1, d)
    gain_head = mine(head_norm, quarter, 0).reshape(1, quarter)
    score = mine(score_kernel.reshape(H, taps * span), heads, 0)
    mix = mine(head_mixing, heads, 0)

    attn_in, g_mlp, seg = gather_inputs(x, g_out, seg_own, gain_first)
    tokens = reps * t
    flat = lambda a: a.reshape(tokens, a.shape[-1])
    stacked = lambda a: a.reshape(reps, t, a.shape[-1])

    qkv = dot(flat(attn_in), w_first[:, : 3 * quarter]).astype(BF)
    head_in, hat, inv, probs, masked = attend(score, mix, stacked(qkv), seg, gain_head, heads, hd, taps, span)
    w_out_cols = w_first[:, 3 * quarter :].reshape(reps, quarter, quarter)
    w_out = lax.all_to_all(w_out_cols, "rep", 0, 0, tiled=True)
    w_out = jnp.moveaxis(w_out, 0, 1).reshape(quarter, d)

    mlp_in, middle, stat_attn = exchange(
        2, head_in, w_out, NN, (x, valid, gain_second), post_attn_out, True,
        (shape_of((t, d), F32), shape_of((1, d), F32)),
    )
    gate_up = dot(flat(mlp_in), w_mlp)
    gate, upper = gate_up[:, :units], gate_up[:, units:]
    sig = jax.nn.sigmoid(gate)
    silu = gate * sig
    hidden_act = (silu * upper).astype(BF)
    d_down = dot(hidden_act, flat(g_mlp), TN).astype(BF)
    s_down = lax.psum_scatter(d_down, "fsdp", scatter_dimension=0, tiled=True)
    g_hidden = dot(flat(g_mlp), w_dn, NT)
    g_gate = g_hidden * upper * sig * (1.0 + gate * (1.0 - sig))
    g_upper = g_hidden * silu
    g_gu = jnp.concatenate([g_gate, g_upper], axis=1).astype(BF)
    d_mlp = dot(flat(mlp_in), g_gu, TN).astype(BF)
    s_mlp = lax.psum_scatter(d_mlp, "fsdp", scatter_dimension=0, tiled=True)

    g_attn, g_middle, g_second = exchange(
        3, stacked(g_gu), w_mlp, NT, (middle, g_out, valid, gain_second), post_mlp_grad, True,
        (shape_of((t, d), F32), shape_of((1, d), F32)),
    )
    g_head_in = dot(flat(g_attn), w_out, NT)
    g_qkv, g_gain, g_score, g_mix = attend_back(
        score, mix, stacked(qkv), seg, gain_head, stacked(g_head_in), hat, inv, probs, masked, heads, hd, taps, span
    )
    d_out_rows = dot(flat(head_in), flat(g_attn), TN).astype(BF)
    d_out = lax.all_to_all(
        jnp.moveaxis(d_out_rows.reshape(quarter, reps, quarter), 1, 0), "rep", 0, 0, tiled=True
    ).reshape(d, quarter)
    d_qkv = dot(flat(attn_in), flat(g_qkv), TN).astype(BF)
    s_first = lax.psum_scatter(jnp.concatenate([d_qkv, d_out], axis=1), "fsdp", scatter_dimension=0, tiled=True)

    grad_in, g_first = exchange(
        4, g_qkv, w_first[:, : 3 * quarter], NT, (x, g_middle, gain_first), post_input_grad, False,
        (shape_of((t, d), BF), shape_of((1, d), F32)),
    )
    block_out, stat_out = exchange(
        5, stacked(hidden_act), w_dn, NN, (middle, valid), post_block_out, False,
        (shape_of((t, d), BF), shape_of((8, d), F32)),
    )

    spread = lambda a: lax.dynamic_update_slice_in_dim(
        jnp.zeros((reps * a.shape[0],), F32), a, me * a.shape[0], 0
    )
    packed = jnp.concatenate(
        [
            g_first[0],
            g_second[0],
            spread(g_gain[0]),
            spread(jnp.sum(g_score[:, : taps * span], axis=2).reshape(-1)),
            spread(jnp.sum(g_mix, axis=1)),
            jnp.stack([jnp.sum(stat_out[0]), jnp.sum(stat_attn), jnp.sum(stat_out[1]), jnp.sum(valid)]),
        ]
    )
    packed = lax.psum(packed, ("rep", "fsdp"))
    ends = [d, 2 * d, 3 * d, 3 * d + H * taps * span, 3 * d + H * taps * span + 2 * H]
    small_first, small_second, small_head, small_score, small_mix, stats = jnp.split(packed, ends)
    root_means = jnp.sqrt(stats[:3] / (stats[3] * d))

    a_first, a_mlp, a_down = gather_grads(s_first, s_mlp, s_down)
    first = a_first.astype(F32).reshape(reps, rows_here, 4, quarter)
    first = jnp.moveaxis(first, 0, 2).reshape(rows_here, 4, d)
    mlp = a_mlp.astype(F32).reshape(reps, rows_here, 2, shards, strip)
    mlp = jnp.moveaxis(mlp, 0, 3).reshape(rows_here, 2, hidden)
    down = a_down.astype(F32).reshape(w_down.shape)
    return (
        block_out.reshape(hidden_in.shape),
        grad_in.reshape(hidden_in.shape),
        first[:, 0],
        first[:, 1],
        first[:, 2],
        first[:, 3],
        mlp[:, 0],
        mlp[:, 1],
        down,
        small_first,
        small_second,
        small_head,
        small_score.reshape(score_kernel.shape),
        small_mix.reshape(head_mixing.shape),
        root_means,
    )


def solution(mesh):
    rows = P(("rep", "fsdp"), None, None)
    split = P("fsdp", None)
    placed = (rows, P(("rep", "fsdp"), None)) + (split,) * 7 + (P(),) * 5 + (rows,)
    return jax.shard_map(
        per_device,
        mesh=mesh,
        in_specs=placed,
        out_specs=(rows, rows) + (split,) * 7 + (P(),) * 6,
        check_vma=False,
    )
```

time: 3260 us -> 673 us (0.21)
  waiting for transfers between devices: 1440 us -> 244 us
  other arithmetic: 801 us -> 13.3 us
  local copies, waits for them, and re-layouts: 754 us -> 103 us
  Pallas kernels: 0 us -> 195 us
  matrix products: 174 us -> 40.6 us
    all_gather x4 -> x3, waiting for transfers between devices: 868 us -> 126 us  [the longest x1 63.4 us: per_device(): w_first = lax.all_gather(first_shard, 'fsdp', axis=0, tiled=True)]
    all_to_all x4 -> x2, waiting for transfers between devices: 383 us -> 0.01 us  [the longest x1 0.01 us: per_device(): w_out = lax.all_to_all(w_out_cols, 'rep', 0, 0, tiled=True)]
    convert_element_type x14 -> x2, other arithmetic: 378 us -> 0.01 us  [the longest x1 0.01 us: per_device(): seg_own = jnp.broadcast_to(seg_ids.astype(F32), (8, t))]
    unnamed x108 -> x95, local copies, waits for them, and re-layouts: 356 us -> 20.1 us
    reduce_sum x59 -> x6, other arithmetic: 205 us -> 2.19 us  [the longest x1 0.63 us: per_device(): jnp.sum(stat_out[1])]
    pallas_call x0 -> x8, Pallas kernels: none -> 195 us  [the longest x4 90.6 us: exchange(): pl.pallas_call(functools.partial(exchange_kernel, dims, post, gather, len...]
    psum x1 -> x0, waiting for transfers between devices: 186 us -> none  [per_device(): lax.psum(group_row.astype(jnp.bfloat16), 'rep').astype(jnp.float32)[0]]
    concatenate x3 -> x4, other arithmetic: 188 us -> 8.15 us  [the longest x1 4.91 us: per_device(): jnp.concatenate([d_qkv, d_out], axis=1)]
  transfers between devices with their start and end apart: 9 -> 8, of which waited for: 6 -> 4; matrix products, arithmetic and copies ran while one was open for 35% -> 12% of each run, Pallas kernels for 0% -> 23%
where the time goes in v1:
time: 673 us; the launch traced here: 662 us
  waiting for transfers between devices  244 us (36%)
  Pallas kernels  195 us (29%)
  local copies, waits for them, and re-layouts  103 us (15%)
  blocking collectives  40.7 us (6%)
  matrix products  40.6 us (6%)
  between operations  15.8 us (2%)
  other arithmetic  13.3 us (2%)
  starting transfers between devices  10.8 us (2%)
    reduce_scatter x1, waiting for transfers between devices, per_device(): s_mlp = lax.psum_scatter(d_mlp, 'fsdp', scatter_dimension=0, tiled=True)  118 us
    pallas_call x4, Pallas kernels, exchange(): pl.pallas_call(functools.partial(exchange_kernel, dims, post, gather, len...  90.6 us
    all_gather x1, waiting for transfers between devices, per_device(): w_first = lax.all_gather(first_shard, 'fsdp', axis=0, tiled=True)  63.4 us
    all_gather x1, waiting for transfers between devices, per_device(): w_dn = lax.all_gather(down_shard, 'fsdp', axis=0, tiled=True)  53.8 us
    pallas_call x1, Pallas kernels, gather_grads(): pl.pallas_call(functools.partial(grads_kernel, count), out_shape=tuple((j...  43.3 us
    psum x1, blocking collectives, per_device(): packed = lax.psum(packed, ('rep', 'fsdp'))  40.7 us
    dot_general x8, matrix products, dot(): return lax.dot_general(a, b, dims, preferred_element_type=F32)  40.6 us
    pallas_call x1, Pallas kernels, gather_inputs(): pl.pallas_call(inputs_kernel, out_shape=(jax.ShapeDtypeStruct((4, t, d),...  35 us
  transfers between devices with their start and end apart: 8, of which 4 were waited for; matrix products, arithmetic and copies ran while one was open for 12% of the time, Pallas kernels for 23%

profile of v1, /device:TPU:9, one launch (start us, length us, event | category | flops | bytes accessed | tf_op | source)
XLA Modules:
  0.0 662.4 jit_solution(4683192670296616860)
XLA Ops:
  17.0 6.1 dynamic-slice_reduce_fusion
  26.4 63.4 %all-gather.4.cloned.1.call-done = bf16[1536,1536]{1,0:T(8,128)(2,1)} async-done(((bf16[192,1536]{1,0:T(8,128)(2,1)}), bf16[1536,1536]{1,0:T(8,128)(2,1)}) %all-gather.4.cloned.1.call-update) | async-done | bytes 4718608 | tf_op jit(solution)/shard_map/all_gather | solution.py:527
  92.3 5.9 all-to-all-start
  98.6 35.0 %shard_map.262 = (bf16[4,128,1536]{2,1,0:T(8,128)(2,1)S(1)}, bf16[4,128,1536]{2,1,0:T(8,128)(2,1)S(1)}, f32[4,8,128]{2,1,0:T(8,128)S(1)}) custom-call(bf16[128,1536]{1,0:T(8,128)(2,1)S(1)} %bitcast.92, bf16[128,1536]{1,0:T(8,128)(2,1)S(1)} %bitcast.95, f32[8,128]{1,0:T(8,128)S(1)} %broadcast_in_dim.16.seg_ref, f32[1,1536]{1,0:T(1,128)S(1)} %reshape.227.norm_ref.refs_2_), custom_call_target="tpu_custom_call" | custom-call | tf_op jit(solution)/shard_map/pallas_call | solution.py:110
  133.6 5.9 convolution_convert_fusion.2
  139.5 9.4 %shard_map.263 = (bf16[4,128,384]{2,1,0:T(8,128)(2,1)S(1)}, f32[4,128,384]{2,1,0:T(8,128)S(1)}, f32[4,128,384]{2,1,0:T(8,128)S(1)}, f32[4,4,128,128]{3,2,1,0:T(8,128)S(1)}, bf16[4,4,128,128]{3,2,1,0:T(8,128)(2,1)S(1)}) custom-call(f32[4,66]{1,0:T(4,128)S(1)} %constant_dynamic-slice_fusion.6.score_ref, f32[4,2]{1,0:T(4,128)S(1)} %copy.81.mix_ref, ...), custom_call_target="tpu_custom_call" | custom-call | tf_op jit(solution)/shard_map/pallas_call | solution.py:359
  154.0 25.7 %shard_map.264 = (bf16[4,128,1536]{2,1,0:T(8,128)(2,1)S(1)}, f32[128,1536]{1,0:T(8,128)S(1)}, f32[1,1536]{1,0:T(1,128)S(1)}) custom-call(bf16[4,128,384]{2,1,0:T(8,128)(2,1)S(1)} %copy-done.23, bf16[384,1536]{1,0:T(8,128)(2,1)S(1)} %bitcast.91, bf16[128,1536]{1,0:T(8,128)(2,1)S(1)} %bitcast.93, f32[128,1]{1,0:T(8,128)S(1)} %copy.64.refs_1_.refs_2_, ...), custom_call_target="tpu_custom_call" | custom-call | tf_op jit(solution)/shard_map/pallas_call | solution.py:207
  180.9 8.7 %all-gather.6.cloned.1.call-done.rhs_ref = bf16[1536,2048]{1,0:T(8,128)(2,1)} async-done(((bf16[192,2048]{1,0:T(8,128)(2,1)}), bf16[1536,2048]{1,0:T(8,128)(2,1)}) %all-gather.6.cloned.1.call-update) | async-done | bytes 6291472 | tf_op jit(solution)/shard_map/all_gather | solution.py:528
  189.6 8.7 %fusion.12 = f32[512,2048]{1,0:T(8,128)} fusion(bf16[512,1536]{1,0:T(8,128)(2,1)} %bitcast.100, bf16[1536,2048]{1,0:T(8,128)(2,1)} %all-gather.6.cloned.1.call-done.rhs_ref), kind=kOutput, calls=%fused_computation.51 | convolution fusion | flops 3221225472 | bytes 12058624 | tf_op jit(solution)/shard_map/dot_general | solution.py:21
  198.3 53.8 %all-gather.8.cloned.1.call-done.rhs_ref = bf16[1024,1536]{1,0:T(8,128)(2,1)} async-done(((bf16[128,1536]{1,0:T(8,128)(2,1)}), bf16[1024,1536]{1,0:T(8,128)(2,1)}) %all-gather.8.cloned.1.call-update) | async-done | bytes 3145744 | tf_op jit(solution)/shard_map/all_gather | solution.py:529
  252.1 7.2 %multiply_convert_fusion.1 = (bf16[512,1024]{1,0:T(8,128)(2,1)S(1)}, bf16[512,1024]{1,0:T(8,128)(2,1)}, bf16[512,1024]{1,0:T(8,128)(2,1)S(1)}) fusion(f32[512,2048]{1,0:T(8,128)} %fusion.12, bf16[512,1536]{1,0:T(8,128)(2,1)} %bitcast.103, bf16[1024,1536]{1,0:T(8,128)(2,1)} %all-gather.8.cloned.1.call-done.rhs_ref), kind=kOutput, calls=%fused_computation.15 | convolution fusion | flops 1618477056 | bytes 12058624 | tf_op jit(solution)/shard_map/dot_general | solution.py:21
  265.3 32.7 %shard_map.266 = (bf16[4,128,1536]{2,1,0:T(8,128)(2,1)S(1)}, f32[128,1536]{1,0:T(8,128)S(1)}, f32[1,1536]{1,0:T(1,128)S(1)}) custom-call(bf16[4,128,2048]{2,1,0:T(8,128)(2,1)S(1)} %pad_maximum_fusion.1.lhs_ref, bf16[1536,2048]{1,0:T(8,128)(2,1)} %all-gather.6.cloned.1.call-done.rhs_ref, f32[128,1536]{1,0:T(8,128)S(1)} %get-tuple-element.44.refs_0_, ...), custom_call_target="tpu_custom_call" | custom-call | tf_op jit(solution)/shard_map/pallas_call | solution.py:207
  314.2 16.4 %shard_map.267 = (bf16[4,128,1152]{2,1,0:T(8,128)(2,1)S(1)}, f32[1,384]{1,0:T(1,128)S(1)}, f32[4,72,128]{2,1,0:T(8,128)S(1)}, f32[8,128]{1,0:T(8,128)S(1)}) custom-call(f32[4,66]{1,0:T(4,128)S(1)} %constant_dynamic-slice_fusion.6.score_ref, f32[4,2]{1,0:T(4,128)S(1)} %copy.81.mix_ref, bf16[4,128,1152]{2,1,0:T(8,128)(2,1)} %bitcast.90, ...), custom_call_target="tpu_custom_call" | custom-call | tf_op jit(solution)/shard_map/pallas_call | solution.py:454
  339.8 8.1 %convolution_convert_fusion = bf16[1536,2048]{1,0:T(8,128)(2,1)} fusion(bf16[512,1536]{1,0:T(8,128)(2,1)} %bitcast.101, bf16[512,1024]{1,0:T(8,128)(2,1)} %get-tuple-element.115, bf16[512,1024]{1,0:T(8,128)(2,1)} %copy-done.37), kind=kOutput, calls=%fused_computation.2 | convolution fusion | flops 3228565504 | bytes 9961472 | tf_op jit(solution)/shard_map/dot_general | solution.py:21
  354.8 17.0 %shard_map.268 = (bf16[128,1536]{1,0:T(8,128)(2,1)S(1)}, f32[1,1536]{1,0:T(1,128)S(1)}) custom-call(bf16[4,128,1152]{2,1,0:T(8,128)(2,1)S(1)} %get-tuple-element.52.lhs_ref, bf16[1536,1152]{1,0:T(8,128)(2,1)} %slice.75.rhs_ref, bf16[128,1536]{1,0:T(8,128)(2,1)S(1)} %bitcast.94, f32[128,1536]{1,0:T(8,128)S(1)} %copy-done.13, ...), custom_call_target="tpu_custom_call" | custom-call | tf_op jit(solution)/shard_map/pallas_call | solution.py:207
  376.6 15.0 %shard_map.265 = (bf16[128,1536]{1,0:T(8,128)(2,1)S(1)}, f32[8,1536]{1,0:T(8,128)S(1)}) custom-call(bf16[4,128,1024]{2,1,0:T(8,128)(2,1)S(1)} %bitcast.97, bf16[1024,1536]{1,0:T(8,128)(2,1)S(1)} %copy-done.4, f32[128,1536]{1,0:T(8,128)S(1)} %get-tuple-element.44.refs_0_, f32[128,1]{1,0:T(8,128)S(1)} %copy.64.refs_1_.refs_2_), custom_call_target="tpu_custom_call" | custom-call | tf_op jit(solution)/shard_map/pallas_call | solution.py:207
  395.0 40.7 %psum.7 = f32[5700]{0:T(1024)S(1)} all-reduce(f32[5700]{0:T(1024)S(1)} %concatenate.31), channel_id=1, replica_groups=mesh['rep'=4,'fsdp'=8] {'rep','fsdp'}, use_global_device_ids=true, to_apply=%region_11.12 | all-reduce | flops 5700 | bytes 45600 | tf_op jit(solution)/shard_map/psum | solution.py:609
  439.9 117.6 %reduce-scatter.6.cloned.1.call-done.refs_1_ = bf16[192,2048]{1,0:T(8,128)(2,1)} async-done(((bf16[1536,2048]{1,0:T(8,128)(2,1)}), bf16[192,2048]{1,0:T(8,128)(2,1)}) %reduce-scatter.6.cloned.1.call-update) | async-done | bytes 786448 | tf_op jit(solution)/shard_map/reduce_scatter | solution.py:570
  560.7 43.3 %shard_map.269 = (bf16[4,192,1536]{2,1,0:T(8,128)(2,1)S(1)}, bf16[4,192,2048]{2,1,0:T(8,128)(2,1)}, bf16[4,128,1536]{2,1,0:T(8,128)(2,1)S(1)}) custom-call(bf16[192,1536]{1,0:T(8,128)(2,1)S(1)} %copy-done.18, bf16[192,2048]{1,0:T(8,128)(2,1)S(1)} %copy-done.11, bf16[128,1536]{1,0:T(8,128)(2,1)S(1)} %copy-done.21), custom_call_target="tpu_custom_call" | custom-call | tf_op jit(solution)/shard_map/pallas_call | solution.py:149
  610.9 7.5 %copy.73 = f32[192,4,4,384]{3,2,0,1:T(4,128)} copy(f32[192,4,4,384]{3,1,0,2:T(4,128)} %bitcast.106) | data formatting | bytes 9437184 | tf_op jit(solution)/shard_map/reshape | solution.py:616
  618.5 6.4 reshape.258
  630.6 6.7 %copy.74 = f32[192,2,8,4,128]{4,3,2,0,1:T(4,128)} copy(f32[192,2,8,4,128]{4,2,1,0,3:T(8,128)S(1)} %bitcast.105) | data formatting | bytes 12582912 | tf_op jit(solution)/shard_map/reshape | solution.py:618
  637.3 7.9 %reshape.260 = f32[192,2,4096]{2,0,1:T(8,128)} reshape(f32[192,2,8,4,128]{4,3,2,0,1:T(4,128)} %copy.74) | data formatting | bytes 12582912 | tf_op jit(solution)/shard_map/reshape | solution.py:618
  645.2 6.3 slice_bitcast_fusion
  (170 shorter events, 91.2 us)
Async XLA Ops:
  7.2 17.1 %copy-start = (bf16[512,1536]{1,0:T(8,128)(2,1)S(1)}, bf16[512,1536]{1,0:T(8,128)(2,1)}, u32[]{:S(2)}) copy-start(bf16[512,1536]{1,0:T(8,128)(2,1)} %param.23) | copy-start | bytes 4718596
  7.2 82.7 %all-gather.4.cloned.1.call-start = ((), (), s32[]{:S(2)}) async-start(), calls=%async_computation.5 | async-start | bytes 5308416 | tf_op jit(solution)/shard_map/all_gather | solution.py:527
  10.3 179.3 %all-gather.6.cloned.1.call-start = ((), (), s32[]{:S(2)}) async-start(), calls=%async_computation.6 | async-start | bytes 7077888 | tf_op jit(solution)/shard_map/all_gather | solution.py:528
  23.2 3.2 copy-start.39
  24.3 227.8 %all-gather.8.cloned.1.call-start = ((), (), s32[]{:S(2)}) async-start(), calls=%async_computation.7 | async-start | bytes 3538944 | tf_op jit(solution)/shard_map/all_gather | solution.py:529
  26.4 71.9 %copy-start.38 = (f32[16,6,11]{0,1,2:T(8,128)S(1)}, f32[16,6,11]{0,1,2:T(8,128)}, u32[]{:S(2)}) copy-start(f32[16,6,11]{0,1,2:T(8,128)} %param.27) | copy-start | bytes 12676
  26.4 72.1 %copy-start.3 = (bf16[1,128,1536]{2,1,0:T(8,128)(2,1)S(1)}, bf16[1,128,1536]{2,1,0:T(8,128)(2,1)}, u32[]{:S(2)}) copy-start(bf16[1,128,1536]{2,1,0:T(8,128)(2,1)} %param.15) | copy-start | bytes 1179652
  26.4 72.1 %copy-start.6 = (bf16[1,128,1536]{2,1,0:T(8,128)(2,1)S(1)}, bf16[1,128,1536]{2,1,0:T(8,128)(2,1)}, u32[]{:S(2)}) copy-start(bf16[1,128,1536]{2,1,0:T(8,128)(2,1)} %param.29) | copy-start | bytes 1179652
  92.3 59.9 %all-to-all-start = ((bf16[4,384,384]{2,1,0:T(8,128)(2,1)}), bf16[4,384,384]{2,1,0:T(8,128)(2,1)}, u32[]{:S(2)}, u32[]{:S(2)}) async-start(bf16[4,384,384]{2,1,0:T(8,128)(2,1)} %bitcast.5), calls=%async_computation | async-start | bytes 2359296 | tf_op jit(solution)/shard_map/all_to_all | solution.py:551
  98.2 341.6 %reduce-scatter.8.cloned.1.call-start = ((), (), s32[]{:S(2)}) async-start(), calls=%async_computation.10 | async-start | bytes 3538944 | tf_op jit(solution)/shard_map/reduce_scatter | solution.py:564
  133.5 5.9 copy-start.30
  133.6 5.9 copy-start.32
  139.5 40.3 %copy-start.2 = (bf16[512,1152]{1,0:T(8,128)(2,1)}, bf16[512,1152]{1,0:T(8,128)(2,1)S(1)}, u32[]{:S(2)}) copy-start(bf16[512,1152]{1,0:T(8,128)(2,1)S(1)} %convolution_convert_fusion.2) | copy-start | bytes 3538948
  252.1 7.2 %copy-start.33 = (bf16[4,128,1536]{2,1,0:T(8,128)(2,1)S(1)}, bf16[4,128,1536]{2,1,0:T(8,128)(2,1)}, u32[]{:S(2)}) copy-start(bf16[4,128,1536]{2,1,0:T(8,128)(2,1)} %copy-done.32) | copy-start | bytes 4718596
  259.3 4.6 copy-start.37
  265.3 32.8 %copy-start.24 = (bf16[4,128,384]{2,1,0:T(8,128)(2,1)S(1)}, bf16[4,128,384]{2,1,0:T(8,128)(2,1)}, u32[]{:S(2)}) copy-start(bf16[4,128,384]{2,1,0:T(8,128)(2,1)} %copy-done.22) | copy-start | bytes 1179652
  300.6 34.0 %all-to-all-start.1 = ((bf16[4,384,384]{2,1,0:T(8,128)(2,1)}), bf16[4,384,384]{2,1,0:T(8,128)(2,1)}, u32[]{:S(2)}, u32[]{:S(2)}) async-start(bf16[4,384,384]{2,1,0:T(8,128)(2,1)} %bitcast.85), calls=%async_computation.1 | async-start | bytes 2359296 | tf_op jit(solution)/shard_map/all_to_all | solution.py:581
  305.1 134.7 %reduce-scatter.4.cloned.1.call-start = ((), (), s32[]{:S(2)}) async-start(), calls=%async_computation.8 | async-start | bytes 5308416 | tf_op jit(solution)/shard_map/reduce_scatter | solution.py:585
  305.1 6.5 copy-start.35
  314.2 16.4 %copy-start.31 = (bf16[4,128,1536]{2,1,0:T(8,128)(2,1)S(1)}, bf16[4,128,1536]{2,1,0:T(8,128)(2,1)}, u32[]{:S(2)}) copy-start(bf16[4,128,1536]{2,1,0:T(8,128)(2,1)} %copy-done.30) | copy-start | bytes 4718596
  339.5 217.9 %reduce-scatter.6.cloned.1.call-start = ((), (), s32[]{:S(2)}) async-start(), calls=%async_computation.9 | async-start | bytes 7077888 | tf_op jit(solution)/shard_map/reduce_scatter | solution.py:570
  391.7 48.2 %copy-start.27 = (bf16[128,1536]{1,0:T(8,128)(2,1)}, bf16[128,1536]{1,0:T(8,128)(2,1)S(1)}, u32[]{:S(2)}) copy-start(bf16[128,1536]{1,0:T(8,128)(2,1)S(1)} %get-tuple-element.45) | copy-start | bytes 1179652
  624.9 4.7 copy-start.36
  651.4 3.7 copy-start.1
  (27 other events, 43.4 us)
Sparse Core Ops, SparseCore 0:
  10.8 79.0 all-gather.3
  92.6 96.9 all-gather.5
  192.4 59.6 all-gather.7
  264.0 73.2 reduce-scatter.7
  340.8 96.7 reduce-scatter.3
  440.9 116.4 reduce-scatter.5

commit v2 on v0

v2 whole, which is shorter than its diff:
```python
import functools

import jax
import jax.numpy as jnp
from jax import lax
from jax.experimental import pallas as pl
from jax.experimental.pallas import tpu as pltpu
from jax.sharding import PartitionSpec as P

H = 16
BF = jnp.bfloat16
F32 = jnp.float32
MESH = pl.DeviceIdType.MESH
VMEM_LIMIT = 61 * 1024 * 1024
NN = (((1,), (0,)), ((), ()))
NT = (((1,), (1,)), ((), ()))
TN = (((0,), (0,)), ((), ()))
FIRST, MLP, DOWN = 0, 1, 2
UP, DN, SIDE = 0, 1, 2
STATS = 4


def dot(a, b, dims=NN):
    return lax.dot_general(a, b, dims, preferred_element_type=F32)


def merge(value):
    n, rows, width = value.shape
    if rows % 16 == 0:
        return value.reshape(n * rows, width)
    return value.astype(F32).reshape(n * rows, width).astype(value.dtype)


def vmem_spec():
    return pl.BlockSpec(memory_space=pltpu.VMEM)


def smem_spec():
    return pl.BlockSpec(memory_space=pltpu.SMEM)


def hbm_spec():
    return pl.BlockSpec(memory_space=pl.ANY)


def grids(t):
    rows = lax.broadcasted_iota(jnp.int32, (t, t), 0)
    cols = lax.broadcasted_iota(jnp.int32, (t, t), 1)
    return rows, cols


def allowed_of(seg_row, rows, cols):
    t = rows.shape[0]
    along = jnp.broadcast_to(seg_row, (t, t))
    return (along == jnp.transpose(along)) & (cols <= rows)


def lagged(masked, taps, rows):
    parts = [masked.astype(BF)]
    for a in range(1, taps):
        parts.append(jnp.where(rows >= a, pltpu.roll(masked, a, 0), 0.0).astype(BF))
    return jnp.concatenate(parts, axis=1)


def row_sum(value):
    return jnp.sum(value, axis=0, keepdims=True)


def mean_of(value):
    return jnp.mean(value, axis=1, keepdims=True)


def layer_kernel(cfg, *refs):
    heads, hd, taps, span, docs, shards, units = cfg
    (
        x_ref, g_ref, seg_ref, valid_ref, gain_first, gain_second, gain_head, score_ref, mix_ref,
        own_first, own_mlp, own_down,
        out_ref, grad_in_ref, small_ref, all_first, all_mlp, all_down,
        land_first, land_mlp, land_down,
        w_first, w_mlp, w_down, wide, g_mlp, seg_all, attn_in, qkv, hat, inv, probs, masked, head_in, w_out,
        middle, slope, silu, hidden, g_gu, g_attn, g_middle, g_qkv, g_hin, d_out, d_out_in,
        psend, pown, r1, ysend, r2, psend2, pown2, r1b, r2b, bands, corr, g_wide, lanes, g_mix,
        stage, small_send, small_recv,
        ag_send, ag_recv, rs_send, rs_recv, rep_send, rep_recv, local,
    ) = refs
    t, d = x_ref.shape
    width = heads * hd
    quarter = d // 4
    lines = shards // 2
    me = lax.axis_index("rep")
    f = lax.axis_index("fsdp")
    plane, core = me // 2, me % 2
    sibling, across = plane * 2 + (1 - core), (1 - plane) * 2 + core
    diagonal = (1 - plane) * 2 + (1 - core)
    z, side = f // 2, f % 2
    partner = 2 * z + (1 - side)
    weights = (w_first, w_mlp, w_down)
    lands = (land_first, land_mlp, land_down)
    peer_of = (f + 2, f - 2, partner)
    tokens = 4 * t
    part = shards // 4
    rows, cols = grids(t)

    def flip(bit):
        return f + (1 - 2 * ((f // bit) % 2)) * bit

    bits = []
    bit = 1
    while bit < shards:
        bits.append(bit)
        bit *= 2

    barrier = pltpu.get_barrier_semaphore()

    def greet(r, s):
        pl.semaphore_signal(barrier, inc=1, device_id=(r, s), device_id_type=MESH)

    for r in (sibling, across, diagonal):
        greet(r, f)
    for bit in bits:
        greet(me, flip(bit))

    @pl.when(z < lines - 1)
    def _():
        greet(me, f + 2)

    @pl.when(z > 0)
    def _():
        greet(me, f - 2)

    ends = (z > 0).astype(jnp.int32) + (z < lines - 1).astype(jnp.int32)
    pl.semaphore_wait(barrier, 3 + len(bits) + ends)

    def rep_copy(src, dst, slot, peer):
        return pltpu.make_async_remote_copy(
            src_ref=src, dst_ref=dst, send_sem=rep_send.at[slot], recv_sem=rep_recv.at[slot],
            device_id=(peer, f), device_id_type=MESH,
        )

    def ag(k, block, way):
        return pltpu.make_async_remote_copy(
            src_ref=weights[k].at[block], dst_ref=weights[k].at[block],
            send_sem=ag_send.at[k, way, block], recv_sem=ag_recv.at[k, block],
            device_id=(me, peer_of[way]), device_id_type=MESH,
        )

    def ag_walk(k, s, first, act):
        sides = (side, 1 - side) if k == DOWN else (side,)
        if isinstance(s, int) and s == 0:
            for q in sides:
                block = 2 * z + q
                if k == DOWN and q is not side:
                    first(k, block)

                @pl.when(z < lines - 1)
                def _():
                    act(k, block, UP)

                @pl.when(z > 0)
                def _():
                    act(k, block, DN)

                if k != DOWN:
                    act(k, block, SIDE)
            return

        @pl.when(z - s >= 0)
        def _():
            for q in sides:
                block = 2 * (z - s) + q
                first(k, block)

                @pl.when(z < lines - 1)
                def _():
                    act(k, block, UP)

                if k != DOWN:
                    act(k, block, SIDE)

        @pl.when(z + s < lines)
        def _():
            for q in sides:
                block = 2 * (z + s) + q
                first(k, block)

                @pl.when(z > 0)
                def _():
                    act(k, block, DN)

                if k != DOWN:
                    act(k, block, SIDE)

    def arrived(k, block):
        ag(k, block, SIDE).wait_recv()

    def go(k, block, way):
        ag(k, block, way).start()

    def gone(k, block, way):
        ag(k, block, way).wait_send()

    def ag_steps(k, low, high):
        if low == 0:
            ag_walk(k, 0, arrived, go)
        else:
            pl.loop(low, high)(lambda s: ag_walk(k, s, arrived, go))

    def ag_done(k):
        if k != DOWN:
            pl.loop(0, lines)(lambda zz: arrived(k, 2 * zz + (1 - side)))

    def ag_drain(k):
        nothing = lambda *_: None
        if k == DOWN:
            gone(k, f, SIDE)
        ag_walk(k, 0, nothing, gone)
        pl.loop(1, lines)(lambda s: ag_walk(k, s, nothing, gone))

    def gather_start(fulls, slot):
        for i, full in enumerate(fulls):
            rep_copy(full.at[me], full.at[me], slot + 3 * i, across).start()
            rep_copy(full.at[me], full.at[me], slot + 3 * i + 1, sibling).start()

    def gather_pass(fulls, slot):
        for i, full in enumerate(fulls):
            rep_copy(full.at[me], full.at[me], slot + 3 * i, across).wait_recv()
            rep_copy(full.at[across], full.at[across], slot + 3 * i + 2, sibling).start()

    def gather_end(fulls, slot):
        for i, full in enumerate(fulls):
            rep_copy(full.at[me], full.at[me], slot + 3 * i + 1, sibling).wait_recv()
            rep_copy(full.at[across], full.at[across], slot + 3 * i + 2, sibling).wait_recv()
        for i, full in enumerate(fulls):
            rep_copy(full.at[me], full.at[me], slot + 3 * i, across).wait_send()
            rep_copy(full.at[me], full.at[me], slot + 3 * i + 1, sibling).wait_send()
            rep_copy(full.at[across], full.at[across], slot + 3 * i + 2, sibling).wait_send()

    def pair_of(ref, a, b):
        return jnp.concatenate([ref[a], ref[b]], axis=0)

    def sum_copies(slot, send_buf, first_land, second_land):
        return (
            rep_copy(send_buf, first_land, slot, sibling),
            rep_copy(ysend, second_land, slot + 1, across),
        )

    def column_chunk(i):
        return pl.ds(pl.multiple_of(i * quarter, quarter), quarter)

    def sum_theirs(product, copies, send_buf):
        @pl.loop(0, 4)
        def _(i):
            value = product(1 - core, 2 + (1 - core), i)
            send_buf[0, :, column_chunk(i)] = value[:t].astype(BF)
            send_buf[1, :, column_chunk(i)] = value[t:].astype(BF)

        copies[0].start()

    def sum_ours(product, own_buf):
        @pl.loop(0, 4)
        def _(i):
            value = product(across, me, i)
            own_buf[0, :, column_chunk(i)] = value[:t]
            own_buf[1, :, column_chunk(i)] = value[t:]

    def sum_turn(copies, own_buf, first_land):
        copies[0].wait_recv()
        ysend[...] = (own_buf[0] + first_land[1 - plane].astype(F32)).astype(BF)
        copies[1].start()
        own_buf[1] = own_buf[1] + first_land[plane].astype(F32)

    def sum_end(copies, own_buf, second_land):
        copies[1].wait_recv()
        total = own_buf[1] + second_land[...].astype(F32)
        copies[0].wait_send()
        copies[1].wait_send()
        return total

    def rs(k, block, way):
        return pltpu.make_async_remote_copy(
            src_ref=weights[k].at[block], dst_ref=lands[k].at[way, block],
            send_sem=rs_send.at[k, way, block], recv_sem=rs_recv.at[k, way, block],
            device_id=(me, peer_of[way]), device_id_type=MESH,
        )

    def rs_add(k, block, way):
        grad = weights[k]
        high, wide_k = grad.shape[1:]
        rs(k, block, way).wait_recv()
        slot = stage.at[pl.ds(0, high), pl.ds(0, wide_k)]
        copy = pltpu.make_async_copy(lands[k].at[way, block], slot, local.at[0])
        copy.start()
        copy.wait()
        step = 16 if high % 16 == 0 else high

        @pl.loop(0, high // step)
        def _(i):
            at = pl.ds(pl.multiple_of(i * step, step), step)
            total = grad[block, at, :].astype(F32) + stage[at, 0:wide_k].astype(F32)
            grad[block, at, :] = total.astype(BF)

    def rs_turn(k, j):
        sides = (side, 1 - side) if k == DOWN else (side,)
        high_target, low_target = lines - 1 - j, j

        @pl.when(high_target > z)
        def _():
            for q in sides:
                block = 2 * high_target + q
                if k != DOWN:
                    rs_add(k, block, SIDE)

                @pl.when(z > 0)
                def _():
                    rs_add(k, block, UP)

                rs(k, block, UP).start()

        @pl.when(low_target < z)
        def _():
            for q in sides:
                block = 2 * low_target + q
                if k != DOWN:
                    rs_add(k, block, SIDE)

                @pl.when(z < lines - 1)
                def _():
                    rs_add(k, block, DN)

                rs(k, block, DN).start()

    def rs_close(k):
        sides = (1 - side, side) if k == DOWN else (side,)
        for q in sides:
            block = 2 * z + q
            if k != DOWN:
                rs_add(k, block, SIDE)

            @pl.when(z > 0)
            def _():
                rs_add(k, block, UP)

            @pl.when(z < lines - 1)
            def _():
                rs_add(k, block, DN)

            if k == DOWN and q is not side:
                rs(k, block, SIDE).start()
        if k == DOWN:
            rs_add(k, f, SIDE)

    def rs_drain(k):
        sides = (side, 1 - side) if k == DOWN else (side,)

        @pl.loop(0, lines)
        def _(zz):
            @pl.when(zz > z)
            def _():
                for q in sides:
                    rs(k, 2 * zz + q, UP).wait_send()

            @pl.when(zz < z)
            def _():
                for q in sides:
                    rs(k, 2 * zz + q, DN).wait_send()

            if k != DOWN:
                rs(k, 2 * zz + (1 - side), SIDE).wait_send()

        if k == DOWN:
            rs(k, partner, SIDE).wait_send()

    outs = (all_first, all_mlp, all_down)

    def final_copies(k, slot):
        own = weights[k].at[f]
        full = outs[k]
        return (
            rep_copy(own, full.at[me], slot, across),
            rep_copy(own, full.at[me], slot + 1, sibling),
            rep_copy(full.at[across], full.at[across], slot + 2, sibling),
            pltpu.make_async_copy(own, full.at[me], local.at[1 + k]),
        )

    def final_start(k, slot):
        a, b, _, here = final_copies(k, slot)
        a.start()
        b.start()
        here.start()

    def final_pass(k, slot):
        a, _, c, _ = final_copies(k, slot)
        a.wait_recv()
        c.start()

    def final_end(k, slot):
        a, b, c, here = final_copies(k, slot)
        b.wait_recv()
        c.wait_recv()
        a.wait_send()
        b.wait_send()
        c.wait_send()
        here.wait()

    owns = (own_first, own_mlp, own_down)
    loads = [pltpu.make_async_copy(owns[k], weights[k].at[f], local.at[4 + k]) for k in range(3)]
    for load in loads:
        load.start()
    wide[me] = x_ref[...]
    g_mlp[me] = g_ref[...]
    seg_all[me] = seg_ref[...]
    entering = (seg_all, wide, g_mlp)
    gather_start(entering, 0)
    loads[FIRST].wait()
    ag_steps(FIRST, 0, 1)

    diff = cols - rows + (span - 1) // 2

    @pl.loop(0, heads)
    def _(h):
        for a in range(taps):
            band = jnp.zeros((t, t), F32)
            for b in range(span):
                band = jnp.where(diff == b, score_ref[h, a * span + b], band)
            bands[h, a * t : (a + 1) * t, :] = band.astype(BF)

    gather_pass(entering, 0)
    ag_steps(FIRST, 1, 2)
    gather_end(entering, 0)

    @pl.loop(0, 4)
    def _(r):
        value = wide[r].astype(F32)
        scale = lax.rsqrt(mean_of(value * value) + 1e-06)
        attn_in[r] = (value * scale * gain_first[...]).astype(BF)
        valid = jnp.transpose(jnp.broadcast_to(seg_all[r][0:1, :], (t, t)))[:, 0:1] < float(docs)
        g_mlp[r] = jnp.where(valid, g_mlp[r].astype(F32), 0.0).astype(BF)

    ag_steps(FIRST, 2, 3)
    loads[MLP].wait()
    loads[DOWN].wait()
    ag_steps(MLP, 0, 1)
    ag_steps(FIRST, 3, lines)
    ag_done(FIRST)

    def w_out_copy(peer, slot):
        return rep_copy(
            w_first.at[pl.ds(peer * part, part), :, pl.ds(3 * quarter, quarter)],
            w_out.at[:, :, pl.ds(pl.multiple_of(me * quarter, quarter), quarter)],
            slot, peer,
        )

    for i, peer in enumerate((sibling, across, diagonal)):
        w_out_copy(peer, 9 + i).start()
    own_out = pltpu.make_async_copy(
        w_first.at[pl.ds(me * part, part), :, pl.ds(3 * quarter, quarter)],
        w_out.at[:, :, pl.ds(pl.multiple_of(me * quarter, quarter), quarter)],
        local.at[0],
    )
    own_out.start()

    for i in range(3):
        value = dot(attn_in[...].reshape(tokens, d), merge(w_first[:, :, i * quarter : (i + 1) * quarter]))
        qkv[:, :, i * quarter : (i + 1) * quarter] = value.astype(BF).reshape(4, t, quarter)
    ag_steps(MLP, 1, 2)

    def split(ref, row, kind, h):
        return ref[row, :, kind * width + h * hd : kind * width + (h + 1) * hd]

    @pl.loop(0, 4)
    def _(row):
        allowed = allowed_of(seg_all[row][0:1, :], rows, cols)
        for pair in range(heads // 2):
            both = []
            for c in range(2):
                h = 2 * pair + c
                scores = dot(split(qkv, row, 0, h), split(qkv, row, 1, h), NT) * hd**-0.5
                kept = jnp.where(allowed, scores, 0.0)
                masked[row, h] = kept.astype(BF)
                logits = jnp.where(allowed, dot(lagged(kept, taps, rows), bands[h]), -1e30)
                e = jnp.exp(logits - jnp.max(logits, axis=1, keepdims=True))
                p = e / jnp.sum(e, axis=1, keepdims=True)
                probs[row, h] = p
                both.append(p)
            for e in range(2):
                h = 2 * pair + e
                mixed = (mix_ref[h, 0] * both[0] + mix_ref[h, 1] * both[1]).astype(BF)
                out = dot(mixed, split(qkv, row, 2, h))
                centred = out - mean_of(out)
                scale = lax.rsqrt(mean_of(centred * centred) + 1e-05)
                hat[row, :, h * hd : (h + 1) * hd] = centred * scale
                inv[row, :, h * hd : (h + 1) * hd] = jnp.broadcast_to(scale, (t, hd))
        head_in[row] = (hat[row] * gain_head[...]).astype(BF)

    for i, peer in enumerate((sibling, across, diagonal)):
        w_out_copy(peer, 9 + i).wait_recv()
    own_out.wait()

    copies = sum_copies(12, psend, r1, r2)
    product = lambda a, b, i: dot(pair_of(head_in, a, b), merge(w_out[:, :, column_chunk(i)]))
    sum_theirs(product, copies, psend)
    sum_ours(product, pown)
    ag_steps(MLP, 2, 3)
    sum_turn(copies, pown, r1)
    ag(DOWN, f, SIDE).start()
    total = sum_end(copies, pown, r2)
    attn_part = valid_ref[...] * total
    value = x_ref[...].astype(F32) + attn_part
    middle[...] = value
    stat_attn = jnp.sum(row_sum(attn_part * attn_part), axis=1, keepdims=True)
    scale = lax.rsqrt(mean_of(value * value) + 1e-06)
    wide[me] = (value * scale * gain_second[...]).astype(BF)
    gather_start((wide,), 14)
    ag_steps(MLP, 3, lines)
    gather_pass((wide,), 14)
    ag_steps(DOWN, 0, 1)
    gather_end((wide,), 14)
    mlp_in = wide
    ag_steps(DOWN, 1, 2)
    ag_done(MLP)

    chunk = 256

    @pl.loop(0, units // chunk)
    def _(i):
        at = pl.ds(pl.multiple_of(i * chunk, chunk), chunk)
        after = pl.ds(pl.multiple_of(units + i * chunk, chunk), chunk)
        operand = mlp_in[...].reshape(tokens, d)
        gate = dot(operand, merge(w_mlp[:, :, at]))
        upper = dot(operand, merge(w_mlp[:, :, after]))
        sig = 1.0 / (1.0 + jnp.exp(-gate))
        act = gate * sig
        hidden[:, :, at] = (act * upper).astype(BF).reshape(4, t, chunk)
        silu[:, at] = act
        slope[:, at] = upper * sig * (1.0 + gate * (1.0 - sig))

    ag_steps(DOWN, 2, 3)
    ag_steps(DOWN, 3, lines)

    @pl.loop(0, 4)
    def _(i):
        span_units = units // 4
        at = pl.ds(pl.multiple_of(i * span_units, span_units), span_units)
        after = pl.ds(pl.multiple_of(units + i * span_units, span_units), span_units)
        g_hidden = dot(g_mlp[...].reshape(tokens, d), merge(w_down[pl.ds(i * part, part)]), NT)
        g_gu[:, :, at] = (g_hidden * slope[:, at]).astype(BF).reshape(4, t, span_units)
        g_gu[:, :, after] = (g_hidden * silu[:, at]).astype(BF).reshape(4, t, span_units)

    mlp_copies = sum_copies(17, psend, r1, r2)
    product = lambda a, b, i: dot(pair_of(g_gu, a, b), merge(w_mlp[pl.ds(i * part, part)]), NT)
    sum_theirs(product, mlp_copies, psend)
    sum_ours(product, pown)

    out_copies = (rep_copy(psend2, r1b, 19, sibling), rep_copy(ysend, r2b, 20, across))
    product = lambda a, b, i: dot(pair_of(hidden, a, b), merge(w_down[:, :, column_chunk(i)]))
    sum_theirs(product, out_copies, psend2)
    sum_ours(product, pown2)
    sum_turn(mlp_copies, pown, r1)

    ag_drain(DOWN)

    @pl.loop(0, 4)
    def _(i):
        span_units = units // 4
        at = pl.ds(pl.multiple_of(i * span_units, span_units), span_units)
        value = dot(hidden[:, :, at].reshape(tokens, span_units), g_mlp[...].reshape(tokens, d), TN)
        w_down[pl.ds(i * part, part)] = value.reshape(part, w_down.shape[1], d).astype(BF)

    def early(k):
        @pl.when(z == 0)
        def _():
            @pl.loop(0, lines - 1)
            def _(j):
                for q in (side, 1 - side):
                    rs(k, 2 * (lines - 1 - j) + q, UP).start()

        @pl.when(z == lines - 1)
        def _():
            @pl.loop(0, lines - 1)
            def _(j):
                for q in (side, 1 - side):
                    rs(k, 2 * j + q, DN).start()

    early(DOWN)
    inner = (z > 0) & (z < lines - 1)

    def down_turn(j):
        @pl.when(inner)
        def _():
            rs_turn(DOWN, j)

    total = sum_end(mlp_copies, pown, r2)
    value = middle[...]
    scale = lax.rsqrt(mean_of(value * value) + 1e-06)
    normed = value * scale
    prod = total * normed
    g_second = row_sum(prod)
    mean = mean_of(prod * gain_second[...])
    value = g_ref[...].astype(F32) + scale * (total * gain_second[...] - normed * mean)
    g_middle[...] = value
    g_attn[me] = (valid_ref[...] * value).astype(BF)
    gather_start((g_attn,), 21)
    ag_drain(MLP)

    def farthest(i):
        return (1 - i % 2) * (3 - i // 2) + (i % 2) * (i // 2)

    def send_side(k, p):
        @pl.loop(0, part // 2)
        def _(j):
            zz = p * (part // 2) + j
            rs(k, 2 * zz + (1 - side), SIDE).start()

    @pl.loop(0, 4)
    def _(i):
        p = farthest(i)
        at = pl.ds(pl.multiple_of(p * quarter, quarter), quarter)
        value = dot(mlp_in[:, :, at].reshape(tokens, quarter), g_gu[...].reshape(tokens, 2 * units), TN)
        w_mlp[pl.ds(p * part, part)] = value.reshape(part, w_mlp.shape[1], 2 * units).astype(BF)
        send_side(MLP, p)

    gather_pass((g_attn,), 21)
    gather_end((g_attn,), 21)

    value = dot(g_attn[...].reshape(tokens, d), merge(w_out[...]), NT)
    g_hin[...] = value.reshape(4, t, width)
    value = dot(head_in[...].reshape(tokens, width), g_attn[...].reshape(tokens, d), TN)
    d_out[...] = value.reshape(part, w_first.shape[1], d).astype(BF)

    def d_out_copy(peer, slot):
        return rep_copy(
            d_out.at[:, :, pl.ds(pl.multiple_of(peer * quarter, quarter), quarter)],
            d_out_in.at[pl.ds(me * part, part)],
            slot, peer,
        )

    for i, peer in enumerate((sibling, across, diagonal)):
        d_out_copy(peer, 24 + i).start()
    own_d_out = pltpu.make_async_copy(
        d_out.at[:, :, pl.ds(pl.multiple_of(me * quarter, quarter), quarter)],
        d_out_in.at[pl.ds(me * part, part)], local.at[7],
    )
    own_d_out.start()
    down_turn(0)

    corr[...] = jnp.zeros_like(corr)
    g_mix[...] = jnp.zeros_like(g_mix)
    lanes[...] = jnp.zeros_like(lanes)

    @pl.loop(0, 4)
    def _(row):
        allowed = allowed_of(seg_all[row][0:1, :], rows, cols)
        g_wide[...] = g_hin[row] * gain_head[...]
        for pair in range(heads // 2):
            g_heads, g_mixed = [], []
            both = [probs[row, 2 * pair + c] for c in range(2)]
            for e in range(2):
                h = 2 * pair + e
                scaled = g_wide[:, h * hd : (h + 1) * hd]
                own_hat = hat[row, :, h * hd : (h + 1) * hd]
                g = inv[row, :, h * hd : (h + 1) * hd] * (scaled - mean_of(scaled) - own_hat * mean_of(scaled * own_hat))
                g = g.astype(BF)
                g_heads.append(g)
                g_mixed.append(dot(g, split(qkv, row, 2, h), NT))
            for e in range(2):
                h = 2 * pair + e
                mixed = (mix_ref[h, 0] * both[0] + mix_ref[h, 1] * both[1]).astype(BF)
                g_v = dot(mixed, g_heads[e], TN)
                g_qkv[row, :, 2 * width + h * hd : 2 * width + (h + 1) * hd] = g_v.astype(BF)
                for c in range(2):
                    place = (2 * pair + e) * 2 + c
                    g_mix[place : place + 1, :] += row_sum(g_mixed[e] * both[c])
            for c in range(2):
                h = 2 * pair + c
                g_probs = mix_ref[2 * pair, c] * g_mixed[0] + mix_ref[2 * pair + 1, c] * g_mixed[1]
                weighted = both[c] * g_probs
                g_conv = weighted - both[c] * jnp.sum(weighted, axis=1, keepdims=True)
                corr[h] += dot(lagged(masked[row, h].astype(F32), taps, rows), g_conv.astype(BF), TN)
                g_kept = dot(g_conv.astype(BF), bands[h, 0:t, :], NT)
                for a in range(1, taps):
                    lead = jnp.where(rows < t - a, pltpu.roll(g_conv, t - a, 0), 0.0).astype(BF)
                    g_kept += dot(lead, bands[h, a * t : (a + 1) * t, :], NT)
                g_raw = jnp.where(allowed, g_kept, 0.0).astype(BF)
                g_q = dot(g_raw, split(qkv, row, 1, h)) * hd**-0.5
                g_k = dot(g_raw, split(qkv, row, 0, h), TN) * hd**-0.5
                g_qkv[row, :, h * hd : (h + 1) * hd] = g_q.astype(BF)
                g_qkv[row, :, width + h * hd : width + (h + 1) * hd] = g_k.astype(BF)

    down_turn(1)
    in_copies = sum_copies(27, psend, r1, r2)
    product = lambda a, b, i: dot(pair_of(g_qkv, a, b), merge(w_first[pl.ds(i * part, part), :, 0 : 3 * quarter]), NT)
    sum_theirs(product, in_copies, psend)
    sum_ours(product, pown)
    sum_turn(in_copies, pown, r1)

    ag_drain(FIRST)
    for i, peer in enumerate((sibling, across, diagonal)):
        w_out_copy(peer, 9 + i).wait_send()
        d_out_copy(peer, 24 + i).wait_recv()
    own_d_out.wait()

    @pl.loop(0, 4)
    def _(i):
        p = farthest(i)
        at = pl.ds(pl.multiple_of(p * quarter, quarter), quarter)
        value = dot(attn_in[:, :, at].reshape(tokens, quarter), g_qkv[...].reshape(tokens, 3 * quarter), TN)
        w_first[pl.ds(p * part, part), :, 0 : 3 * quarter] = value.reshape(part, w_first.shape[1], 3 * quarter).astype(BF)
        w_first[pl.ds(p * part, part), :, 3 * quarter :] = d_out_in[pl.ds(p * part, part)]
        send_side(FIRST, p)

    total = sum_end(in_copies, pown, r2)
    value = x_ref[...].astype(F32)
    scale = lax.rsqrt(mean_of(value * value) + 1e-06)
    normed = value * scale
    prod = total * normed
    g_first = row_sum(prod)
    mean = mean_of(prod * gain_first[...])
    grad_in_ref[...] = (g_middle[...] + scale * (total * gain_first[...] - normed * mean)).astype(BF)

    sum_turn(out_copies, pown2, r1b)
    pl.loop(2, lines - 1)(lambda j: down_turn(j))
    total = sum_end(out_copies, pown2, r2b)
    mlp_part = valid_ref[...] * total
    value = middle[...] + mlp_part
    out_ref[...] = value.astype(BF)
    stat_out = jnp.sum(row_sum(valid_ref[...] * value * value), axis=1, keepdims=True)
    stat_mlp = jnp.sum(row_sum(mlp_part * mlp_part), axis=1, keepdims=True)

    strips = d // 128
    small_ref[...] = jnp.zeros_like(small_ref)
    for i in range(strips):
        at = slice(128 * i, 128 * (i + 1))
        small_ref[i : i + 1, :] = g_first[:, at]
        small_ref[strips + i : strips + i + 1, :] = g_second[:, at]
    own_gain = row_sum((g_hin[...] * hat[...]).reshape(tokens, width))
    for i in range(width // 128):
        small_ref[pl.ds(2 * strips + me * (width // 128) + i, 1), :] = own_gain[:, 128 * i : 128 * (i + 1)]
    base = 3 * strips
    for h in range(heads):
        for a in range(taps):
            tile = corr[h, a * t : (a + 1) * t, :]
            for b in range(span):
                lanes[a * span + b : a * span + b + 1, :] = row_sum(jnp.where(diff == b, tile, 0.0))
        small_ref[pl.ds(base + me * heads + h, 1), :] = row_sum(jnp.transpose(lanes[...]))
    base += 4 * heads
    lanes[0 : 2 * heads, :] = g_mix[...]
    lanes[2 * heads :, :] = jnp.zeros((t - 2 * heads, t), F32)
    small_ref[pl.ds(base + me, 1), :] = row_sum(jnp.transpose(lanes[...]))
    base += 4
    lane = lax.broadcasted_iota(jnp.int32, (1, 128), 1)
    count = jnp.sum(row_sum(jnp.broadcast_to(valid_ref[...], (t, 128))), axis=1, keepdims=True) * (1.0 / 128.0)
    stats = jnp.zeros((1, 128), F32)
    for i, stat in enumerate((stat_out, stat_attn, stat_mlp, count)):
        stats = jnp.where(lane == i, stat, stats)
    small_ref[base : base + 1, :] = stats

    peers = [(sibling, f), (across, f)] + [(me, flip(bit)) for bit in bits]

    def small_copy(i):
        return pltpu.make_async_remote_copy(
            src_ref=small_send.at[i], dst_ref=small_recv.at[i],
            send_sem=rep_send.at[40 + i], recv_sem=rep_recv.at[40 + i],
            device_id=peers[i], device_id_type=MESH,
        )

    def small_step(i):
        small_send[i] = small_ref[...]
        small_copy(i).start()

    def small_take(i):
        small_copy(i).wait_recv()
        small_ref[...] = small_ref[...] + small_recv[i]

    small_step(0)
    rs_close(DOWN)
    final_start(DOWN, 30)
    small_take(0)
    small_step(1)
    rs_turn(MLP, 0)
    small_take(1)
    small_step(2)
    final_pass(DOWN, 30)
    pl.loop(1, lines - 1)(lambda j: rs_turn(MLP, j))
    for i in range(2, len(peers)):
        small_take(i)
        if i + 1 < len(peers):
            small_step(i + 1)
    rs_close(MLP)
    final_start(MLP, 33)
    rs_turn(FIRST, 0)
    final_pass(MLP, 33)
    pl.loop(1, lines - 1)(lambda j: rs_turn(FIRST, j))
    rs_close(FIRST)
    final_start(FIRST, 36)
    final_pass(FIRST, 36)
    for k in range(3):
        final_end(k, (36, 33, 30)[k])
    for k in range(3):
        rs_drain(k)
    for i in range(len(peers)):
        small_copy(i).wait_send()
    for i, peer in enumerate((sibling, across, diagonal)):
        d_out_copy(peer, 24 + i).wait_send()


def run_layer(cfg, x, g, seg, valid, gains, score, mix, shards_in):
    heads, hd, taps, span, docs, shards, units = cfg
    t, d = x.shape
    width = heads * hd
    first, mlp, down = shards_in
    bits = shards.bit_length() - 1
    tall = max(s.shape[0] for s in shards_in)
    broad = max(s.shape[1] for s in shards_in)

    def shape(dtype, *dims):
        return jax.ShapeDtypeStruct(dims, dtype)

    v = pltpu.VMEM
    dma = pltpu.SemaphoreType.DMA
    out_shape = (
        shape(BF, t, d), shape(BF, t, d), shape(F32, 64, 128),
        *(shape(BF, 4, *s.shape) for s in shards_in),
        *(shape(BF, 3, shards, *s.shape) for s in shards_in),
    )
    scratch = [
        *(v((shards, *s.shape), BF) for s in shards_in),
        v((4, t, d), BF), v((4, t, d), BF), v((4, 8, t), F32), v((4, t, d), BF), v((4, t, 3 * width), BF),
        v((4, t, width), F32), v((4, t, width), F32), v((4, heads, t, t), F32), v((4, heads, t, t), BF),
        v((4, t, width), BF), v((shards // 4, first.shape[0], d), BF),
        v((t, d), F32), v((4 * t, units), F32), v((4 * t, units), F32), v((4, t, units), BF), v((4, t, 2 * units), BF),
        v((4, t, d), BF), v((t, d), F32), v((4, t, 3 * width), BF), v((4, t, width), F32),
        v((shards // 4, first.shape[0], d), BF), v((shards, first.shape[0], width), BF),
        v((2, t, d), BF), v((2, t, d), F32), v((2, t, d), BF), v((t, d), BF), v((t, d), BF),
        v((2, t, d), BF), v((2, t, d), F32), v((2, t, d), BF), v((t, d), BF),
        v((heads, taps * t, t), BF), v((heads, taps * t, t), F32), v((t, width), F32), v((t, t), F32), v((2 * heads, t), F32),
        v((tall, broad), BF), v((2 + bits, 64, 128), F32), v((2 + bits, 64, 128), F32),
        dma((3, 3, shards)), dma((3, shards)), dma((3, 3, shards)), dma((3, 3, shards)), dma((48,)), dma((48,)), dma((8,)),
    ]
    return pl.pallas_call(
        functools.partial(layer_kernel, cfg),
        out_shape=out_shape,
        in_specs=[vmem_spec()] * 7 + [smem_spec()] * 2 + [hbm_spec()] * 3,
        out_specs=(vmem_spec(),) * 3 + (hbm_spec(),) * 6,
        scratch_shapes=scratch,
        compiler_params=pltpu.CompilerParams(
            collective_id=0, has_side_effects=True, vmem_limit_bytes=VMEM_LIMIT
        ),
    )(x, g, seg, valid, *gains, score, mix, *shards_in)


def widen_kernel(strip, count, first_ref, mlp_ref, down_ref, *outs):
    quarter = first_ref.shape[2] // 4
    for r in range(4):
        for k in range(4):
            outs[k][:, r * quarter : (r + 1) * quarter] = first_ref[r, :, k * quarter : (k + 1) * quarter].astype(F32)
        outs[6][r] = down_ref[r].astype(F32)
        for k in range(2):
            for i in range(count):
                at = (4 * i + r) * strip
                outs[4 + k][:, at : at + strip] = mlp_ref[r, :, (k * count + i) * strip : (k * count + i + 1) * strip].astype(F32)


def widen(first, mlp, down, strip, count):
    _, rows, d = first.shape
    steps = 4 if rows % 64 == 0 and down.shape[1] % 64 == 0 else 1
    hidden = 4 * strip * count
    rows_step, down_step = rows // steps, down.shape[1] // steps

    def taken(array, size):
        return pl.BlockSpec((4, size, array.shape[2]), lambda i: (0, i, 0))

    def given(size, width):
        return pl.BlockSpec((size, width), lambda i: (i, 0))

    return pl.pallas_call(
        functools.partial(widen_kernel, strip, count),
        grid=(steps,),
        out_shape=tuple(jax.ShapeDtypeStruct((rows, d), F32) for _ in range(4))
        + tuple(jax.ShapeDtypeStruct((rows, hidden), F32) for _ in range(2))
        + (jax.ShapeDtypeStruct(down.shape, F32),),
        in_specs=[taken(first, rows_step), taken(mlp, rows_step), taken(down, down_step)],
        out_specs=tuple(given(rows_step, d) for _ in range(4))
        + tuple(given(rows_step, hidden) for _ in range(2))
        + (taken(down, down_step),),
        compiler_params=pltpu.CompilerParams(vmem_limit_bytes=VMEM_LIMIT),
    )(first, mlp, down)


def per_device(
    hidden_in,
    doc_lengths,
    w_query,
    w_key,
    w_value,
    w_output,
    w_gate,
    w_up,
    w_down,
    attn_norm,
    mlp_norm,
    head_norm,
    score_kernel,
    head_mixing,
    grad_out,
):
    _, t, d = hidden_in.shape
    reps = lax.axis_size("rep")
    shards = lax.axis_size("fsdp")
    me = lax.axis_index("rep")
    hidden = w_gate.shape[1]
    heads = H // reps
    hd = d // H
    quarter = d // reps
    units = hidden // reps
    strip = units // shards
    taps, span = score_kernel.shape[1:]
    docs = doc_lengths.shape[1] - 1
    rows_here = w_gate.shape[0]

    def mine(array, size, axis):
        return lax.dynamic_slice_in_dim(array, me * size, size, axis)

    def strips(w):
        return mine(w.reshape(rows_here, shards, reps, strip), 1, 2).reshape(rows_here, units)

    first_shard = jnp.concatenate([mine(w, quarter, 1) for w in (w_query, w_key, w_value, w_output)], axis=1)
    mlp_shard = jnp.concatenate([strips(w_gate), strips(w_up)], axis=1)
    down_shard = mine(w_down, strip, 0)

    boundary = jnp.cumsum(doc_lengths[:, :-1], axis=1)
    places = jnp.arange(t, dtype=jnp.int32)
    seg_ids = jnp.sum((places[None, :, None] >= boundary[:, None, :]).astype(jnp.int32), axis=2)
    seg_own = jnp.broadcast_to(seg_ids.astype(F32), (8, t))
    valid = (seg_ids < docs).astype(F32).reshape(t, 1)
    gains = (attn_norm.reshape(1, d), mlp_norm.reshape(1, d), mine(head_norm, quarter, 0).reshape(1, quarter))
    score = mine(score_kernel.reshape(H, taps * span), heads, 0)
    mix = mine(head_mixing, heads, 0)
    cfg = (heads, hd, taps, span, docs, shards, units)
    block_out, grad_in, small, a_first, a_mlp, a_down = run_layer(
        cfg, hidden_in.reshape(t, d), grad_out.reshape(t, d), seg_own, valid, gains, score, mix,
        (first_shard, mlp_shard, down_shard),
    )[:6]

    lines = d // 128
    base = 3 * lines
    small_score = small[base : base + H, : taps * span]
    base += H
    small_mix = small[base : base + reps, : 2 * heads]
    stats = small[base + reps, :STATS]
    root_means = jnp.sqrt(stats[:3] / (stats[3] * d))

    if strip % 128 == 0:
        g_q, g_k, g_v, g_o, g_gate, g_up, g_down = widen(a_first, a_mlp, a_down, strip, shards)
    else:
        first = a_first.astype(F32).reshape(reps, rows_here, 4, quarter)
        first = jnp.moveaxis(first, 0, 2).reshape(rows_here, 4, d)
        g_q, g_k, g_v, g_o = (first[:, k] for k in range(4))
        mlp = a_mlp.astype(F32).reshape(reps, rows_here, 2, shards, strip)
        mlp = jnp.moveaxis(mlp, 0, 3).reshape(rows_here, 2, hidden)
        g_gate, g_up = mlp[:, 0], mlp[:, 1]
        g_down = a_down.astype(F32)
    return (
        block_out.reshape(hidden_in.shape),
        grad_in.reshape(hidden_in.shape),
        g_q,
        g_k,
        g_v,
        g_o,
        g_gate,
        g_up,
        g_down.reshape(w_down.shape),
        small[:lines].reshape(d),
        small[lines : 2 * lines].reshape(d),
        small[2 * lines : 3 * lines].reshape(d),
        small_score.reshape(score_kernel.shape),
        small_mix.reshape(head_mixing.shape),
        root_means,
    )


def solution(mesh):
    rows = P(("rep", "fsdp"), None, None)
    split = P("fsdp", None)
    placed = (rows, P(("rep", "fsdp"), None)) + (split,) * 7 + (P(),) * 5 + (rows,)
    return jax.shard_map(
        per_device,
        mesh=mesh,
        in_specs=placed,
        out_specs=(rows, rows) + (split,) * 7 + (P(),) * 6,
        check_vma=False,
    )
```

time: 3260 us -> 515 us (0.16)
  waiting for transfers between devices: 1440 us -> 0 us
  other arithmetic: 801 us -> 4.06 us
  local copies, waits for them, and re-layouts: 754 us -> 27.1 us
  Pallas kernels: 0 us -> 473 us
  matrix products: 174 us -> 0 us
  blocking collectives: 43.7 us -> 0 us
    all_gather x4 -> x0, waiting for transfers between devices: 868 us -> none  [the longest x1 479 us: per_device(): lax.all_gather(mlp_shard, 'fsdp', axis=0, tiled=True)]
    pallas_call x0 -> x2, Pallas kernels: none -> 473 us  [the longest x1 465 us: run_layer(): pl.pallas_call(functools.partial(layer_kernel, cfg), out_shape=out_shape,...]
    all_to_all x4 -> x0, waiting for transfers between devices: 383 us -> none  [owner_total(): lax.all_to_all(term.astype(jnp.bfloat16), 'fsdp', split_axis=0, concat_ax...]
    convert_element_type x14 -> x2, other arithmetic: 378 us -> 0.01 us  [the longest x1 0.01 us: per_device(): valid = (seg_ids < docs).astype(F32).reshape(t, 1)]
    unnamed x108 -> x18, local copies, waits for them, and re-layouts: 356 us -> 4.62 us
    reduce_sum x59 -> x1, other arithmetic: 205 us -> 0.09 us  [per_device(): jnp.sum((places[None, :, None] >= boundary[:, None, :]).astype(jnp.int32)...]
    concatenate x3 -> x2, other arithmetic: 188 us -> 1.81 us  [the longest x1 0.94 us: per_device(): mlp_shard = jnp.concatenate([strips(w_gate), strips(w_up)], axis=1)]
    psum x1 -> x0, waiting for transfers between devices: 186 us -> none  [per_device(): lax.psum(group_row.astype(jnp.bfloat16), 'rep').astype(jnp.float32)[0]]
  transfers between devices with their start and end apart: 9 -> 0, of which waited for: 6 -> 0; matrix products, arithmetic and copies ran while one was open for 35% -> 0% of each run, Pallas kernels for 0% -> 0%
where the time goes in v2:
time: 515 us; the launch traced here: 506 us
  Pallas kernels  473 us (92%)
  local copies, waits for them, and re-layouts  27.1 us (5%)
    pallas_call x1, Pallas kernels, run_layer(): pl.pallas_call(functools.partial(layer_kernel, cfg), out_shape=out_shape,...  465 us

profile of v2, /device:TPU:9, one launch (start us, length us, event | category | flops | bytes accessed | tf_op | source)
XLA Modules:
  0.0 505.8 jit_solution(9842118015188652038)
XLA Ops:
  0.7 0.9 reduce_window_sum.11
  1.7 0.8 constant_dynamic-slice_fusion.5
  3.1 0.8 dynamic_slice.30
  5.1 1.3 reshape.164.refs_4_
  6.4 1.3 reshape.165.refs_5_
  7.7 0.7 copy.48.refs_3_
  8.4 0.9 copy.44
  10.0 1.1 constant_dynamic-slice_fusion.3
  11.1 1.0 constant_dynamic-slice_fusion.1
  12.1 0.9 pad_maximum_fusion.1.refs_9_
  13.0 0.8 constant_dynamic-slice_fusion.refs_11_
  13.8 1.1 reshape.168
  14.9 2.8 reshape.170
  17.7 4.7 dynamic-slice_reduce_fusion
  22.6 0.9 pad_maximum_fusion.refs_10_
  23.5 464.7 %shard_map.262 = (bf16[128,1536]{1,0:T(8,128)(2,1)}, bf16[128,1536]{1,0:T(8,128)(2,1)}, f32[64,128]{1,0:T(8,128)}, bf16[4,192,1536]{2,1,0:T(8,128)(2,1)}, bf16[4...) custom-call(bf16[128,1536]{1,0:T(8,128)(2,1)} %bitcast.32, ...), custom_call_target="tpu_custom_call" | custom-call | tf_op jit(solution)/shard_map/pallas_call | solution.py:839
  488.3 1.3 slice.36
  490.2 1.2 sqrt_bitcast_fusion
  492.8 0.7 slice.33
  493.5 1.4 slice_bitcast_fusion
  495.0 0.8 copy.49
  495.8 8.5 %shard_map.263 = (f32[192,1536]{1,0:T(8,128)}, f32[192,1536]{1,0:T(8,128)}, f32[192,1536]{1,0:T(8,128)}, f32[192,1536]{1,0:T(8,128)}, f32[192,4096]{1,0:T(8,128)...) custom-call(bf16[4,192,1536]{2,1,0:T(8,128)(2,1)} %get-tuple-element.30.first_ref, ...), custom_call_target="tpu_custom_call" | custom-call | tf_op jit(solution)/shard_map/pallas_call | solution.py:875
  504.3 0.7 copy.62
  505.0 0.7 copy.63
  (24 shorter events, 4.2 us)
Async XLA Ops:
  0.6 12.4 %copy-start = (bf16[512,1536]{1,0:T(8,128)(2,1)S(1)}, bf16[512,1536]{1,0:T(8,128)(2,1)}, u32[]{:S(2)}) copy-start(bf16[512,1536]{1,0:T(8,128)(2,1)} %param.23) | copy-start | bytes 4718596
  10.0 3.8 copy-start.2
  495.7 8.5 %copy-start.4 = (bf16[128,1536]{1,0:T(8,128)(2,1)S(1)}, bf16[128,1536]{1,0:T(8,128)(2,1)}, u32[]{:S(2)}) copy-start(bf16[128,1536]{1,0:T(8,128)(2,1)} %get-tuple-element.28) | copy-start | bytes 1179652
  495.7 9.3 %copy-start.3 = (bf16[128,1536]{1,0:T(8,128)(2,1)S(1)}, bf16[128,1536]{1,0:T(8,128)(2,1)}, u32[]{:S(2)}) copy-start(bf16[128,1536]{1,0:T(8,128)(2,1)} %get-tuple-element.29) | copy-start | bytes 1179652
  495.8 10.0 %copy-start.1 = (bf16[512,1536]{1,0:T(8,128)(2,1)S(1)}, bf16[512,1536]{1,0:T(8,128)(2,1)}, u32[]{:S(2)}) copy-start(bf16[512,1536]{1,0:T(8,128)(2,1)} %param.23) | copy-start | bytes 4718596

commit v3 on v2

--- a/solution.py
+++ b/solution.py
@@ -11,7 +11,7 @@
 BF = jnp.bfloat16
 F32 = jnp.float32
 MESH = pl.DeviceIdType.MESH
-VMEM_LIMIT = 61 * 1024 * 1024
+VMEM_LIMIT = 62 * 1024 * 1024
 NN = (((1,), (0,)), ((), ()))
 NT = (((1,), (1,)), ((), ()))
 TN = (((0,), (0,)), ((), ()))
@@ -76,12 +76,11 @@
         x_ref, g_ref, seg_ref, valid_ref, gain_first, gain_second, gain_head, score_ref, mix_ref,
         own_first, own_mlp, own_down,
         out_ref, grad_in_ref, small_ref, all_first, all_mlp, all_down,
-        land_first, land_mlp, land_down,
         w_first, w_mlp, w_down, wide, g_mlp, seg_all, attn_in, qkv, hat, inv, probs, masked, head_in, w_out,
-        middle, slope, silu, hidden, g_gu, g_attn, g_middle, g_qkv, g_hin, d_out, d_out_in,
+        middle, slope, silu, hidden, g_gu, g_attn, g_middle, g_qkv, g_hin, d_out_in,
         psend, pown, r1, ysend, r2, psend2, pown2, r1b, r2b, bands, corr, g_wide, lanes, g_mix,
-        stage, small_send, small_recv,
-        ag_send, ag_recv, rs_send, rs_recv, rep_send, rep_recv, local,
+        x_first, x_mlp, x_down, z_first, z_mlp, z_down, small_send, small_recv,
+        ag_send, ag_recv, rs_send, rs_recv, rep_send, rep_recv, local, credit,
     ) = refs
     t, d = x_ref.shape
     width = heads * hd
@@ -95,10 +94,11 @@
     z, side = f // 2, f % 2
     partner = 2 * z + (1 - side)
     weights = (w_first, w_mlp, w_down)
-    lands = (land_first, land_mlp, land_down)
+    x_lands, z_lands = (x_first, x_mlp, x_down), (z_first, z_mlp, z_down)
     peer_of = (f + 2, f - 2, partner)
     tokens = 4 * t
     part = shards // 4
+    strip = units // shards
     rows, cols = grids(t)
 
     def flip(bit):
@@ -117,19 +117,13 @@
 
     for r in (sibling, across, diagonal):
         greet(r, f)
-    for bit in bits:
-        greet(me, flip(bit))
-
-    @pl.when(z < lines - 1)
-    def _():
-        greet(me, f + 2)
-
-    @pl.when(z > 0)
-    def _():
-        greet(me, f - 2)
-
-    ends = (z > 0).astype(jnp.int32) + (z < lines - 1).astype(jnp.int32)
-    pl.semaphore_wait(barrier, 3 + len(bits) + ends)
+    greet(me, partner)
+
+    @pl.loop(1, lines)
+    def _(s):
+        greet(me, 2 * ((z + s) % lines) + side)
+
+    pl.semaphore_wait(barrier, 3 + lines)
 
     def rep_copy(src, dst, slot, peer):
         return pltpu.make_async_remote_copy(
@@ -260,115 +254,83 @@
         @pl.loop(0, 4)
         def _(i):
             value = product(across, me, i)
-            own_buf[0, :, column_chunk(i)] = value[:t]
-            own_buf[1, :, column_chunk(i)] = value[t:]
+            own_buf[0, :, column_chunk(i)] = value[:t].astype(own_buf.dtype)
+            own_buf[1, :, column_chunk(i)] = value[t:].astype(own_buf.dtype)
 
     def sum_turn(copies, own_buf, first_land):
         copies[0].wait_recv()
-        ysend[...] = (own_buf[0] + first_land[1 - plane].astype(F32)).astype(BF)
+        ysend[...] = (own_buf[0].astype(F32) + first_land[1 - plane].astype(F32)).astype(BF)
         copies[1].start()
-        own_buf[1] = own_buf[1] + first_land[plane].astype(F32)
+        own_buf[1] = (own_buf[1].astype(F32) + first_land[plane].astype(F32)).astype(own_buf.dtype)
 
     def sum_end(copies, own_buf, second_land):
         copies[1].wait_recv()
-        total = own_buf[1] + second_land[...].astype(F32)
+        total = own_buf[1].astype(F32) + second_land[...].astype(F32)
         copies[0].wait_send()
         copies[1].wait_send()
         return total
 
-    def rs(k, block, way):
+    def rs_side(k, zz):
+        source = weights[k].at[2 * zz + (1 - side)]
+        if k == DOWN:
+            source = x_mlp.at[zz, pl.ds(0, strip), pl.ds(0, d)]
         return pltpu.make_async_remote_copy(
-            src_ref=weights[k].at[block], dst_ref=lands[k].at[way, block],
-            send_sem=rs_send.at[k, way, block], recv_sem=rs_recv.at[k, way, block],
-            device_id=(me, peer_of[way]), device_id_type=MESH,
+            src_ref=source, dst_ref=x_lands[k].at[zz],
+            send_sem=rs_send.at[k, 0, zz], recv_sem=rs_recv.at[k, 0, zz],
+            device_id=(me, partner), device_id_type=MESH,
         )
 
-    def rs_add(k, block, way):
+    def rs_owner(k, zz):
+        return pltpu.make_async_remote_copy(
+            src_ref=weights[k].at[2 * zz + side], dst_ref=z_lands[k].at[z],
+            send_sem=rs_send.at[k, 1, zz], recv_sem=rs_recv.at[k, 1, z],
+            device_id=(me, 2 * zz + side), device_id_type=MESH,
+        )
+
+    def rs_from(k, zz):
+        return pltpu.make_async_remote_copy(
+            src_ref=weights[k].at[2 * zz + side], dst_ref=z_lands[k].at[zz],
+            send_sem=rs_send.at[k, 1, zz], recv_sem=rs_recv.at[k, 1, zz],
+            device_id=(me, 2 * zz + side), device_id_type=MESH,
+        )
+
+    def rs_add(k, block, landed):
         grad = weights[k]
-        high, wide_k = grad.shape[1:]
-        rs(k, block, way).wait_recv()
-        slot = stage.at[pl.ds(0, high), pl.ds(0, wide_k)]
-        copy = pltpu.make_async_copy(lands[k].at[way, block], slot, local.at[0])
-        copy.start()
-        copy.wait()
+        high = grad.shape[1]
         step = 16 if high % 16 == 0 else high
 
         @pl.loop(0, high // step)
         def _(i):
             at = pl.ds(pl.multiple_of(i * step, step), step)
-            total = grad[block, at, :].astype(F32) + stage[at, 0:wide_k].astype(F32)
+            total = grad[block, at, :].astype(F32)
+            for land, slot in landed:
+                total = total + land[slot, at, :].astype(F32)
             grad[block, at, :] = total.astype(BF)
 
-    def rs_turn(k, j):
-        sides = (side, 1 - side) if k == DOWN else (side,)
-        high_target, low_target = lines - 1 - j, j
-
-        @pl.when(high_target > z)
-        def _():
-            for q in sides:
-                block = 2 * high_target + q
-                if k != DOWN:
-                    rs_add(k, block, SIDE)
-
-                @pl.when(z > 0)
-                def _():
-                    rs_add(k, block, UP)
-
-                rs(k, block, UP).start()
-
-        @pl.when(low_target < z)
-        def _():
-            for q in sides:
-                block = 2 * low_target + q
-                if k != DOWN:
-                    rs_add(k, block, SIDE)
-
-                @pl.when(z < lines - 1)
-                def _():
-                    rs_add(k, block, DN)
-
-                rs(k, block, DN).start()
+    def after(s):
+        return (z + s) % lines
+
+    def rs_turn(k, s):
+        zz = after(s)
+        rs_side(k, zz).wait_recv()
+        rs_add(k, 2 * zz + side, [(x_lands[k], zz)])
+        rs_owner(k, zz).start()
 
     def rs_close(k):
-        sides = (1 - side, side) if k == DOWN else (side,)
-        for q in sides:
-            block = 2 * z + q
-            if k != DOWN:
-                rs_add(k, block, SIDE)
-
-            @pl.when(z > 0)
-            def _():
-                rs_add(k, block, UP)
-
-            @pl.when(z < lines - 1)
-            def _():
-                rs_add(k, block, DN)
-
-            if k == DOWN and q is not side:
-                rs(k, block, SIDE).start()
-        if k == DOWN:
-            rs_add(k, f, SIDE)
+        rs_side(k, z).wait_recv()
+        landed = [(x_lands[k], z)]
+        for s in range(1, lines):
+            rs_from(k, after(s)).wait_recv()
+            landed.append((z_lands[k], after(s)))
+        rs_add(k, f, landed)
 
     def rs_drain(k):
-        sides = (side, 1 - side) if k == DOWN else (side,)
-
-        @pl.loop(0, lines)
-        def _(zz):
-            @pl.when(zz > z)
-            def _():
-                for q in sides:
-                    rs(k, 2 * zz + q, UP).wait_send()
-
-            @pl.when(zz < z)
-            def _():
-                for q in sides:
-                    rs(k, 2 * zz + q, DN).wait_send()
-
-            if k != DOWN:
-                rs(k, 2 * zz + (1 - side), SIDE).wait_send()
-
-        if k == DOWN:
-            rs(k, partner, SIDE).wait_send()
+        if k != DOWN:
+            pl.loop(0, lines)(lambda s: rs_side(k, after(s)).wait_send())
+
+        @pl.loop(1, lines)
+        def _(s):
+            rs_owner(k, after(s)).wait_send()
 
     outs = (all_first, all_mlp, all_down)
 
@@ -426,6 +388,8 @@
 
     gather_pass(entering, 0)
     ag_steps(FIRST, 1, 2)
+    loads[DOWN].wait()
+    ag(DOWN, f, SIDE).start()
     gather_end(entering, 0)
 
     @pl.loop(0, 4)
@@ -438,9 +402,9 @@
 
     ag_steps(FIRST, 2, 3)
     loads[MLP].wait()
-    loads[DOWN].wait()
     ag_steps(MLP, 0, 1)
     ag_steps(FIRST, 3, lines)
+    ag_steps(MLP, 1, 2)
     ag_done(FIRST)
 
     def w_out_copy(peer, slot):
@@ -462,7 +426,8 @@
     for i in range(3):
         value = dot(attn_in[...].reshape(tokens, d), merge(w_first[:, :, i * quarter : (i + 1) * quarter]))
         qkv[:, :, i * quarter : (i + 1) * quarter] = value.astype(BF).reshape(4, t, quarter)
-    ag_steps(MLP, 1, 2)
+    ag_steps(MLP, 2, 3)
+    ag_steps(DOWN, 0, 1)
 
     def split(ref, row, kind, h):
         return ref[row, :, kind * width + h * hd : kind * width + (h + 1) * hd]
@@ -489,7 +454,7 @@
                 centred = out - mean_of(out)
                 scale = lax.rsqrt(mean_of(centred * centred) + 1e-05)
                 hat[row, :, h * hd : (h + 1) * hd] = centred * scale
-                inv[row, :, h * hd : (h + 1) * hd] = jnp.broadcast_to(scale, (t, hd))
+                inv[row, :, h : h + 1] = scale
         head_in[row] = (hat[row] * gain_head[...]).astype(BF)
 
     for i, peer in enumerate((sibling, across, diagonal)):
@@ -500,9 +465,8 @@
     product = lambda a, b, i: dot(pair_of(head_in, a, b), merge(w_out[:, :, column_chunk(i)]))
     sum_theirs(product, copies, psend)
     sum_ours(product, pown)
-    ag_steps(MLP, 2, 3)
+    ag_steps(MLP, 3, lines)
     sum_turn(copies, pown, r1)
-    ag(DOWN, f, SIDE).start()
     total = sum_end(copies, pown, r2)
     attn_part = valid_ref[...] * total
     value = x_ref[...].astype(F32) + attn_part
@@ -511,12 +475,11 @@
     scale = lax.rsqrt(mean_of(value * value) + 1e-06)
     wide[me] = (value * scale * gain_second[...]).astype(BF)
     gather_start((wide,), 14)
-    ag_steps(MLP, 3, lines)
+    ag_steps(DOWN, 1, 2)
     gather_pass((wide,), 14)
-    ag_steps(DOWN, 0, 1)
     gather_end((wide,), 14)
     mlp_in = wide
-    ag_steps(DOWN, 1, 2)
+    ag_steps(DOWN, 2, 3)
     ag_done(MLP)
 
     chunk = 256
@@ -531,10 +494,23 @@
         sig = 1.0 / (1.0 + jnp.exp(-gate))
         act = gate * sig
         hidden[:, :, at] = (act * upper).astype(BF).reshape(4, t, chunk)
-        silu[:, at] = act
-        slope[:, at] = upper * sig * (1.0 + gate * (1.0 - sig))
-
-    ag_steps(DOWN, 2, 3)
+        silu[:, at] = act.astype(BF)
+        slope[:, at] = (upper * sig * (1.0 + gate * (1.0 - sig))).astype(BF)
+
+    @pl.loop(0, 4)
+    def _(i):
+        span_units = units // 4
+        at = pl.ds(pl.multiple_of(i * span_units, span_units), span_units)
+        value = dot(hidden[:, :, at].reshape(tokens, span_units), g_mlp[...].reshape(tokens, d), TN)
+        value = value.reshape(part, strip, d)
+        for j in range(part // 2):
+            half = jnp.where(side == 0, value[2 * j + 1], value[2 * j])
+            x_mlp[i * (part // 2) + j, 0:strip, 0:d] = half.astype(BF)
+
+    @pl.loop(1, lines + 1)
+    def _(s):
+        rs_side(DOWN, after(s)).start()
+
     ag_steps(DOWN, 3, lines)
 
     @pl.loop(0, 4)
@@ -543,8 +519,8 @@
         at = pl.ds(pl.multiple_of(i * span_units, span_units), span_units)
         after = pl.ds(pl.multiple_of(units + i * span_units, span_units), span_units)
         g_hidden = dot(g_mlp[...].reshape(tokens, d), merge(w_down[pl.ds(i * part, part)]), NT)
-        g_gu[:, :, at] = (g_hidden * slope[:, at]).astype(BF).reshape(4, t, span_units)
-        g_gu[:, :, after] = (g_hidden * silu[:, at]).astype(BF).reshape(4, t, span_units)
+        g_gu[:, :, at] = (g_hidden * slope[:, at].astype(F32)).astype(BF).reshape(4, t, span_units)
+        g_gu[:, :, after] = (g_hidden * silu[:, at].astype(F32)).astype(BF).reshape(4, t, span_units)
 
     mlp_copies = sum_copies(17, psend, r1, r2)
     product = lambda a, b, i: dot(pair_of(g_gu, a, b), merge(w_mlp[pl.ds(i * part, part)]), NT)
@@ -565,29 +541,6 @@
         at = pl.ds(pl.multiple_of(i * span_units, span_units), span_units)
         value = dot(hidden[:, :, at].reshape(tokens, span_units), g_mlp[...].reshape(tokens, d), TN)
         w_down[pl.ds(i * part, part)] = value.reshape(part, w_down.shape[1], d).astype(BF)
-
-    def early(k):
-        @pl.when(z == 0)
-        def _():
-            @pl.loop(0, lines - 1)
-            def _(j):
-                for q in (side, 1 - side):
-                    rs(k, 2 * (lines - 1 - j) + q, UP).start()
-
-        @pl.when(z == lines - 1)
-        def _():
-            @pl.loop(0, lines - 1)
-            def _(j):
-                for q in (side, 1 - side):
-                    rs(k, 2 * j + q, DN).start()
-
-    early(DOWN)
-    inner = (z > 0) & (z < lines - 1)
-
-    def down_turn(j):
-        @pl.when(inner)
-        def _():
-            rs_turn(DOWN, j)
 
     total = sum_end(mlp_copies, pown, r2)
     value = middle[...]
@@ -601,22 +554,35 @@
     g_attn[me] = (valid_ref[...] * value).astype(BF)
     gather_start((g_attn,), 21)
     ag_drain(MLP)
-
-    def farthest(i):
-        return (1 - i % 2) * (3 - i // 2) + (i % 2) * (i // 2)
+    pl.loop(0, lines)(lambda s: rs_side(DOWN, after(s)).wait_send())
+    pl.semaphore_signal(credit, inc=1, device_id=(me, partner), device_id_type=MESH)
+
+    def in_turn(i):
+        return (z // (part // 2) + 1 + i) % 4
 
     def send_side(k, p):
         @pl.loop(0, part // 2)
         def _(j):
             zz = p * (part // 2) + j
-            rs(k, 2 * zz + (1 - side), SIDE).start()
+            rs_side(k, zz).start()
 
     @pl.loop(0, 4)
     def _(i):
-        p = farthest(i)
+        p = in_turn(i)
         at = pl.ds(pl.multiple_of(p * quarter, quarter), quarter)
-        value = dot(mlp_in[:, :, at].reshape(tokens, quarter), g_gu[...].reshape(tokens, 2 * units), TN)
-        w_mlp[pl.ds(p * part, part)] = value.reshape(part, w_mlp.shape[1], 2 * units).astype(BF)
+        size = units // 2
+
+        @pl.loop(0, 4)
+        def _(j):
+            to = pl.ds(pl.multiple_of(j * size, size), size)
+            value = dot(mlp_in[:, :, at].reshape(tokens, quarter), g_gu[:, :, to].reshape(tokens, size), TN)
+            w_mlp[pl.ds(p * part, part), :, to] = value.reshape(part, w_mlp.shape[1], size).astype(BF)
+
+
+        @pl.when(i == 0)
+        def _():
+            pl.semaphore_wait(credit, 1)
+
         send_side(MLP, p)
 
     gather_pass((g_attn,), 21)
@@ -624,8 +590,13 @@
 
     value = dot(g_attn[...].reshape(tokens, d), merge(w_out[...]), NT)
     g_hin[...] = value.reshape(4, t, width)
-    value = dot(head_in[...].reshape(tokens, width), g_attn[...].reshape(tokens, d), TN)
-    d_out[...] = value.reshape(part, w_first.shape[1], d).astype(BF)
+    d_out = w_out
+
+    @pl.loop(0, 4)
+    def _(i):
+        value = dot(head_in[...].reshape(tokens, width), g_attn[:, :, column_chunk(i)].reshape(tokens, quarter), TN)
+        d_out[:, :, column_chunk(i)] = value.reshape(part, w_first.shape[1], quarter).astype(BF)
+
 
     def d_out_copy(peer, slot):
         return rep_copy(
@@ -641,7 +612,7 @@
         d_out_in.at[pl.ds(me * part, part)], local.at[7],
     )
     own_d_out.start()
-    down_turn(0)
+    pl.loop(1, lines)(lambda s: rs_turn(DOWN, s))
 
     corr[...] = jnp.zeros_like(corr)
     g_mix[...] = jnp.zeros_like(g_mix)
@@ -658,7 +629,7 @@
                 h = 2 * pair + e
                 scaled = g_wide[:, h * hd : (h + 1) * hd]
                 own_hat = hat[row, :, h * hd : (h + 1) * hd]
-                g = inv[row, :, h * hd : (h + 1) * hd] * (scaled - mean_of(scaled) - own_hat * mean_of(scaled * own_hat))
+                g = inv[row, :, h : h + 1] * (scaled - mean_of(scaled) - own_hat * mean_of(scaled * own_hat))
                 g = g.astype(BF)
                 g_heads.append(g)
                 g_mixed.append(dot(g, split(qkv, row, 2, h), NT))
@@ -686,7 +657,6 @@
                 g_qkv[row, :, h * hd : (h + 1) * hd] = g_q.astype(BF)
                 g_qkv[row, :, width + h * hd : width + (h + 1) * hd] = g_k.astype(BF)
 
-    down_turn(1)
     in_copies = sum_copies(27, psend, r1, r2)
     product = lambda a, b, i: dot(pair_of(g_qkv, a, b), merge(w_first[pl.ds(i * part, part), :, 0 : 3 * quarter]), NT)
     sum_theirs(product, in_copies, psend)
@@ -701,7 +671,7 @@
 
     @pl.loop(0, 4)
     def _(i):
-        p = farthest(i)
+        p = in_turn(i)
         at = pl.ds(pl.multiple_of(p * quarter, quarter), quarter)
         value = dot(attn_in[:, :, at].reshape(tokens, quarter), g_qkv[...].reshape(tokens, 3 * quarter), TN)
         w_first[pl.ds(p * part, part), :, 0 : 3 * quarter] = value.reshape(part, w_first.shape[1], 3 * quarter).astype(BF)
@@ -718,7 +688,6 @@
     grad_in_ref[...] = (g_middle[...] + scale * (total * gain_first[...] - normed * mean)).astype(BF)
 
     sum_turn(out_copies, pown2, r1b)
-    pl.loop(2, lines - 1)(lambda j: down_turn(j))
     total = sum_end(out_copies, pown2, r2b)
     mlp_part = valid_ref[...] * total
     value = middle[...] + mlp_part
@@ -771,25 +740,20 @@
         small_copy(i).wait_recv()
         small_ref[...] = small_ref[...] + small_recv[i]
 
-    small_step(0)
     rs_close(DOWN)
     final_start(DOWN, 30)
-    small_take(0)
-    small_step(1)
-    rs_turn(MLP, 0)
-    small_take(1)
-    small_step(2)
+    pl.loop(1, lines)(lambda s: rs_turn(MLP, s))
     final_pass(DOWN, 30)
-    pl.loop(1, lines - 1)(lambda j: rs_turn(MLP, j))
-    for i in range(2, len(peers)):
+    small_step(0)
+    for i in range(len(peers)):
         small_take(i)
         if i + 1 < len(peers):
             small_step(i + 1)
+    rs_turn(FIRST, 1)
     rs_close(MLP)
     final_start(MLP, 33)
-    rs_turn(FIRST, 0)
+    pl.loop(2, lines)(lambda s: rs_turn(FIRST, s))
     final_pass(MLP, 33)
-    pl.loop(1, lines - 1)(lambda j: rs_turn(FIRST, j))
     rs_close(FIRST)
     final_start(FIRST, 36)
     final_pass(FIRST, 36)
@@ -809,8 +773,6 @@
     width = heads * hd
     first, mlp, down = shards_in
     bits = shards.bit_length() - 1
-    tall = max(s.shape[0] for s in shards_in)
-    broad = max(s.shape[1] for s in shards_in)
 
     def shape(dtype, *dims):
         return jax.ShapeDtypeStruct(dims, dtype)
@@ -820,27 +782,26 @@
     out_shape = (
         shape(BF, t, d), shape(BF, t, d), shape(F32, 64, 128),
         *(shape(BF, 4, *s.shape) for s in shards_in),
-        *(shape(BF, 3, shards, *s.shape) for s in shards_in),
     )
     scratch = [
         *(v((shards, *s.shape), BF) for s in shards_in),
         v((4, t, d), BF), v((4, t, d), BF), v((4, 8, t), F32), v((4, t, d), BF), v((4, t, 3 * width), BF),
-        v((4, t, width), F32), v((4, t, width), F32), v((4, heads, t, t), F32), v((4, heads, t, t), BF),
+        v((4, t, width), F32), v((4, t, 128), F32), v((4, heads, t, t), F32), v((4, heads, t, t), BF),
         v((4, t, width), BF), v((shards // 4, first.shape[0], d), BF),
-        v((t, d), F32), v((4 * t, units), F32), v((4 * t, units), F32), v((4, t, units), BF), v((4, t, 2 * units), BF),
+        v((t, d), F32), v((4 * t, units), BF), v((4 * t, units), BF), v((4, t, units), BF), v((4, t, 2 * units), BF),
         v((4, t, d), BF), v((t, d), F32), v((4, t, 3 * width), BF), v((4, t, width), F32),
-        v((shards // 4, first.shape[0], d), BF), v((shards, first.shape[0], width), BF),
-        v((2, t, d), BF), v((2, t, d), F32), v((2, t, d), BF), v((t, d), BF), v((t, d), BF),
-        v((2, t, d), BF), v((2, t, d), F32), v((2, t, d), BF), v((t, d), BF),
+        v((shards, first.shape[0], width), BF),
+        v((2, t, d), BF), v((2, t, d), BF), v((2, t, d), BF), v((t, d), BF), v((t, d), BF),
+        v((2, t, d), BF), v((2, t, d), BF), v((2, t, d), BF), v((t, d), BF),
         v((heads, taps * t, t), BF), v((heads, taps * t, t), F32), v((t, width), F32), v((t, t), F32), v((2 * heads, t), F32),
-        v((tall, broad), BF), v((2 + bits, 64, 128), F32), v((2 + bits, 64, 128), F32),
-        dma((3, 3, shards)), dma((3, shards)), dma((3, 3, shards)), dma((3, 3, shards)), dma((48,)), dma((48,)), dma((8,)),
+        *(v((shards // 2, *s.shape), BF) for s in shards_in + shards_in), v((2 + bits, 64, 128), F32), v((2 + bits, 64, 128), F32),
+        dma((3, 3, shards)), dma((3, shards)), dma((3, 2, shards // 2)), dma((3, 2, shards // 2)), dma((48,)), dma((48,)), dma((8,)), pltpu.SemaphoreType.REGULAR,
     ]
     return pl.pallas_call(
         functools.partial(layer_kernel, cfg),
         out_shape=out_shape,
         in_specs=[vmem_spec()] * 7 + [smem_spec()] * 2 + [hbm_spec()] * 3,
-        out_specs=(vmem_spec(),) * 3 + (hbm_spec(),) * 6,
+        out_specs=(vmem_spec(),) * 3 + (hbm_spec(),) * 3,
         scratch_shapes=scratch,
         compiler_params=pltpu.CompilerParams(
             collective_id=0, has_side_effects=True, vmem_limit_bytes=VMEM_LIMIT
@@ -939,7 +900,7 @@
     block_out, grad_in, small, a_first, a_mlp, a_down = run_layer(
         cfg, hidden_in.reshape(t, d), grad_out.reshape(t, d), seg_own, valid, gains, score, mix,
         (first_shard, mlp_shard, down_shard),
-    )[:6]
+    )
 
     lines = d // 128
     base = 3 * lines

time: 515 us -> 416 us (0.81); the launches traced: 506 us -> 415 us
  Pallas kernels: 473 us -> 382 us
    pallas_call x1, Pallas kernels: 465 us -> 373 us  [run_layer(): pl.pallas_call(functools.partial(layer_kernel, cfg), out_shape=out_shape,...]
where the time goes in v3:
time: 416 us; the launch traced here: 415 us
  Pallas kernels  382 us (92%)
  local copies, waits for them, and re-layouts  29.2 us (7%)
    pallas_call x1, Pallas kernels, run_layer(): pl.pallas_call(functools.partial(layer_kernel, cfg), out_shape=out_shape,...  373 us
    dynamic_slice x7, local copies, waits for them, and re-layouts, mine(): return lax.dynamic_slice_in_dim(array, me * size, size, axis)  11 us
    pallas_call x1, Pallas kernels, widen(): pl.pallas_call(functools.partial(widen_kernel, strip, count), grid=(steps...  8.42 us

profile of v3, /device:TPU:9, one launch (start us, length us, event | category | flops | bytes accessed | tf_op | source)
XLA Modules:
  0.0 415.5 jit_solution(15988425140420894653)
XLA Ops:
  0.7 0.9 reduce_window_sum.11
  1.7 0.6 broadcast_in_dim.2.refs_2_
  2.3 0.7 copy.48.refs_3_
  3.0 1.3 reshape.164.refs_4_
  4.3 1.3 reshape.165.refs_5_
  5.6 0.8 dynamic_slice.30
  7.0 0.9 copy.44
  8.5 0.7 constant_dynamic-slice_fusion.5
  9.3 0.7 copy.51.refs_8_
  10.0 1.0 constant_dynamic-slice_fusion.1
  11.0 1.0 constant_dynamic-slice_fusion.3
  12.0 0.9 pad_maximum_fusion.1.refs_9_
  12.9 2.8 reshape.170
  15.7 3.8 reshape.168
  19.5 6.1 %dynamic-slice_reduce_fusion = (bf16[192,8,128]{2,1,0:T(8,128)(2,1)S(1)}, bf16[192,8,128]{2,1,0:T(8,128)(2,1)S(1)}) fusion(bf16[192,8,4,128]{3,2,1,0:T(4,128)(2,1)S(1)} %reshape.170, s32[]{:T(128)S(6)} %select_n.20, bf16[192,8,4,128]{3,2,1,0:T(4,128)(2,1)} %reshape.168), kind=kLoop, calls=%fused_computation.1 | loop fusion | bytes 1572868 | tf_op jit(solution)/shard_map/dynamic_slice | solution.py:882
  25.8 0.9 pad_maximum_fusion.refs_10_
  26.7 0.8 constant_dynamic-slice_fusion.refs_11_
  27.5 373.1 %shard_map.262 = (bf16[128,1536]{1,0:T(8,128)(2,1)}, bf16[128,1536]{1,0:T(8,128)(2,1)}, f32[64,128]{1,0:T(8,128)}, bf16[4,192,1536]{2,1,0:T(8,128)(2,1)}, bf16[4...) custom-call(bf16[128,1536]{1,0:T(8,128)(2,1)} %bitcast.32, bf16[128,1536]{1,0:T(8,128)(2,1)} %bitcast.33, ...), custom_call_target="tpu_custom_call" | custom-call | tf_op jit(solution)/shard_map/pallas_call | solution.py:800
  400.6 8.4 %shard_map.263 = (f32[192,1536]{1,0:T(8,128)}, f32[192,1536]{1,0:T(8,128)}, f32[192,1536]{1,0:T(8,128)}, f32[192,1536]{1,0:T(8,128)}, f32[192,4096]{1,0:T(8,128)...) custom-call(bf16[4,192,1536]{2,1,0:T(8,128)(2,1)} %get-tuple-element.30.first_ref, ...), custom_call_target="tpu_custom_call" | custom-call | tf_op jit(solution)/shard_map/pallas_call | solution.py:836
  409.0 0.6 slice_bitcast_fusion
  409.7 0.8 copy.49
  410.6 0.6 copy.50
  413.0 1.8 copy.62
  414.7 0.7 copy.63
  (20 shorter events, 2.7 us)
Async XLA Ops:
  0.6 26.1 %copy-start = (bf16[512,1536]{1,0:T(8,128)(2,1)S(1)}, bf16[512,1536]{1,0:T(8,128)(2,1)}, u32[]{:S(2)}) copy-start(bf16[512,1536]{1,0:T(8,128)(2,1)} %param.23) | copy-start | bytes 4718596
  400.6 8.4 %copy-start.2 = (f32[64,128]{1,0:T(8,128)S(1)}, f32[64,128]{1,0:T(8,128)}, u32[]{:S(2)}) copy-start(f32[64,128]{1,0:T(8,128)} %get-tuple-element.40) | copy-start | bytes 98308
  400.6 14.1 %copy-start.1 = (bf16[128,1536]{1,0:T(8,128)(2,1)S(1)}, bf16[128,1536]{1,0:T(8,128)(2,1)}, u32[]{:S(2)}) copy-start(bf16[128,1536]{1,0:T(8,128)(2,1)} %get-tuple-element.29) | copy-start | bytes 1179652

commit v4 on v3

--- a/solution.py
+++ b/solution.py
@@ -72,14 +72,18 @@
 
 def layer_kernel(cfg, *refs):
     heads, hd, taps, span, docs, shards, units = cfg
+    strip = units // shards
+    mlp_parts = 2 if strip % 128 == 0 else 1
+    given, refs = refs[: 13 + mlp_parts], refs[13 + mlp_parts :]
+    x_ref, g_ref, first_norm, second_norm, head_norm, docs_ref, score_ref, mix_ref = given[:8]
+    own_first, own_down, own_mlp = given[8:12], given[12], given[13:]
     (
-        x_ref, g_ref, seg_ref, valid_ref, gain_first, gain_second, gain_head, score_ref, mix_ref,
-        own_first, own_mlp, own_down,
-        out_ref, grad_in_ref, small_ref, all_first, all_mlp, all_down,
+        out_ref, grad_in_ref, grad_first_norm, grad_second_norm, grad_head_norm, grad_score, grad_mix, means,
+        all_first, all_mlp, all_down,
         w_first, w_mlp, w_down, wide, g_mlp, seg_all, attn_in, qkv, hat, inv, probs, masked, head_in, w_out,
         middle, slope, silu, hidden, g_gu, g_attn, g_middle, g_qkv, g_hin, d_out_in,
         psend, pown, r1, ysend, r2, psend2, pown2, r1b, r2b, bands, corr, g_wide, lanes, g_mix,
-        x_first, x_mlp, x_down, z_first, z_mlp, z_down, small_send, small_recv,
+        x_first, x_mlp, x_down, z_first, z_mlp, z_down, small_send, small_recv, small_ref, valid_ref, gain_first, gain_second, gain_all, gain_head,
         ag_send, ag_recv, rs_send, rs_recv, rep_send, rep_recv, local, credit,
     ) = refs
     t, d = x_ref.shape
@@ -98,7 +102,6 @@
     peer_of = (f + 2, f - 2, partner)
     tokens = 4 * t
     part = shards // 4
-    strip = units // shards
     rows, cols = grids(t)
 
     def flip(bit):
@@ -364,16 +367,53 @@
         c.wait_send()
         here.wait()
 
-    owns = (own_first, own_mlp, own_down)
-    loads = [pltpu.make_async_copy(owns[k], weights[k].at[f], local.at[4 + k]) for k in range(3)]
-    for load in loads:
-        load.start()
+    def cut(ref, at, size):
+        return ref.at[:, pl.ds(pl.multiple_of(at, size), size)]
+
+    sources = [
+        [(cut(own_first[i], me * quarter, quarter), w_first.at[f, :, pl.ds(i * quarter, quarter)]) for i in range(4)],
+        [(own_mlp[0], w_mlp.at[f])],
+        [(own_down.at[pl.ds(pl.multiple_of(me * strip, strip), strip), :], w_down.at[f])],
+    ]
+    if mlp_parts == 2:
+        sources[MLP] = [
+            (cut(own_mlp[i // shards], (4 * (i % shards) + me) * strip, strip), w_mlp.at[f, :, pl.ds(i * strip, strip)])
+            for i in range(2 * shards)
+        ]
+    loads, used = [], 4
+    for pairs in sources:
+        loads.append([pltpu.make_async_copy(a, b, local.at[used + i]) for i, (a, b) in enumerate(pairs)])
+        used += len(pairs)
+    for k in range(3):
+        for load in loads[k]:
+            load.start()
+
+    def load_wait(k):
+        for load in loads[k]:
+            load.wait()
+
+    lane = lax.broadcasted_iota(jnp.int32, (1, t), 1)
+    seg = jnp.zeros((1, t), F32)
+    edge = 0
+    for i in range(docs):
+        edge = edge + docs_ref[0, i]
+        seg = seg + jnp.where(lane >= edge, 1.0, 0.0)
+    valid = jnp.where(jnp.transpose(jnp.broadcast_to(seg, (t, t))) < float(docs), 1.0, 0.0)
+    valid_ref[...] = valid[:, 0:1]
+
+    def as_row(ref):
+        return jnp.concatenate([ref[i : i + 1, :] for i in range(ref.shape[0])], axis=1)
+
+    gain_first[...] = as_row(first_norm)
+    gain_second[...] = as_row(second_norm)
+    gain_all[...] = as_row(head_norm)
+    gain_head[...] = gain_all[:, pl.ds(pl.multiple_of(me * quarter, quarter), quarter)]
     wide[me] = x_ref[...]
     g_mlp[me] = g_ref[...]
-    seg_all[me] = seg_ref[...]
+    seg_all[me] = jnp.broadcast_to(seg, (8, t))
     entering = (seg_all, wide, g_mlp)
     gather_start(entering, 0)
-    loads[FIRST].wait()
+    load_wait(FIRST)
     ag_steps(FIRST, 0, 1)
 
     diff = cols - rows + (span - 1) // 2
@@ -383,12 +423,12 @@
         for a in range(taps):
             band = jnp.zeros((t, t), F32)
             for b in range(span):
-                band = jnp.where(diff == b, score_ref[h, a * span + b], band)
+                band = jnp.where(diff == b, score_ref[me * heads + h, a, b], band)
             bands[h, a * t : (a + 1) * t, :] = band.astype(BF)
 
     gather_pass(entering, 0)
     ag_steps(FIRST, 1, 2)
-    loads[DOWN].wait()
+    load_wait(DOWN)
     ag(DOWN, f, SIDE).start()
     gather_end(entering, 0)
 
@@ -401,7 +441,7 @@
         g_mlp[r] = jnp.where(valid, g_mlp[r].astype(F32), 0.0).astype(BF)
 
     ag_steps(FIRST, 2, 3)
-    loads[MLP].wait()
+    load_wait(MLP)
     ag_steps(MLP, 0, 1)
     ag_steps(FIRST, 3, lines)
     ag_steps(MLP, 1, 2)
@@ -449,7 +489,7 @@
                 both.append(p)
             for e in range(2):
                 h = 2 * pair + e
-                mixed = (mix_ref[h, 0] * both[0] + mix_ref[h, 1] * both[1]).astype(BF)
+                mixed = (mix_ref[me * heads + h, 0] * both[0] + mix_ref[me * heads + h, 1] * both[1]).astype(BF)
                 out = dot(mixed, split(qkv, row, 2, h))
                 centred = out - mean_of(out)
                 scale = lax.rsqrt(mean_of(centred * centred) + 1e-05)
@@ -609,7 +649,7 @@
         d_out_copy(peer, 24 + i).start()
     own_d_out = pltpu.make_async_copy(
         d_out.at[:, :, pl.ds(pl.multiple_of(me * quarter, quarter), quarter)],
-        d_out_in.at[pl.ds(me * part, part)], local.at[7],
+        d_out_in.at[pl.ds(me * part, part)], local.at[4],
     )
     own_d_out.start()
     pl.loop(1, lines)(lambda s: rs_turn(DOWN, s))
@@ -635,7 +675,7 @@
                 g_mixed.append(dot(g, split(qkv, row, 2, h), NT))
             for e in range(2):
                 h = 2 * pair + e
-                mixed = (mix_ref[h, 0] * both[0] + mix_ref[h, 1] * both[1]).astype(BF)
+                mixed = (mix_ref[me * heads + h, 0] * both[0] + mix_ref[me * heads + h, 1] * both[1]).astype(BF)
                 g_v = dot(mixed, g_heads[e], TN)
                 g_qkv[row, :, 2 * width + h * hd : 2 * width + (h + 1) * hd] = g_v.astype(BF)
                 for c in range(2):
@@ -643,7 +683,7 @@
                     g_mix[place : place + 1, :] += row_sum(g_mixed[e] * both[c])
             for c in range(2):
                 h = 2 * pair + c
-                g_probs = mix_ref[2 * pair, c] * g_mixed[0] + mix_ref[2 * pair + 1, c] * g_mixed[1]
+                g_probs = mix_ref[me * heads + 2 * pair, c] * g_mixed[0] + mix_ref[me * heads + 2 * pair + 1, c] * g_mixed[1]
                 weighted = both[c] * g_probs
                 g_conv = weighted - both[c] * jnp.sum(weighted, axis=1, keepdims=True)
                 corr[h] += dot(lagged(masked[row, h].astype(F32), taps, rows), g_conv.astype(BF), TN)
@@ -749,6 +789,14 @@
         small_take(i)
         if i + 1 < len(peers):
             small_step(i + 1)
+    grad_first_norm[...] = small_ref[0:strips, :]
+    grad_second_norm[...] = small_ref[strips : 2 * strips, :]
+    grad_head_norm[...] = small_ref[2 * strips : 3 * strips, :]
+    at = 3 * strips
+    grad_score[...] = small_ref[at : at + 4 * heads, :]
+    grad_mix[...] = small_ref[at + 4 * heads : at + 4 * heads + 4, :]
+    sums = small_ref[at + 4 * heads + 4 : at + 4 * heads + 5, :]
+    means[...] = jnp.sqrt(sums / (sums[:, 3:4] * float(d)))
     rs_turn(FIRST, 1)
     rs_close(MLP)
     final_start(MLP, 33)
@@ -767,11 +815,11 @@
         d_out_copy(peer, 24 + i).wait_send()
 
 
-def run_layer(cfg, x, g, seg, valid, gains, score, mix, shards_in):
+def run_layer(cfg, vectors, scalars, first_in, down_in, mlp_in, sizes):
     heads, hd, taps, span, docs, shards, units = cfg
-    t, d = x.shape
+    t, d = vectors[0].shape
     width = heads * hd
-    first, mlp, down = shards_in
+    first, mlp, down = shards_in = sizes
     bits = shards.bit_length() - 1
 
     def shape(dtype, *dims):
@@ -780,7 +828,8 @@
     v = pltpu.VMEM
     dma = pltpu.SemaphoreType.DMA
     out_shape = (
-        shape(BF, t, d), shape(BF, t, d), shape(F32, 64, 128),
+        shape(BF, t, d), shape(BF, t, d), *(shape(F32, d // 128, 128) for _ in range(3)),
+        shape(F32, 4 * heads, 128), shape(F32, 4, 128), shape(F32, 1, 128),
         *(shape(BF, 4, *s.shape) for s in shards_in),
     )
     scratch = [
@@ -795,18 +844,19 @@
         v((2, t, d), BF), v((2, t, d), BF), v((2, t, d), BF), v((t, d), BF),
         v((heads, taps * t, t), BF), v((heads, taps * t, t), F32), v((t, width), F32), v((t, t), F32), v((2 * heads, t), F32),
         *(v((shards // 2, *s.shape), BF) for s in shards_in + shards_in), v((2 + bits, 64, 128), F32), v((2 + bits, 64, 128), F32),
-        dma((3, 3, shards)), dma((3, shards)), dma((3, 2, shards // 2)), dma((3, 2, shards // 2)), dma((48,)), dma((48,)), dma((8,)), pltpu.SemaphoreType.REGULAR,
+        v((64, 128), F32), v((t, 1), F32), v((1, d), F32), v((1, d), F32), v((1, d), F32), v((1, width), F32),
+        dma((3, 3, shards)), dma((3, shards)), dma((3, 2, shards // 2)), dma((3, 2, shards // 2)), dma((48,)), dma((48,)), dma((10 + 2 * shards,)), pltpu.SemaphoreType.REGULAR,
     ]
     return pl.pallas_call(
         functools.partial(layer_kernel, cfg),
         out_shape=out_shape,
-        in_specs=[vmem_spec()] * 7 + [smem_spec()] * 2 + [hbm_spec()] * 3,
-        out_specs=(vmem_spec(),) * 3 + (hbm_spec(),) * 3,
+        in_specs=[vmem_spec()] * 5 + [smem_spec()] * 3 + [hbm_spec()] * (5 + len(mlp_in)),
+        out_specs=(vmem_spec(),) * 8 + (hbm_spec(),) * 3,
         scratch_shapes=scratch,
         compiler_params=pltpu.CompilerParams(
             collective_id=0, has_side_effects=True, vmem_limit_bytes=VMEM_LIMIT
         ),
-    )(x, g, seg, valid, *gains, score, mix, *shards_in)
+    )(*vectors, *scalars, *first_in, down_in, *mlp_in)
 
 
 def widen_kernel(strip, count, first_ref, mlp_ref, down_ref, *outs):
@@ -884,32 +934,22 @@
     def strips(w):
         return mine(w.reshape(rows_here, shards, reps, strip), 1, 2).reshape(rows_here, units)
 
-    first_shard = jnp.concatenate([mine(w, quarter, 1) for w in (w_query, w_key, w_value, w_output)], axis=1)
-    mlp_shard = jnp.concatenate([strips(w_gate), strips(w_up)], axis=1)
-    down_shard = mine(w_down, strip, 0)
-
-    boundary = jnp.cumsum(doc_lengths[:, :-1], axis=1)
-    places = jnp.arange(t, dtype=jnp.int32)
-    seg_ids = jnp.sum((places[None, :, None] >= boundary[:, None, :]).astype(jnp.int32), axis=2)
-    seg_own = jnp.broadcast_to(seg_ids.astype(F32), (8, t))
-    valid = (seg_ids < docs).astype(F32).reshape(t, 1)
-    gains = (attn_norm.reshape(1, d), mlp_norm.reshape(1, d), mine(head_norm, quarter, 0).reshape(1, quarter))
-    score = mine(score_kernel.reshape(H, taps * span), heads, 0)
-    mix = mine(head_mixing, heads, 0)
+    if strip % 128 == 0:
+        mlp_in = (w_gate, w_up)
+    else:
+        mlp_in = (jnp.concatenate([strips(w_gate), strips(w_up)], axis=1),)
+    lines = d // 128
     cfg = (heads, hd, taps, span, docs, shards, units)
-    block_out, grad_in, small, a_first, a_mlp, a_down = run_layer(
-        cfg, hidden_in.reshape(t, d), grad_out.reshape(t, d), seg_own, valid, gains, score, mix,
-        (first_shard, mlp_shard, down_shard),
+    shape_of = jax.ShapeDtypeStruct
+    block_out, grad_in, n_first, n_second, n_head, g_score, g_mix, means, a_first, a_mlp, a_down = run_layer(
+        cfg,
+        (hidden_in.reshape(t, d), grad_out.reshape(t, d), *(n.reshape(lines, 128) for n in (attn_norm, mlp_norm, head_norm))),
+        (doc_lengths, score_kernel, head_mixing),
+        (w_query, w_key, w_value, w_output),
+        w_down,
+        mlp_in,
+        (shape_of((rows_here, d), BF), shape_of((rows_here, 2 * units), BF), shape_of((strip, d), BF)),
     )
-
-    lines = d // 128
-    base = 3 * lines
-    small_score = small[base : base + H, : taps * span]
-    base += H
-    small_mix = small[base : base + reps, : 2 * heads]
-    stats = small[base + reps, :STATS]
-    root_means = jnp.sqrt(stats[:3] / (stats[3] * d))
-
     if strip % 128 == 0:
         g_q, g_k, g_v, g_o, g_gate, g_up, g_down = widen(a_first, a_mlp, a_down, strip, shards)
     else:
@@ -930,12 +970,12 @@
         g_gate,
         g_up,
         g_down.reshape(w_down.shape),
-        small[:lines].reshape(d),
-        small[lines : 2 * lines].reshape(d),
-        small[2 * lines : 3 * lines].reshape(d),
-        small_score.reshape(score_kernel.shape),
-        small_mix.reshape(head_mixing.shape),
-        root_means,
+        n_first.reshape(d),
+        n_second.reshape(d),
+        n_head.reshape(d),
+        g_score[:, : taps * span].reshape(score_kernel.shape),
+        g_mix[:, : 2 * heads].reshape(head_mixing.shape),
+        means[0, :3],
     )
 
 

time: 416 us -> 392 us (0.942)
  local copies, waits for them, and re-layouts: 29.2 us -> 8.27 us
    dynamic_slice x7 -> x0, local copies, waits for them, and re-layouts: 11 us -> none  [mine(): return lax.dynamic_slice_in_dim(array, me * size, size, axis)]
    reshape x9 -> x2, local copies, waits for them, and re-layouts: 10.6 us -> 0.15 us  [the longest x1 0.08 us: per_device(): g_mix[:, :2 * heads].reshape(head_mixing.shape)]
where the time goes in v4:
time: 392 us
  Pallas kernels  383 us (98%)
  local copies, waits for them, and re-layouts  8.27 us (2%)
    pallas_call x1, Pallas kernels, run_layer(): pl.pallas_call(functools.partial(layer_kernel, cfg), out_shape=out_shape,...  374 us
    pallas_call x1, Pallas kernels, widen(): pl.pallas_call(functools.partial(widen_kernel, strip, count), grid=(steps...  8.44 us

profile of v4, /device:TPU:9, one launch (start us, length us, event | category | flops | bytes accessed | tf_op | source)
XLA Modules:
  0.0 391.7 jit_solution(5188801235547285435)
XLA Ops:
  0.6 1.5 copy.34.refs_6_
  2.2 1.4 copy.35.refs_7_
  3.5 374.3 %shard_map.262 = (bf16[128,1536]{1,0:T(8,128)(2,1)}, bf16[128,1536]{1,0:T(8,128)(2,1)}, f32[12,128]{1,0:T(8,128)}, f32[12,128]{1,0:T(8,128)}, f32[12,128]{1,0:T(...) custom-call(bf16[128,1536]{1,0:T(8,128)(2,1)} %bitcast.15, ...), custom_call_target="tpu_custom_call" | custom-call | tf_op jit(solution)/shard_map/pallas_call | solution.py:850
  377.8 0.0 copy-start.2
  377.8 0.0 copy-start.6
  377.9 0.0 copy-start.7
  377.9 0.0 copy-start.1
  377.9 0.0 copy-start
  377.9 8.4 %shard_map.263 = (f32[192,1536]{1,0:T(8,128)}, f32[192,1536]{1,0:T(8,128)}, f32[192,1536]{1,0:T(8,128)}, f32[192,1536]{1,0:T(8,128)}, f32[192,4096]{1,0:T(8,128)...) custom-call(bf16[4,192,1536]{2,1,0:T(8,128)(2,1)} %get-tuple-element.35.first_ref, ...), custom_call_target="tpu_custom_call" | custom-call | tf_op jit(solution)/shard_map/pallas_call | solution.py:886
  386.3 0.0 copy-start.3
  386.3 0.0 copy-done.2
  386.3 0.1 reshape.80
  386.4 0.8 copy.36
  387.2 0.0 copy-done.6
  387.2 0.1 reshape.81
  387.3 0.6 copy.37
  387.9 0.5 slice_bitcast_fusion
  388.4 0.7 copy.43
  389.2 0.7 copy.44
  389.9 0.0 copy-done.5
  389.9 0.6 copy.45
  390.5 0.6 copy.46
  391.1 0.0 copy-done.3
  391.1 0.6 copy.47
  (6 shorter events, 0.0 us)
Async XLA Ops:
  377.8 8.5 %copy-start.2 = (f32[16,128]{1,0:T(8,128)S(1)}, f32[16,128]{1,0:T(8,128)}, u32[]{:S(2)}) copy-start(f32[16,128]{1,0:T(8,128)} %get-tuple-element.48) | copy-start | bytes 24580
  377.8 9.3 %copy-start.6 = (f32[4,128]{1,0:T(4,128)S(1)}, f32[4,128]{1,0:T(4,128)}, u32[]{:S(2)}) copy-start(f32[4,128]{1,0:T(4,128)} %get-tuple-element.49) | copy-start | bytes 6148
  377.9 10.0 %copy-start.7 = (f32[1,128]{1,0:T(1,128)S(1)}, f32[1,128]{1,0:T(1,128)}, u32[]{:S(2)}) copy-start(f32[1,128]{1,0:T(1,128)} %get-tuple-element.50) | copy-start | bytes 1540
  377.9 10.6 %copy-start.1 = (bf16[128,1536]{1,0:T(8,128)(2,1)S(1)}, bf16[128,1536]{1,0:T(8,128)(2,1)}, u32[]{:S(2)}) copy-start(bf16[128,1536]{1,0:T(8,128)(2,1)} %get-tuple-element.33) | copy-start | bytes 1179652
  377.9 11.3 %copy-start = (bf16[128,1536]{1,0:T(8,128)(2,1)S(1)}, bf16[128,1536]{1,0:T(8,128)(2,1)}, u32[]{:S(2)}) copy-start(bf16[128,1536]{1,0:T(8,128)(2,1)} %get-tuple-element.34) | copy-start | bytes 1179652
  386.3 3.6 copy-start.5
  386.3 4.2 %copy-start.4 = (f32[12,128]{1,0:T(8,128)S(1)}, f32[12,128]{1,0:T(8,128)}, u32[]{:S(2)}) copy-start(f32[12,128]{1,0:T(8,128)} %get-tuple-element.46) | copy-start | bytes 18436
  386.3 4.8 %copy-start.3 = (f32[12,128]{1,0:T(8,128)S(1)}, f32[12,128]{1,0:T(8,128)}, u32[]{:S(2)}) copy-start(f32[12,128]{1,0:T(8,128)} %get-tuple-element.47) | copy-start | bytes 18436

commit v5 on v4

--- a/solution.py
+++ b/solution.py
@@ -84,7 +84,7 @@
         middle, slope, silu, hidden, g_gu, g_attn, g_middle, g_qkv, g_hin, d_out_in,
         psend, pown, r1, ysend, r2, psend2, pown2, r1b, r2b, bands, corr, g_wide, lanes, g_mix,
         x_first, x_mlp, x_down, z_first, z_mlp, z_down, small_send, small_recv, small_ref, valid_ref, gain_first, gain_second, gain_all, gain_head,
-        ag_send, ag_recv, rs_send, rs_recv, rep_send, rep_recv, local, credit,
+        ag_send, ag_recv, rs_send, rs_recv, rs_side_recv, rep_send, rep_recv, local, credit,
     ) = refs
     t, d = x_ref.shape
     width = heads * hd
@@ -273,29 +273,57 @@
         copies[1].wait_send()
         return total
 
+    def yes(condition):
+        return int(condition) if isinstance(condition, bool) else condition.astype(jnp.int32)
+
+    def far_slot(at, target):
+        return at if lines == 4 else target
+
+    def near_slot(source, target):
+        return source if lines == 4 else lines + source - target + 2 - yes(source > target)
+
+    def target_of(s):
+        ahead = lines - 1 - z
+        first_end, last_end = yes(z == 0), yes(z == lines - 1)
+        inner = 1 - first_end - last_end
+        if lines == 4:
+            near = yes(s == 1) * (z + 1) + yes(s == 2) * (z - 1) + yes(s == 3) * (3 * (2 - z))
+        else:
+            near = yes(s <= ahead) * (z + s) + yes(s > ahead) * (z - (s - ahead))
+        return first_end * (lines - s) + last_end * (s - 1) + inner * near
+
     def rs_side(k, zz):
         source = weights[k].at[2 * zz + (1 - side)]
         if k == DOWN:
             source = x_mlp.at[zz, pl.ds(0, strip), pl.ds(0, d)]
         return pltpu.make_async_remote_copy(
             src_ref=source, dst_ref=x_lands[k].at[zz],
-            send_sem=rs_send.at[k, 0, zz], recv_sem=rs_recv.at[k, 0, zz],
+            send_sem=rs_send.at[k, 0, zz], recv_sem=rs_side_recv.at[k, zz],
             device_id=(me, partner), device_id_type=MESH,
         )
 
-    def rs_owner(k, zz):
+    def rs_hop(k, target):
+        up = yes(target > z)
+        toward = z + 2 * up - 1
+        distance = up * (target - z) + (1 - up) * (z - target)
+        far = yes(distance >= 3)
+        to = far * toward + (1 - far) * target
+        slot = far * far_slot(toward, target) + (1 - far) * near_slot(z, target)
+        at = slot
         return pltpu.make_async_remote_copy(
-            src_ref=weights[k].at[2 * zz + side], dst_ref=z_lands[k].at[z],
-            send_sem=rs_send.at[k, 1, zz], recv_sem=rs_recv.at[k, 1, z],
-            device_id=(me, 2 * zz + side), device_id_type=MESH,
+            src_ref=weights[k].at[2 * target + side], dst_ref=z_lands[k].at[at],
+            send_sem=rs_send.at[k, 1, 2 * target], recv_sem=rs_recv.at[k, at],
+            device_id=(me, 2 * to + side), device_id_type=MESH,
         )
 
-    def rs_from(k, zz):
-        return pltpu.make_async_remote_copy(
-            src_ref=weights[k].at[2 * zz + side], dst_ref=z_lands[k].at[zz],
-            send_sem=rs_send.at[k, 1, zz], recv_sem=rs_recv.at[k, 1, zz],
-            device_id=(me, 2 * zz + side), device_id_type=MESH,
-        )
+    def rs_landed(k, slot):
+        at = slot
+        pltpu.make_async_remote_copy(
+            src_ref=weights[k].at[f], dst_ref=z_lands[k].at[at],
+            send_sem=rs_send.at[k, 1, f], recv_sem=rs_recv.at[k, at],
+            device_id=(me, partner), device_id_type=MESH,
+        ).wait_recv()
+        return z_lands[k], at
 
     def rs_add(k, block, landed):
         grad = weights[k]
@@ -310,30 +338,45 @@
                 total = total + land[slot, at, :].astype(F32)
             grad[block, at, :] = total.astype(BF)
 
-    def after(s):
-        return (z + s) % lines
-
     def rs_turn(k, s):
-        zz = after(s)
-        rs_side(k, zz).wait_recv()
-        rs_add(k, 2 * zz + side, [(x_lands[k], zz)])
-        rs_owner(k, zz).start()
+        target = target_of(s)
+        up = yes(target > z)
+        distance = up * (target - z) + (1 - up) * (z - target)
+        behind = up * yes(z > 0) + (1 - up) * yes(z < lines - 1)
+        rs_side(k, target).wait_recv()
+        handed = (distance >= 2) & (behind == 1)
+
+        @pl.when(handed)
+        def _():
+            land = rs_landed(k, far_slot(z, target))
+            rs_add(k, 2 * target + side, [(x_lands[k], target), land])
+
+        @pl.when(jnp.logical_not(handed))
+        def _():
+            rs_add(k, 2 * target + side, [(x_lands[k], target)])
+
+        rs_hop(k, target).start()
 
     def rs_close(k):
+        first_end, last_end = yes(z == 0), yes(z == lines - 1)
+        inner = 1 - first_end - last_end
+        one = first_end * 1 + (1 - first_end) * (z - 1)
+        two = first_end * 2 + last_end * (lines - 3) + inner * (z + 1)
         rs_side(k, z).wait_recv()
-        landed = [(x_lands[k], z)]
-        for s in range(1, lines):
-            rs_from(k, after(s)).wait_recv()
-            landed.append((z_lands[k], after(s)))
-        rs_add(k, f, landed)
+        rs_add(k, f, [(x_lands[k], z), rs_landed(k, near_slot(one, z)), rs_landed(k, near_slot(two, z))])
+
+        @pl.when((z > 0) & (z + 2 < lines))
+        def _():
+            rs_add(k, f, [rs_landed(k, near_slot(z + 2, z))])
+
+        @pl.when((z < lines - 1) & (z >= 2))
+        def _():
+            rs_add(k, f, [rs_landed(k, near_slot(z - 2, z))])
 
     def rs_drain(k):
         if k != DOWN:
-            pl.loop(0, lines)(lambda s: rs_side(k, after(s)).wait_send())
-
-        @pl.loop(1, lines)
-        def _(s):
-            rs_owner(k, after(s)).wait_send()
+            pl.loop(0, lines)(lambda zz: rs_side(k, zz).wait_send())
+        pl.loop(1, lines)(lambda s: rs_hop(k, target_of(s)).wait_send())
 
     outs = (all_first, all_mlp, all_down)
 
@@ -547,9 +590,8 @@
             half = jnp.where(side == 0, value[2 * j + 1], value[2 * j])
             x_mlp[i * (part // 2) + j, 0:strip, 0:d] = half.astype(BF)
 
-    @pl.loop(1, lines + 1)
-    def _(s):
-        rs_side(DOWN, after(s)).start()
+    pl.loop(1, lines)(lambda s: rs_side(DOWN, target_of(s)).start())
+    rs_side(DOWN, z).start()
 
     ag_steps(DOWN, 3, lines)
 
@@ -594,11 +636,13 @@
     g_attn[me] = (valid_ref[...] * value).astype(BF)
     gather_start((g_attn,), 21)
     ag_drain(MLP)
-    pl.loop(0, lines)(lambda s: rs_side(DOWN, after(s)).wait_send())
+    pl.loop(0, lines)(lambda zz: rs_side(DOWN, zz).wait_send())
     pl.semaphore_signal(credit, inc=1, device_id=(me, partner), device_id_type=MESH)
 
     def in_turn(i):
-        return (z // (part // 2) + 1 + i) % 4
+        if lines != 4:
+            return i
+        return yes(i < 3) * target_of(i + 1) + yes(i == 3) * z
 
     def send_side(k, p):
         @pl.loop(0, part // 2)
@@ -697,6 +741,7 @@
                 g_qkv[row, :, h * hd : (h + 1) * hd] = g_q.astype(BF)
                 g_qkv[row, :, width + h * hd : width + (h + 1) * hd] = g_k.astype(BF)
 
+    rs_turn(MLP, 1)
     in_copies = sum_copies(27, psend, r1, r2)
     product = lambda a, b, i: dot(pair_of(g_qkv, a, b), merge(w_first[pl.ds(i * part, part), :, 0 : 3 * quarter]), NT)
     sum_theirs(product, in_copies, psend)
@@ -718,6 +763,7 @@
         w_first[pl.ds(p * part, part), :, 3 * quarter :] = d_out_in[pl.ds(p * part, part)]
         send_side(FIRST, p)
 
+    rs_turn(MLP, 2)
     total = sum_end(in_copies, pown, r2)
     value = x_ref[...].astype(F32)
     scale = lax.rsqrt(mean_of(value * value) + 1e-06)
@@ -782,13 +828,25 @@
 
     rs_close(DOWN)
     final_start(DOWN, 30)
-    pl.loop(1, lines)(lambda s: rs_turn(MLP, s))
+    pl.loop(3, lines)(lambda s: rs_turn(MLP, s))
     final_pass(DOWN, 30)
     small_step(0)
-    for i in range(len(peers)):
+    small_take(0)
+    small_step(1)
+    rs_turn(FIRST, 1)
+    rs_close(MLP)
+    final_start(MLP, 33)
+    small_take(1)
+    small_step(2)
+    pl.loop(2, lines)(lambda s: rs_turn(FIRST, s))
+    final_pass(MLP, 33)
+    rs_close(FIRST)
+    final_start(FIRST, 36)
+    for i in range(2, len(peers)):
         small_take(i)
         if i + 1 < len(peers):
             small_step(i + 1)
+    final_pass(FIRST, 36)
     grad_first_norm[...] = small_ref[0:strips, :]
     grad_second_norm[...] = small_ref[strips : 2 * strips, :]
     grad_head_norm[...] = small_ref[2 * strips : 3 * strips, :]
@@ -797,14 +855,6 @@
     grad_mix[...] = small_ref[at + 4 * heads : at + 4 * heads + 4, :]
     sums = small_ref[at + 4 * heads + 4 : at + 4 * heads + 5, :]
     means[...] = jnp.sqrt(sums / (sums[:, 3:4] * float(d)))
-    rs_turn(FIRST, 1)
-    rs_close(MLP)
-    final_start(MLP, 33)
-    pl.loop(2, lines)(lambda s: rs_turn(FIRST, s))
-    final_pass(MLP, 33)
-    rs_close(FIRST)
-    final_start(FIRST, 36)
-    final_pass(FIRST, 36)
     for k in range(3):
         final_end(k, (36, 33, 30)[k])
     for k in range(3):
@@ -821,6 +871,8 @@
     width = heads * hd
     first, mlp, down = shards_in = sizes
     bits = shards.bit_length() - 1
+    lines = shards // 2
+    slots = lines if lines == 4 else lines + 4
 
     def shape(dtype, *dims):
         return jax.ShapeDtypeStruct(dims, dtype)
@@ -843,9 +895,9 @@
         v((2, t, d), BF), v((2, t, d), BF), v((2, t, d), BF), v((t, d), BF), v((t, d), BF),
         v((2, t, d), BF), v((2, t, d), BF), v((2, t, d), BF), v((t, d), BF),
         v((heads, taps * t, t), BF), v((heads, taps * t, t), F32), v((t, width), F32), v((t, t), F32), v((2 * heads, t), F32),
-        *(v((shards // 2, *s.shape), BF) for s in shards_in + shards_in), v((2 + bits, 64, 128), F32), v((2 + bits, 64, 128), F32),
+        *(v((lines, *s.shape), BF) for s in shards_in), *(v((slots, *s.shape), BF) for s in shards_in), v((2 + bits, 64, 128), F32), v((2 + bits, 64, 128), F32),
         v((64, 128), F32), v((t, 1), F32), v((1, d), F32), v((1, d), F32), v((1, d), F32), v((1, width), F32),
-        dma((3, 3, shards)), dma((3, shards)), dma((3, 2, shards // 2)), dma((3, 2, shards // 2)), dma((48,)), dma((48,)), dma((10 + 2 * shards,)), pltpu.SemaphoreType.REGULAR,
+        dma((3, 3, shards)), dma((3, shards)), dma((3, 2, shards)), dma((3, slots)), dma((3, lines)), dma((48,)), dma((48,)), dma((10 + 2 * shards,)), pltpu.SemaphoreType.REGULAR,
     ]
     return pl.pallas_call(
         functools.partial(layer_kernel, cfg),

time: 392 us -> 350 us (0.89); the launches traced: 392 us -> 344 us
  Pallas kernels: 383 us -> 335 us
    pallas_call x1, Pallas kernels: 374 us -> 327 us  [run_layer(): pl.pallas_call(functools.partial(layer_kernel, cfg), out_shape=out_shape,...]
where the time goes in v5:
time: 350 us; the launch traced here: 344 us
  Pallas kernels  335 us (96%)
  local copies, waits for them, and re-layouts  8.27 us (2%)
    pallas_call x1, Pallas kernels, run_layer(): pl.pallas_call(functools.partial(layer_kernel, cfg), out_shape=out_shape,...  327 us
    pallas_call x1, Pallas kernels, widen(): pl.pallas_call(functools.partial(widen_kernel, strip, count), grid=(steps...  8.44 us
    unnamed x25, local copies, waits for them, and re-layouts  7.6 us

profile of v5, /device:TPU:9, one launch (start us, length us, event | category | flops | bytes accessed | tf_op | source)
XLA Modules:
  0.0 344.0 jit_solution(12035373576048939242)
XLA Ops:
  0.6 1.5 copy.34.refs_6_
  2.2 1.4 copy.35.refs_7_
  3.5 326.6 %shard_map.262 = (bf16[128,1536]{1,0:T(8,128)(2,1)}, bf16[128,1536]{1,0:T(8,128)(2,1)}, f32[12,128]{1,0:T(8,128)}, f32[12,128]{1,0:T(8,128)}, f32[12,128]{1,0:T(...) custom-call(bf16[128,1536]{1,0:T(8,128)(2,1)} %bitcast.15, ...), custom_call_target="tpu_custom_call" | custom-call | tf_op jit(solution)/shard_map/pallas_call | solution.py:902
  330.1 0.0 copy-start.2
  330.2 0.0 copy-start.6
  330.2 0.0 copy-start.7
  330.2 0.0 copy-start.1
  330.2 0.0 copy-start
  330.2 8.4 %shard_map.263 = (f32[192,1536]{1,0:T(8,128)}, f32[192,1536]{1,0:T(8,128)}, f32[192,1536]{1,0:T(8,128)}, f32[192,1536]{1,0:T(8,128)}, f32[192,4096]{1,0:T(8,128)...) custom-call(bf16[4,192,1536]{2,1,0:T(8,128)(2,1)} %get-tuple-element.35.first_ref, ...), custom_call_target="tpu_custom_call" | custom-call | tf_op jit(solution)/shard_map/pallas_call | solution.py:938
  338.6 0.0 copy-start.3
  338.6 0.0 copy-done.2
  338.7 0.1 reshape.80
  338.7 0.8 copy.36
  339.5 0.0 copy-done.6
  339.5 0.1 reshape.81
  339.6 0.6 copy.37
  340.2 0.0 copy-done.7
  340.2 0.5 slice_bitcast_fusion
  340.7 0.7 copy.43
  341.5 0.7 copy.44
  342.2 0.0 copy-done.5
  342.2 0.6 copy.45
  342.8 0.6 copy.46
  343.4 0.6 copy.47
  (6 shorter events, 0.0 us)
Async XLA Ops:
  330.1 8.5 %copy-start.2 = (f32[16,128]{1,0:T(8,128)S(1)}, f32[16,128]{1,0:T(8,128)}, u32[]{:S(2)}) copy-start(f32[16,128]{1,0:T(8,128)} %get-tuple-element.48) | copy-start | bytes 24580
  330.2 9.3 %copy-start.6 = (f32[4,128]{1,0:T(4,128)S(1)}, f32[4,128]{1,0:T(4,128)}, u32[]{:S(2)}) copy-start(f32[4,128]{1,0:T(4,128)} %get-tuple-element.49) | copy-start | bytes 6148
  330.2 10.0 %copy-start.7 = (f32[1,128]{1,0:T(1,128)S(1)}, f32[1,128]{1,0:T(1,128)}, u32[]{:S(2)}) copy-start(f32[1,128]{1,0:T(1,128)} %get-tuple-element.50) | copy-start | bytes 1540
  330.2 10.6 %copy-start.1 = (bf16[128,1536]{1,0:T(8,128)(2,1)S(1)}, bf16[128,1536]{1,0:T(8,128)(2,1)}, u32[]{:S(2)}) copy-start(bf16[128,1536]{1,0:T(8,128)(2,1)} %get-tuple-element.33) | copy-start | bytes 1179652
  330.2 11.3 %copy-start = (bf16[128,1536]{1,0:T(8,128)(2,1)S(1)}, bf16[128,1536]{1,0:T(8,128)(2,1)}, u32[]{:S(2)}) copy-start(bf16[128,1536]{1,0:T(8,128)(2,1)} %get-tuple-element.34) | copy-start | bytes 1179652
  338.6 3.6 %copy-start.5 = (f32[12,128]{1,0:T(8,128)S(1)}, f32[12,128]{1,0:T(8,128)}, u32[]{:S(2)}) copy-start(f32[12,128]{1,0:T(8,128)} %get-tuple-element.45) | copy-start | bytes 18436
  338.6 4.2 %copy-start.4 = (f32[12,128]{1,0:T(8,128)S(1)}, f32[12,128]{1,0:T(8,128)}, u32[]{:S(2)}) copy-start(f32[12,128]{1,0:T(8,128)} %get-tuple-element.46) | copy-start | bytes 18436
  338.6 4.8 %copy-start.3 = (f32[12,128]{1,0:T(8,128)S(1)}, f32[12,128]{1,0:T(8,128)}, u32[]{:S(2)}) copy-start(f32[12,128]{1,0:T(8,128)} %get-tuple-element.47) | copy-start | bytes 18436

commit v6 on v5

--- a/solution.py
+++ b/solution.py
@@ -11,7 +11,7 @@
 BF = jnp.bfloat16
 F32 = jnp.float32
 MESH = pl.DeviceIdType.MESH
-VMEM_LIMIT = 62 * 1024 * 1024
+VMEM_LIMIT = 63 * 1024 * 1024
 NN = (((1,), (0,)), ((), ()))
 NT = (((1,), (1,)), ((), ()))
 TN = (((0,), (0,)), ((), ()))
@@ -435,6 +435,11 @@
         for load in loads[k]:
             load.wait()
 
+    load_wait(FIRST)
+    ag_steps(FIRST, 0, 1)
+    load_wait(DOWN)
+    ag(DOWN, f, SIDE).start()
+
     lane = lax.broadcasted_iota(jnp.int32, (1, t), 1)
     seg = jnp.zeros((1, t), F32)
     edge = 0
@@ -454,10 +459,8 @@
     wide[me] = x_ref[...]
     g_mlp[me] = g_ref[...]
     seg_all[me] = jnp.broadcast_to(seg, (8, t))
-    entering = (seg_all, wide, g_mlp)
+    entering = (seg_all, wide)
     gather_start(entering, 0)
-    load_wait(FIRST)
-    ag_steps(FIRST, 0, 1)
 
     diff = cols - rows + (span - 1) // 2
 
@@ -470,9 +473,8 @@
             bands[h, a * t : (a + 1) * t, :] = band.astype(BF)
 
     gather_pass(entering, 0)
+    gather_start((g_mlp,), 6)
     ag_steps(FIRST, 1, 2)
-    load_wait(DOWN)
-    ag(DOWN, f, SIDE).start()
     gather_end(entering, 0)
 
     @pl.loop(0, 4)
@@ -480,12 +482,18 @@
         value = wide[r].astype(F32)
         scale = lax.rsqrt(mean_of(value * value) + 1e-06)
         attn_in[r] = (value * scale * gain_first[...]).astype(BF)
-        valid = jnp.transpose(jnp.broadcast_to(seg_all[r][0:1, :], (t, t)))[:, 0:1] < float(docs)
-        g_mlp[r] = jnp.where(valid, g_mlp[r].astype(F32), 0.0).astype(BF)
 
     ag_steps(FIRST, 2, 3)
     load_wait(MLP)
     ag_steps(MLP, 0, 1)
+    gather_pass((g_mlp,), 6)
+    gather_end((g_mlp,), 6)
+
+    @pl.loop(0, 4)
+    def _(r):
+        valid = jnp.transpose(jnp.broadcast_to(seg_all[r][0:1, :], (t, t)))[:, 0:1] < float(docs)
+        g_mlp[r] = jnp.where(valid, g_mlp[r].astype(F32), 0.0).astype(BF)
+
     ag_steps(FIRST, 3, lines)
     ag_steps(MLP, 1, 2)
     ag_done(FIRST)
@@ -565,33 +573,33 @@
     ag_steps(DOWN, 2, 3)
     ag_done(MLP)
 
-    chunk = 256
-
-    @pl.loop(0, units // chunk)
+    chunk = units // 4
+
+    def in_turn(i):
+        if lines != 4:
+            return i
+        return yes(i < 3) * target_of(i + 1) + yes(i == 3) * z
+
+
+    @pl.loop(0, 4)
     def _(i):
-        at = pl.ds(pl.multiple_of(i * chunk, chunk), chunk)
-        after = pl.ds(pl.multiple_of(units + i * chunk, chunk), chunk)
+        p = in_turn(i)
+        at = pl.ds(pl.multiple_of(p * chunk, chunk), chunk)
+        after = pl.ds(pl.multiple_of(units + p * chunk, chunk), chunk)
         operand = mlp_in[...].reshape(tokens, d)
         gate = dot(operand, merge(w_mlp[:, :, at]))
         upper = dot(operand, merge(w_mlp[:, :, after]))
         sig = 1.0 / (1.0 + jnp.exp(-gate))
         act = gate * sig
-        hidden[:, :, at] = (act * upper).astype(BF).reshape(4, t, chunk)
+        product = (act * upper).astype(BF)
+        hidden[:, :, at] = product.reshape(4, t, chunk)
         silu[:, at] = act.astype(BF)
         slope[:, at] = (upper * sig * (1.0 + gate * (1.0 - sig))).astype(BF)
-
-    @pl.loop(0, 4)
-    def _(i):
-        span_units = units // 4
-        at = pl.ds(pl.multiple_of(i * span_units, span_units), span_units)
-        value = dot(hidden[:, :, at].reshape(tokens, span_units), g_mlp[...].reshape(tokens, d), TN)
-        value = value.reshape(part, strip, d)
+        value = dot(product, g_mlp[...].reshape(tokens, d), TN).reshape(part, strip, d)
         for j in range(part // 2):
             half = jnp.where(side == 0, value[2 * j + 1], value[2 * j])
-            x_mlp[i * (part // 2) + j, 0:strip, 0:d] = half.astype(BF)
-
-    pl.loop(1, lines)(lambda s: rs_side(DOWN, target_of(s)).start())
-    rs_side(DOWN, z).start()
+            x_mlp[p * (part // 2) + j, 0:strip, 0:d] = half.astype(BF)
+        pl.loop(0, part // 2)(lambda j: rs_side(DOWN, p * (part // 2) + j).start())
 
     ag_steps(DOWN, 3, lines)
 
@@ -609,20 +617,26 @@
     sum_theirs(product, mlp_copies, psend)
     sum_ours(product, pown)
 
-    out_copies = (rep_copy(psend2, r1b, 19, sibling), rep_copy(ysend, r2b, 20, across))
-    product = lambda a, b, i: dot(pair_of(hidden, a, b), merge(w_down[:, :, column_chunk(i)]))
-    sum_theirs(product, out_copies, psend2)
-    sum_ours(product, pown2)
     sum_turn(mlp_copies, pown, r1)
 
-    ag_drain(DOWN)
+    ag_drain(MLP)
+
+    def send_side(k, p):
+        @pl.loop(0, part // 2)
+        def _(j):
+            zz = p * (part // 2) + j
+            rs_side(k, zz).start()
 
     @pl.loop(0, 4)
-    def _(i):
-        span_units = units // 4
-        at = pl.ds(pl.multiple_of(i * span_units, span_units), span_units)
-        value = dot(hidden[:, :, at].reshape(tokens, span_units), g_mlp[...].reshape(tokens, d), TN)
-        w_down[pl.ds(i * part, part)] = value.reshape(part, w_down.shape[1], d).astype(BF)
+    def _(p):
+        at = pl.ds(pl.multiple_of(p * quarter, quarter), quarter)
+        size = units // 2
+
+        @pl.loop(0, 4)
+        def _(j):
+            to = pl.ds(pl.multiple_of(j * size, size), size)
+            value = dot(mlp_in[:, :, at].reshape(tokens, quarter), g_gu[:, :, to].reshape(tokens, size), TN)
+            w_mlp[pl.ds(p * part, part), :, to] = value.reshape(part, w_mlp.shape[1], size).astype(BF)
 
     total = sum_end(mlp_copies, pown, r2)
     value = middle[...]
@@ -635,45 +649,35 @@
     g_middle[...] = value
     g_attn[me] = (valid_ref[...] * value).astype(BF)
     gather_start((g_attn,), 21)
-    ag_drain(MLP)
+    out_copies = (rep_copy(psend2, r1b, 19, sibling), rep_copy(ysend, r2b, 20, across))
+    product = lambda a, b, i: dot(pair_of(hidden, a, b), merge(w_down[:, :, column_chunk(i)]))
+    sum_theirs(product, out_copies, psend2)
+    sum_ours(product, pown2)
+    ag_drain(DOWN)
+
+    @pl.loop(0, 4)
+    def _(i):
+        span_units = units // 4
+        at = pl.ds(pl.multiple_of(i * span_units, span_units), span_units)
+        value = dot(hidden[:, :, at].reshape(tokens, span_units), g_mlp[...].reshape(tokens, d), TN)
+        w_down[pl.ds(i * part, part)] = value.reshape(part, w_down.shape[1], d).astype(BF)
+
     pl.loop(0, lines)(lambda zz: rs_side(DOWN, zz).wait_send())
     pl.semaphore_signal(credit, inc=1, device_id=(me, partner), device_id_type=MESH)
 
-    def in_turn(i):
-        if lines != 4:
-            return i
-        return yes(i < 3) * target_of(i + 1) + yes(i == 3) * z
-
-    def send_side(k, p):
-        @pl.loop(0, part // 2)
-        def _(j):
-            zz = p * (part // 2) + j
-            rs_side(k, zz).start()
-
-    @pl.loop(0, 4)
-    def _(i):
-        p = in_turn(i)
-        at = pl.ds(pl.multiple_of(p * quarter, quarter), quarter)
-        size = units // 2
-
-        @pl.loop(0, 4)
-        def _(j):
-            to = pl.ds(pl.multiple_of(j * size, size), size)
-            value = dot(mlp_in[:, :, at].reshape(tokens, quarter), g_gu[:, :, to].reshape(tokens, size), TN)
-            w_mlp[pl.ds(p * part, part), :, to] = value.reshape(part, w_mlp.shape[1], size).astype(BF)
-
-
-        @pl.when(i == 0)
-        def _():
-            pl.semaphore_wait(credit, 1)
-
-        send_side(MLP, p)
+    pl.semaphore_wait(credit, 1)
+    pl.loop(1, lines)(lambda s: rs_side(MLP, target_of(s)).start())
+    rs_side(MLP, z).start()
 
     gather_pass((g_attn,), 21)
     gather_end((g_attn,), 21)
 
-    value = dot(g_attn[...].reshape(tokens, d), merge(w_out[...]), NT)
-    g_hin[...] = value.reshape(4, t, width)
+    @pl.loop(0, 2)
+    def _(i):
+        both = pl.ds(2 * i, 2)
+        value = dot(g_attn[both].reshape(2 * t, d), merge(w_out[...]), NT)
+        g_hin[both] = value.reshape(2, t, width)
+
     d_out = w_out
 
     @pl.loop(0, 4)

time: 350 us -> 339 us (0.969)
  Pallas kernels: 335 us -> 324 us
    pallas_call x1, Pallas kernels: 327 us -> 316 us  [run_layer(): pl.pallas_call(functools.partial(layer_kernel, cfg), out_shape=out_shape,...]
where the time goes in v6:
time: 339 us; the launch traced here: 333 us
  Pallas kernels  324 us (96%)
  local copies, waits for them, and re-layouts  8.27 us (2%)
    pallas_call x1, Pallas kernels, run_layer(): pl.pallas_call(functools.partial(layer_kernel, cfg), out_shape=out_shape,...  316 us
    pallas_call x1, Pallas kernels, widen(): pl.pallas_call(functools.partial(widen_kernel, strip, count), grid=(steps...  8.44 us
    unnamed x25, local copies, waits for them, and re-layouts  7.6 us

profile of v6, /device:TPU:9, one launch (start us, length us, event | category | flops | bytes accessed | tf_op | source)
XLA Modules:
  0.0 333.2 jit_solution(17917924911273620443)
XLA Ops:
  0.6 1.5 copy.34.refs_6_
  2.2 1.4 copy.35.refs_7_
  3.5 315.8 %shard_map.262 = (bf16[128,1536]{1,0:T(8,128)(2,1)}, bf16[128,1536]{1,0:T(8,128)(2,1)}, f32[12,128]{1,0:T(8,128)}, f32[12,128]{1,0:T(8,128)}, f32[12,128]{1,0:T(...) custom-call(bf16[128,1536]{1,0:T(8,128)(2,1)} %bitcast.15, ...), custom_call_target="tpu_custom_call" | custom-call | tf_op jit(solution)/shard_map/pallas_call | solution.py:906
  319.3 0.0 copy-start.2
  319.3 0.0 copy-start.6
  319.3 0.0 copy-start.7
  319.3 0.0 copy-start.1
  319.3 0.0 copy-start
  319.3 8.4 %shard_map.263 = (f32[192,1536]{1,0:T(8,128)}, f32[192,1536]{1,0:T(8,128)}, f32[192,1536]{1,0:T(8,128)}, f32[192,1536]{1,0:T(8,128)}, f32[192,4096]{1,0:T(8,128)...) custom-call(bf16[4,192,1536]{2,1,0:T(8,128)(2,1)} %get-tuple-element.35.first_ref, ...), custom_call_target="tpu_custom_call" | custom-call | tf_op jit(solution)/shard_map/pallas_call | solution.py:942
  327.8 0.0 copy-start.3
  327.8 0.0 copy-done.2
  327.8 0.1 reshape.80
  327.9 0.8 copy.36
  328.6 0.0 copy-done.6
  328.6 0.1 reshape.81
  328.7 0.6 copy.37
  329.4 0.5 slice_bitcast_fusion
  329.9 0.7 copy.43
  330.6 0.0 copy-done
  330.6 0.7 copy.44
  331.4 0.6 copy.45
  332.0 0.0 copy-done.4
  332.0 0.6 copy.46
  332.6 0.6 copy.47
  (6 shorter events, 0.0 us)
Async XLA Ops:
  319.3 8.5 %copy-start.2 = (f32[16,128]{1,0:T(8,128)S(1)}, f32[16,128]{1,0:T(8,128)}, u32[]{:S(2)}) copy-start(f32[16,128]{1,0:T(8,128)} %get-tuple-element.48) | copy-start | bytes 24580
  319.3 9.3 %copy-start.6 = (f32[4,128]{1,0:T(4,128)S(1)}, f32[4,128]{1,0:T(4,128)}, u32[]{:S(2)}) copy-start(f32[4,128]{1,0:T(4,128)} %get-tuple-element.49) | copy-start | bytes 6148
  319.3 10.0 %copy-start.7 = (f32[1,128]{1,0:T(1,128)S(1)}, f32[1,128]{1,0:T(1,128)}, u32[]{:S(2)}) copy-start(f32[1,128]{1,0:T(1,128)} %get-tuple-element.50) | copy-start | bytes 1540
  319.3 10.6 %copy-start.1 = (bf16[128,1536]{1,0:T(8,128)(2,1)S(1)}, bf16[128,1536]{1,0:T(8,128)(2,1)}, u32[]{:S(2)}) copy-start(bf16[128,1536]{1,0:T(8,128)(2,1)} %get-tuple-element.33) | copy-start | bytes 1179652
  319.3 11.3 %copy-start = (bf16[128,1536]{1,0:T(8,128)(2,1)S(1)}, bf16[128,1536]{1,0:T(8,128)(2,1)}, u32[]{:S(2)}) copy-start(bf16[128,1536]{1,0:T(8,128)(2,1)} %get-tuple-element.34) | copy-start | bytes 1179652
  327.8 3.6 %copy-start.5 = (f32[12,128]{1,0:T(8,128)S(1)}, f32[12,128]{1,0:T(8,128)}, u32[]{:S(2)}) copy-start(f32[12,128]{1,0:T(8,128)} %get-tuple-element.45) | copy-start | bytes 18436
  327.8 4.2 %copy-start.4 = (f32[12,128]{1,0:T(8,128)S(1)}, f32[12,128]{1,0:T(8,128)}, u32[]{:S(2)}) copy-start(f32[12,128]{1,0:T(8,128)} %get-tuple-element.46) | copy-start | bytes 18436
  327.8 4.8 %copy-start.3 = (f32[12,128]{1,0:T(8,128)S(1)}, f32[12,128]{1,0:T(8,128)}, u32[]{:S(2)}) copy-start(f32[12,128]{1,0:T(8,128)} %get-tuple-element.47) | copy-start | bytes 18436

commit v7 on v6

--- a/solution.py
+++ b/solution.py
@@ -745,11 +745,11 @@
                 g_qkv[row, :, h * hd : (h + 1) * hd] = g_q.astype(BF)
                 g_qkv[row, :, width + h * hd : width + (h + 1) * hd] = g_k.astype(BF)
 
-    rs_turn(MLP, 1)
     in_copies = sum_copies(27, psend, r1, r2)
     product = lambda a, b, i: dot(pair_of(g_qkv, a, b), merge(w_first[pl.ds(i * part, part), :, 0 : 3 * quarter]), NT)
     sum_theirs(product, in_copies, psend)
     sum_ours(product, pown)
+    rs_turn(MLP, 1)
     sum_turn(in_copies, pown, r1)
 
     ag_drain(FIRST)

time: 339 us -> 339 us (level)
  no operation moved by 1% of the time
where the time goes in v7:
time: 339 us; the launch traced here: 333 us
  Pallas kernels  324 us (96%)
  local copies, waits for them, and re-layouts  8.27 us (2%)
    pallas_call x1, Pallas kernels, run_layer(): pl.pallas_call(functools.partial(layer_kernel, cfg), out_shape=out_shape,...  316 us
    pallas_call x1, Pallas kernels, widen(): pl.pallas_call(functools.partial(widen_kernel, strip, count), grid=(steps...  8.44 us
    unnamed x25, local copies, waits for them, and re-layouts  7.6 us

profile of v7, /device:TPU:9, one launch (start us, length us, event | category | flops | bytes accessed | tf_op | source)
XLA Modules:
  0.0 333.2 jit_solution(1659181001414177195)
XLA Ops:
  0.6 1.5 copy.34.refs_6_
  2.2 1.4 copy.35.refs_7_
  3.5 315.8 %shard_map.262 = (bf16[128,1536]{1,0:T(8,128)(2,1)}, bf16[128,1536]{1,0:T(8,128)(2,1)}, f32[12,128]{1,0:T(8,128)}, f32[12,128]{1,0:T(8,128)}, f32[12,128]{1,0:T(...) custom-call(bf16[128,1536]{1,0:T(8,128)(2,1)} %bitcast.15, ...), custom_call_target="tpu_custom_call" | custom-call | tf_op jit(solution)/shard_map/pallas_call | solution.py:906
  319.3 0.0 copy-start.2
  319.3 0.0 copy-start.6
  319.3 0.0 copy-start.7
  319.3 0.0 copy-start.1
  319.3 0.0 copy-start
  319.3 8.4 %shard_map.263 = (f32[192,1536]{1,0:T(8,128)}, f32[192,1536]{1,0:T(8,128)}, f32[192,1536]{1,0:T(8,128)}, f32[192,1536]{1,0:T(8,128)}, f32[192,4096]{1,0:T(8,128)...) custom-call(bf16[4,192,1536]{2,1,0:T(8,128)(2,1)} %get-tuple-element.35.first_ref, ...), custom_call_target="tpu_custom_call" | custom-call | tf_op jit(solution)/shard_map/pallas_call | solution.py:942
  327.8 0.0 copy-start.3
  327.8 0.0 copy-done.2
  327.8 0.1 reshape.80
  327.9 0.8 copy.36
  328.6 0.0 copy-done.6
  328.6 0.1 reshape.81
  328.7 0.6 copy.37
  329.4 0.5 slice_bitcast_fusion
  329.9 0.7 copy.43
  330.6 0.0 copy-done
  330.6 0.7 copy.44
  331.4 0.6 copy.45
  332.0 0.0 copy-done.4
  332.0 0.6 copy.46
  332.6 0.6 copy.47
  (6 shorter events, 0.0 us)
Async XLA Ops:
  319.3 8.5 %copy-start.2 = (f32[16,128]{1,0:T(8,128)S(1)}, f32[16,128]{1,0:T(8,128)}, u32[]{:S(2)}) copy-start(f32[16,128]{1,0:T(8,128)} %get-tuple-element.48) | copy-start | bytes 24580
  319.3 9.3 %copy-start.6 = (f32[4,128]{1,0:T(4,128)S(1)}, f32[4,128]{1,0:T(4,128)}, u32[]{:S(2)}) copy-start(f32[4,128]{1,0:T(4,128)} %get-tuple-element.49) | copy-start | bytes 6148
  319.3 10.0 %copy-start.7 = (f32[1,128]{1,0:T(1,128)S(1)}, f32[1,128]{1,0:T(1,128)}, u32[]{:S(2)}) copy-start(f32[1,128]{1,0:T(1,128)} %get-tuple-element.50) | copy-start | bytes 1540
  319.3 10.6 %copy-start.1 = (bf16[128,1536]{1,0:T(8,128)(2,1)S(1)}, bf16[128,1536]{1,0:T(8,128)(2,1)}, u32[]{:S(2)}) copy-start(bf16[128,1536]{1,0:T(8,128)(2,1)} %get-tuple-element.33) | copy-start | bytes 1179652
  319.3 11.3 %copy-start = (bf16[128,1536]{1,0:T(8,128)(2,1)S(1)}, bf16[128,1536]{1,0:T(8,128)(2,1)}, u32[]{:S(2)}) copy-start(bf16[128,1536]{1,0:T(8,128)(2,1)} %get-tuple-element.34) | copy-start | bytes 1179652
  327.8 3.6 %copy-start.5 = (f32[12,128]{1,0:T(8,128)S(1)}, f32[12,128]{1,0:T(8,128)}, u32[]{:S(2)}) copy-start(f32[12,128]{1,0:T(8,128)} %get-tuple-element.45) | copy-start | bytes 18436
  327.8 4.2 %copy-start.4 = (f32[12,128]{1,0:T(8,128)S(1)}, f32[12,128]{1,0:T(8,128)}, u32[]{:S(2)}) copy-start(f32[12,128]{1,0:T(8,128)} %get-tuple-element.46) | copy-start | bytes 18436
  327.8 4.8 %copy-start.3 = (f32[12,128]{1,0:T(8,128)S(1)}, f32[12,128]{1,0:T(8,128)}, u32[]{:S(2)}) copy-start(f32[12,128]{1,0:T(8,128)} %get-tuple-element.47) | copy-start | bytes 18436
